TPU v7x, 32 devices: a whole 2x2x4 slice. The times are simulated.
32 devices in a mesh: wide: 8 (over z, y), narrow: 4 (over x, core).
Axes of the slice: x: 2, y: 2, z: 4, core: 2. Of those that a mesh axis runs over, the one named last changes fastest.
Arguments:
- dense: bfloat16 [4096, 256], P(('wide', 'narrow')), may hold values from -6 to 6
- pooled: bfloat16 [4096, 8, 256], P(('wide', 'narrow')), may hold values from -1.5 to 1.5
- w_top: bfloat16 [1024, 292], replicated, may hold values from -0.375 to 0.375
- bias: float32 [1024], replicated, may hold values from -3 to 3
- d_hidden: bfloat16 [4096, 1024], P(('wide', 'narrow')), may hold values from -6 to 6
- bag_ids: int32 [8, 4096, 2], P('wide'), may hold values from 0 to 4095
- tables: float32 [8, 4096, 256], P('wide', 'narrow'), may hold values from -6 to 6
- accum: float32 [8, 4096], P('wide', 'narrow'), may hold values from 0.1 to 10
Outputs:
- new_tables: float32 [8, 4096, 256], P('wide', 'narrow')
- new_accum: float32 [8, 4096], P('wide', 'narrow')
- w_grad: float32 [1024, 292], P('wide')
All inputs are finite; a program needn't handle non-finite values.
Results may differ from a plain program's by a relative error of at most 0.0047.
Values may be sent and summed in bfloat16 or wider, within the bound.
No kernel may reach another device: no remote copies, remote signals or barrier semaphores. Data moves between devices by JAX's collectives and lax.ppermute only.
A program may use at most 128 MiB of HBM per device.

v0:
```python
import math

import jax
import jax.numpy as jnp
import numpy as np
from jax import lax
from jax.sharding import PartitionSpec as P


def row_sums(grads, ids, offset, count):
    local = ids - offset
    local = jnp.where((local >= 0) & (local < count), local, count)
    result = jnp.zeros((count, grads.shape[1]), jnp.float32)
    for slot in range(ids.shape[1]):
        result = result + jax.ops.segment_sum(grads, local[:, slot], num_segments=count + 1)[:count]
    return result


def body(dense, pooled, w_top, bias, d_hidden, bag_ids, tables, accum):
    samples = dense.shape[0]
    width = dense.shape[1]
    n_wide = lax.axis_size("wide")
    n_narrow = lax.axis_size("narrow")
    total = samples * n_wide * n_narrow
    feats = jnp.concatenate([dense[:, None, :], pooled], axis=1)
    count = feats.shape[1]
    low_i, low_j = np.tril_indices(count, -1)
    zmat = jnp.einsum("bfd,bgd->bfg", feats, feats, preferred_element_type=jnp.float32)
    z_in = jnp.concatenate([dense.astype(jnp.float32), zmat[:, low_i, low_j]], axis=1).astype(
        jnp.bfloat16
    )
    pre = jnp.dot(z_in, w_top.T, preferred_element_type=jnp.float32) + bias
    sig = jax.nn.sigmoid(pre)
    slope = sig * (1.0 + pre * (1.0 - sig))
    dpre = (d_hidden.astype(jnp.float32) * slope).astype(jnp.bfloat16)
    dz_full = jnp.dot(dpre, w_top, preferred_element_type=jnp.float32)
    dpairs = dz_full[:, width:]
    dmat = jnp.zeros((samples, count * count), jnp.float32).at[:, low_i * count + low_j].set(dpairs)
    dmat = dmat.reshape(samples, count, count)
    dsym = (dmat + jnp.transpose(dmat, (0, 2, 1))).astype(jnp.bfloat16)
    dfeat = jnp.einsum("bfg,bgd->bfd", dsym, feats, preferred_element_type=jnp.float32)
    dpooled = dfeat[:, 1:, :].astype(jnp.bfloat16)
    part = lax.slice_in_dim(dpre, 0, w_top.shape[0] // n_wide * lax.axis_size("wide"), axis=1)
    wide_part = lax.psum_scatter(
        jnp.dot(part.T, z_in, preferred_element_type=jnp.float32),
        "wide",
        scatter_dimension=0,
        tiled=True,
    )
    w_grad = lax.psum(wide_part, "narrow") / math.sqrt(total)
    owned = lax.all_to_all(dpooled, "wide", split_axis=1, concat_axis=0, tiled=True).reshape(
        n_wide * samples, width
    )
    bag = bag_ids.shape[2]
    ids_four = bag_ids[0].reshape(n_wide, n_narrow, samples, bag)
    rows_dev = tables.shape[1]
    narrow_pos = lax.axis_index("narrow")
    every = lax.all_gather(owned, "narrow", axis=0, tiled=True)
    ids_all = jnp.transpose(ids_four, (1, 0, 2, 3)).reshape(-1, bag)
    row_grad = row_sums(every.astype(jnp.float32), ids_all, narrow_pos * rows_dev, rows_dev)
    acc_new = accum[0] + jnp.mean(row_grad * row_grad, axis=1)
    table_new = tables[0] - 0.1 * row_grad / (jnp.sqrt(acc_new)[:, None] + 1e-08)
    return (table_new[None], acc_new[None], w_grad)


def solution(mesh):
    placed = (
        P(("wide", "narrow"), None),
        P(("wide", "narrow"), None, None),
        P(),
        P(),
        P(("wide", "narrow"), None),
        P("wide", None, None),
        P("wide", "narrow", None),
        P("wide", "narrow"),
    )
    return jax.shard_map(
        body,
        mesh=mesh,
        in_specs=placed,
        out_specs=(P("wide", "narrow", None), P("wide", "narrow"), P("wide", None)),
        check_vma=False,
    )
```

profile of v0, /device:TPU:0, one launch (start us, length us, event | category | flops | bytes accessed | tf_op | source)
XLA Modules:
  0.0 194.6 jit_solution(13491152778797779090)
XLA Ops:
  7.2 0.0 copy-start.2
  7.2 0.0 reduce-scatter.2.cloned.1.call-start
  7.3 1.0 copy.29
  8.3 2.0 %fusion.7 = bf16[128,9,9]{2,1,0:T(8,128)(2,1)S(1)} fusion(bf16[128,8,256]{2,1,0:T(8,128)(2,1)} %param.15, bf16[128,1,256]{2,1,0:T(2,128)(2,1)S(1)} %copy.29), kind=kOutput, calls=%fused_computation.19 | convolution fusion | flops 6488064 | bytes 610560 | tf_op jit(solution)/shard_map/bfd,bgd->bfg/dot_general | solution.py:28
  10.3 0.3 copy.30
  10.7 1.0 gather_fusion
  11.7 0.1 copy.31
  11.9 0.4 multiply_convert_fusion
  12.3 1.4 fusion.12
  13.7 0.0 reduce-scatter.2.cloned.1.call-update
  13.7 0.2 convolution_bitcast_fusion
  13.9 0.8 scatter_custom_fusion
  14.8 0.5 copy.33
  15.3 0.5 copy.32
  15.8 0.6 fusion.6
  16.4 0.2 slice.46
  16.6 0.9 copy.34
  17.5 7.3 %all-to-all-start = ((bf16[128,8,256]{2,0,1:T(8,128)(2,1)}), bf16[128,8,256]{2,0,1:T(8,128)(2,1)S(1)}, u32[]{:S(2)}, u32[]{:S(2)}) async-start(bf16[128,8,256]{2,0,1:T(8,128)(2,1)} %copy.34), calls=%async_computation | async-start | bytes 1048576 | tf_op jit(solution)/shard_map/all_to_all | solution.py:51
  24.8 0.0 all-reduce.2.cloned.1.call-start
  24.8 57.3 %reduce-scatter.2.cloned.1.call-done = f32[128,292]{0,1:T(8,128)} async-done(((f32[1024,292]{0,1:T(8,128)}), f32[128,292]{0,1:T(8,128)}) %reduce-scatter.2.cloned.1.call-update) | async-done | bytes 149520 | tf_op jit(solution)/shard_map/reduce_scatter | solution.py:44
  82.1 0.0 all-reduce.2.cloned.1.call-update
  82.1 0.0 all-gather.2.cloned.1.call-start
  82.2 0.8 copy-done
  83.0 0.0 all-gather.2.cloned.1.call-update
  83.2 31.3 %all-reduce.2.cloned.1.call-done = f32[128,292]{0,1:T(8,128)} async-done(((f32[128,292]{0,1:T(8,128)}), f32[128,292]{0,1:T(8,128)}) %all-reduce.2.cloned.1.call-update) | async-done | bytes 149520 | tf_op jit(solution)/shard_map/psum | solution.py:50
  114.4 1.6 broadcast_multiply_fusion
  116.0 23.9 %all-gather.2.cloned.1.call-done = bf16[4096,256]{1,0:T(8,128)(2,1)} async-done(((bf16[1024,256]{1,0:T(8,128)(2,1)}), bf16[4096,256]{1,0:T(8,128)(2,1)}) %all-gather.2.cloned.1.call-update) | async-done | bytes 2097168 | tf_op jit(solution)/shard_map/all_gather | solution.py:58
  139.9 23.0 %scatter_custom_fusion.2 = f32[1025,256]{1,0:T(8,128)S(1)} fusion(s32[4096]{0:T(1024)S(1)} %bitcast.50, bf16[4096,256]{1,0:T(8,128)(2,1)} %all-gather.2.cloned.1.call-done, f32[]{:T(128)} %constant.15.clone.1), kind=kCustom, calls=%fused_computation.4 | custom fusion | flops 2097152 | bytes 3146756 | tf_op jit(solution)/shard_map/scatter-add | solution.py:15
  162.9 23.1 %scatter_custom_fusion.1 = f32[1025,256]{1,0:T(8,128)S(1)} fusion(s32[4096]{0:T(1024)S(1)} %bitcast.49, bf16[4096,256]{1,0:T(8,128)(2,1)} %all-gather.2.cloned.1.call-done, f32[]{:T(128)} %constant.15.clone.1), kind=kCustom, calls=%fused_computation.6 | custom fusion | flops 2097152 | bytes 3146756 | tf_op jit(solution)/shard_map/scatter-add | solution.py:15
  186.0 0.3 multiply_reduce_fusion
  186.3 0.6 add.74
  186.9 1.2 fusion.5
  (26 shorter events, 0.2 us)
Async XLA Ops:
  7.2 3.5 %copy-start.2 = (s32[36]{0:T(128)S(1)}, s32[36]{0:T(128)}, u32[]{:S(2)}) copy-start(s32[36]{0:T(128)} %constant.69) | copy-start | bytes 436
  7.2 4.7 %copy-start.4 = (bf16[128,256]{1,0:T(8,128)(2,1)S(1)}, bf16[128,256]{1,0:T(8,128)(2,1)}, u32[]{:S(2)}) copy-start(bf16[128,256]{1,0:T(8,128)(2,1)} %param.14) | copy-start | bytes 196612
  7.2 4.7 %copy-start.7 = (bf16[1024,292]{0,1:T(8,128)(2,1)S(1)}, bf16[1024,292]{0,1:T(8,128)(2,1)}, u32[]{:S(2)}) copy-start(bf16[1024,292]{0,1:T(8,128)(2,1)} %param.16) | copy-start | bytes 1794052
  7.2 4.7 %copy-start.8 = (bf16[128,1024]{1,0:T(8,128)(2,1)S(1)}, bf16[128,1024]{1,0:T(8,128)(2,1)}, u32[]{:S(2)}) copy-start(bf16[128,1024]{1,0:T(8,128)(2,1)} %param.18) | copy-start | bytes 786436
  7.2 4.7 %copy-start.9 = (f32[1024]{0:T(1024)S(1)}, f32[1024]{0:T(1024)}, u32[]{:S(2)}) copy-start(f32[1024]{0:T(1024)} %param.17) | copy-start | bytes 12292
  7.2 74.9 %reduce-scatter.2.cloned.1.call-start = ((), (), s32[]{:S(2)}) async-start(), calls=%async_computation.3 | async-start | bytes 1363968 | tf_op jit(solution)/shard_map/reduce_scatter | solution.py:44
  13.7 2.1 %copy-start.3 = (bf16[128,8,256]{2,1,0:T(8,128)(2,1)S(1)}, bf16[128,8,256]{2,1,0:T(8,128)(2,1)}, u32[]{:S(2)}) copy-start(bf16[128,8,256]{2,1,0:T(8,128)(2,1)} %param.15) | copy-start | bytes 1572868
  16.4 66.6 %copy-start.5 = (s32[1,4096,2]{1,2,0:T(2,128)S(1)}, s32[1,4096,2]{1,2,0:T(2,128)}, u32[]{:S(2)}) copy-start(s32[1,4096,2]{1,2,0:T(2,128)} %param.19) | copy-start | bytes 98308
  17.5 64.7 %all-to-all-start = ((bf16[128,8,256]{2,0,1:T(8,128)(2,1)}), bf16[128,8,256]{2,0,1:T(8,128)(2,1)S(1)}, u32[]{:S(2)}, u32[]{:S(2)}) async-start(bf16[128,8,256]{2,0,1:T(8,128)(2,1)} %copy.34), calls=%async_computation | async-start | bytes 1048576 | tf_op jit(solution)/shard_map/all_to_all | solution.py:51
  24.8 89.6 %all-reduce.2.cloned.1.call-start = ((), (), s32[]{:S(2)}) async-start(), calls=%async_computation.4 | async-start | bytes 303104 | tf_op jit(solution)/shard_map/psum | solution.py:50
  82.1 57.8 %all-gather.2.cloned.1.call-start = ((), (), s32[]{:S(2)}) async-start(), calls=%async_computation.2 | async-start | bytes 2621440 | tf_op jit(solution)/shard_map/all_gather | solution.py:58
  82.2 0.8 copy-start
  162.9 23.4 %copy-start.6 = (f32[1,1024]{1,0:T(1,128)S(1)}, f32[1,1024]{1,0:T(1,128)}, u32[]{:S(2)}) copy-start(f32[1,1024]{1,0:T(1,128)} %param.21) | copy-start | bytes 12292
  162.9 24.0 %copy-start.1 = (f32[1,1024,256]{2,1,0:T(8,128)S(1)}, f32[1,1024,256]{2,1,0:T(8,128)}, u32[]{:S(2)}) copy-start(f32[1,1024,256]{2,1,0:T(8,128)} %param.20) | copy-start | bytes 3145732
Sparse Core Ops, SparseCore 0:
  13.9 68.1 reduce-scatter.1
  84.5 29.8 all-reduce.1
  116.6 23.2 all-gather.1
where the time goes:
time: 195 us
  waiting for transfers between devices  112 us (57%)
  other arithmetic  49.8 us (26%)
  between operations  14 us (7%)
  starting transfers between devices  7.4 us (4%)
  local copies, waits for them, and re-layouts  6.38 us (3%)
  matrix products  4.61 us (2%)
    reduce_scatter x1, waiting for transfers between devices, body(): lax.psum_scatter(jnp.dot(part.T, z_in, preferred_element_type=jnp.float32...  57.3 us
    scatter-add x2, other arithmetic, row_sums(): jax.ops.segment_sum(grads, local[:, slot], num_segments=count + 1)[:count]  46.1 us
    psum x1, waiting for transfers between devices, body(): w_grad = lax.psum(wide_part, 'narrow') / math.sqrt(total)  31.3 us
    all_gather x1, waiting for transfers between devices, body(): every = lax.all_gather(owned, 'narrow', axis=0, tiled=True)  23.9 us
    all_to_all x1, starting transfers between devices, body(): lax.all_to_all(dpooled, 'wide', split_axis=1, concat_axis=0, tiled=True)  7.29 us
  transfers between devices with their start and end apart: 4, of which 3 were waited for; matrix products, arithmetic and copies ran while one was open for 3% of the time, Pallas kernels for 0%

commit v1 on v0

--- a/solution.py
+++ b/solution.py
@@ -1,10 +1,210 @@
+import functools
 import math
 
 import jax
 import jax.numpy as jnp
 import numpy as np
 from jax import lax
+from jax.experimental import pallas as pl
+from jax.experimental.pallas import tpu as pltpu
 from jax.sharding import PartitionSpec as P
+
+NT = (((1,), (1,)), ((), ()))
+
+
+def eye(n):
+    r = lax.broadcasted_iota(jnp.int32, (n, n), 0)
+    c = lax.broadcasted_iota(jnp.int32, (n, n), 1)
+    return jnp.where(r == c, 1.0, 0.0).astype(jnp.bfloat16)
+
+
+def local_kernel(
+    place, dense_in, pooled_in, w_in, bias_in, d_hidden_in,
+    out, keep, send,
+    dense, pooled, w_t, bias, d_hidden,
+    pooled32, feat_t, zrows, z_t, dp_t, wg, sems,
+):
+    moves = [
+        pltpu.make_async_copy(source, target, sems.at[i])
+        for i, (source, target) in enumerate(
+            ((pooled_in, pooled), (dense_in, dense), (w_in, w_t), (bias_in, bias), (d_hidden_in, d_hidden))
+        )
+    ]
+    for move in moves:
+        move.start()
+    samples, width = dense.shape
+    tables = pooled.shape[0] // samples
+    count = tables + 1
+    low_i, low_j = np.tril_indices(count, -1)
+    pairs = len(low_i)
+    of_pair = {}
+    for p, (i, j) in enumerate(zip(low_i, low_j)):
+        of_pair[int(i), int(j)] = of_pair[int(j), int(i)] = p
+    wide, core = place[0], place[1]
+
+    moves[0].wait()
+    for h in range(width // 128):
+        pooled32[h] = pooled[:, h * 128 : (h + 1) * 128].astype(jnp.float32)
+    ident = eye(width)
+    moves[1].wait()
+    feat_t[0] = lax.dot_general(ident, dense[...], NT, preferred_element_type=jnp.float32)
+    for t in range(tables):
+        rows = jnp.concatenate(
+            [pooled32[h, pl.ds(t, samples, stride=tables), :] for h in range(width // 128)], axis=1
+        ).astype(jnp.bfloat16)
+        feat_t[t + 1] = lax.dot_general(ident, rows, NT, preferred_element_type=jnp.float32)
+
+    def products(c, sums):
+        f = [feat_t[i, pl.ds(pl.multiple_of(c * 8, 8), 8), :] for i in range(count)]
+        return tuple(s + f[i] * f[j] for s, i, j in zip(sums, low_i, low_j))
+
+    zero = jnp.zeros((8, samples), jnp.float32)
+    sums = lax.fori_loop(0, width // 8, products, (zero,) * pairs, unroll=4)
+    zrows[...] = jnp.zeros_like(zrows)
+    for p in range(pairs):
+        zrows[p : p + 1, :] = jnp.sum(sums[p], axis=0, keepdims=True)
+
+    z_t[:width, :] = feat_t[0].astype(jnp.bfloat16)
+    extra = z_t.shape[0] - width
+    z_t[width:, :] = zrows[:extra, :].astype(jnp.bfloat16)
+    z_pairs = zrows[...].T[:, :pairs].astype(jnp.bfloat16)
+    for move in moves[2:]:
+        move.wait()
+    w_pairs = w_t[width : width + pairs, :]
+    pre = (
+        jnp.dot(dense[...], w_t[:width, :], preferred_element_type=jnp.float32)
+        + jnp.dot(z_pairs, w_pairs, preferred_element_type=jnp.float32)
+        + bias[...]
+    )
+    sig = 1.0 / (1.0 + jnp.exp(-pre))
+    slope = sig * (1.0 + pre * (1.0 - sig))
+    dpre = (d_hidden[...].astype(jnp.float32) * slope).astype(jnp.bfloat16)
+    dsym = lax.dot_general(w_pairs, dpre, NT, preferred_element_type=jnp.float32)
+    dsym = dsym.astype(jnp.bfloat16).astype(jnp.float32)
+
+    spread = [jnp.broadcast_to(dsym[p : p + 1, :], (8, samples)) for p in range(pairs)]
+
+    def gradients(c, carry):
+        for h in range(2):
+            at = pl.ds(pl.multiple_of(c * 16 + h * 8, 8), 8)
+            f = [feat_t[i, at, :] for i in range(count)]
+            for t in range(tables):
+                total = None
+                for g in range(count):
+                    if g != t + 1:
+                        term = spread[of_pair[t + 1, g]] * f[g]
+                        total = term if total is None else total + term
+                dp_t[t, at, :] = total
+        return carry
+
+    lax.fori_loop(0, width // 16, gradients, 0)
+    ident_s = eye(samples)
+    for t in range(tables):
+        got = lax.dot_general(ident_s, dp_t[t].astype(jnp.bfloat16), NT, preferred_element_type=jnp.float32)
+        out[jnp.bitwise_xor(wide, t)] = got.astype(jnp.bfloat16)
+
+    half = wg.shape[1]
+    for h in range(2):
+        wg[h] = jnp.dot(z_t[h * half : (h + 1) * half, :], dpre, preferred_element_type=jnp.float32)
+    keep[...] = wg[core]
+    send[...] = wg[1 - core].astype(send.dtype)
+
+
+def local_part(place, dense, pooled, w_t, bias, d_hidden, send_type):
+    samples, width = dense.shape
+    tables = pooled.shape[1]
+    hidden = w_t.shape[1]
+    padded = -(-w_t.shape[0] // 64) * 64
+    half = padded // 2
+    vmem = pl.BlockSpec(memory_space=pltpu.VMEM)
+    return pl.pallas_call(
+        local_kernel,
+        out_shape=(
+            jax.ShapeDtypeStruct((tables, samples, width), jnp.bfloat16),
+            jax.ShapeDtypeStruct((half, hidden), jnp.float32),
+            jax.ShapeDtypeStruct((half, hidden), send_type),
+        ),
+        in_specs=[pl.BlockSpec(memory_space=pltpu.SMEM)] + [pl.BlockSpec(memory_space=pltpu.HBM)] * 5,
+        out_specs=(vmem,) * 3,
+        scratch_shapes=[
+            pltpu.VMEM((samples, width), dense.dtype),
+            pltpu.VMEM((samples * tables, width), pooled.dtype),
+            pltpu.VMEM(w_t.shape, w_t.dtype),
+            pltpu.VMEM((1, hidden), bias.dtype),
+            pltpu.VMEM((samples, hidden), d_hidden.dtype),
+            pltpu.VMEM((width // 128, samples * tables, 128), jnp.float32),
+            pltpu.VMEM((tables + 1, width, samples), jnp.float32),
+            pltpu.VMEM((128, samples), jnp.float32),
+            pltpu.VMEM((padded, samples), jnp.bfloat16),
+            pltpu.VMEM((tables, width, samples), jnp.float32),
+            pltpu.VMEM((2, half, hidden), jnp.float32),
+            pltpu.SemaphoreType.DMA((5,)),
+        ],
+        compiler_params=pltpu.CompilerParams(vmem_limit_bytes=60 * 2**20),
+    )(place, dense, pooled.reshape(samples * tables, width), w_t, bias.reshape(1, hidden), d_hidden)
+
+
+def update_kernel(place, ids, table, accum, *refs):
+    grads, (new_table, new_accum, ids_a, ids_b) = refs[:4], refs[4:]
+    rows, width = table.shape
+    blocks, samples = grads[0].shape[:2]
+    n_narrow = 4
+    wide, narrow = place[0], place[2]
+    step = 16
+    down = lax.broadcasted_iota(jnp.int32, (step, samples), 0)
+    for j in range(4):
+        for k in range(blocks):
+            at = jnp.bitwise_xor(wide, k) * n_narrow + jnp.bitwise_xor(narrow, j)
+            local = ids[:, pl.ds(pl.multiple_of(at * samples, samples), samples)] - narrow * rows
+            for s, keep in enumerate((ids_a, ids_b)):
+                keep[j, :, k * samples : (k + 1) * samples] = (
+                    jnp.broadcast_to(local[s : s + 1, :], (step, samples)) - down
+                ).astype(jnp.int16)
+    tile = 128
+    one, none = jnp.bfloat16(1), jnp.bfloat16(0)
+    scale_rows = width
+
+    def tile_step(m, carry):
+        base = m * tile
+        total = jnp.zeros((tile, width), jnp.float32)
+        for j in range(4):
+            a, b = ids_a[j], ids_b[j]
+            parts = []
+            for i in range(tile // step):
+                want = (base + i * step).astype(jnp.int16)
+                parts.append(jnp.where(a == want, one, none) + jnp.where(b == want, one, none))
+            hot = jnp.concatenate(parts, axis=0)
+            total += jnp.dot(hot, grads[j][...].reshape(blocks * samples, width), preferred_element_type=jnp.float32)
+        at = pl.ds(pl.multiple_of(base, tile), tile)
+        mean = jnp.sum(total * total, axis=1, keepdims=True) * (1.0 / width)
+        row = jnp.broadcast_to(mean, (tile, tile)).T[:1, :]
+        fresh = accum[:, at] + row
+        new_accum[:, at] = fresh
+        rate = 0.1 / (jnp.sqrt(fresh) + 1e-8)
+        rate = jnp.broadcast_to(rate, (tile, tile)).T
+        for h in range(width // tile):
+            cols = slice(h * tile, (h + 1) * tile)
+            new_table[at, cols] = table[at, cols] - total[:, cols] * rate
+        return carry
+
+    lax.fori_loop(0, rows // tile, tile_step, 0)
+
+
+def update_part(place, ids, table, accum, grads):
+    rows, width = table.shape
+    blocks, samples = grads[0].shape[:2]
+    vmem = pl.BlockSpec(memory_space=pltpu.VMEM)
+    return pl.pallas_call(
+        update_kernel,
+        out_shape=(
+            jax.ShapeDtypeStruct((rows, width), jnp.float32),
+            jax.ShapeDtypeStruct((1, rows), jnp.float32),
+        ),
+        in_specs=[pl.BlockSpec(memory_space=pltpu.SMEM)] + [vmem] * 7,
+        out_specs=(vmem,) * 2,
+        scratch_shapes=[pltpu.VMEM((4, 16, blocks * samples), jnp.int16)] * 2,
+        compiler_params=pltpu.CompilerParams(vmem_limit_bytes=60 * 2**20),
+    )(place, ids, table, accum, *grads)
 
 
 def row_sums(grads, ids, offset, count):
@@ -16,7 +216,7 @@
     return result
 
 
-def body(dense, pooled, w_top, bias, d_hidden, bag_ids, tables, accum):
+def plain_body(dense, pooled, w_top, bias, d_hidden, bag_ids, tables, accum):
     samples = dense.shape[0]
     width = dense.shape[1]
     n_wide = lax.axis_size("wide")
@@ -63,6 +263,51 @@
     return (table_new[None], acc_new[None], w_grad)
 
 
+def body(dense, pooled, w_top, bias, d_hidden, bag_ids, tables, accum):
+    n_wide, n_narrow = lax.axis_size("wide"), lax.axis_size("narrow")
+    samples, count = dense.shape[0], pooled.shape[1]
+    rows, width = tables.shape[1:]
+    inputs = w_top.shape[1]
+    total = samples * n_wide * n_narrow
+    if n_narrow != 4 or n_wide & (n_wide - 1) or count != n_wide or total * width > 2**21:
+        return plain_body(dense, pooled, w_top, bias, d_hidden, bag_ids, tables, accum)
+    wide, narrow = lax.axis_index("wide"), lax.axis_index("narrow")
+    core, chip = narrow % 2, narrow // 2
+    place = jnp.stack([wide, core, narrow]).astype(jnp.int32)
+
+    def swap(array, axis, bit):
+        n = lax.axis_size(axis)
+        return lax.ppermute(array, axis, [(i, i ^ bit) for i in range(n)])
+
+    out, keep, send = local_part(place, dense, pooled, w_top.T, bias, d_hidden, jnp.float32)
+    owned = jnp.stack([out[0]] + [swap(out[k], "wide", k) for k in range(1, n_wide)])
+    beside = swap(owned, "narrow", 1)
+    across = swap(owned, "narrow", 2)
+    opposite = swap(across, "narrow", 1)
+    ids = bag_ids[0].T
+    new_table, new_accum = update_part(place, ids, tables[0], accum, [owned, beside, across, opposite])
+
+    half = keep + swap(send, "narrow", 1)
+    quarter = half.shape[0] // 2
+    mine = lax.dynamic_slice_in_dim(half, chip * quarter, quarter, 0)
+    theirs = lax.dynamic_slice_in_dim(half, (1 - chip) * quarter, quarter, 0)
+    mine = mine + swap(theirs.astype(jnp.bfloat16), "narrow", 2).astype(jnp.float32)
+    hidden = mine.shape[1]
+    block = hidden // n_wide
+    blocks = jnp.transpose(mine.astype(jnp.bfloat16).reshape(quarter, n_wide, block), (1, 0, 2))
+    got = lax.all_to_all(blocks, "wide", 0, 0, tiled=True)
+    part = jnp.sum(got.astype(jnp.float32), axis=0) / math.sqrt(total)
+    other = swap(part, "narrow", 2)
+    low = jnp.where(chip == 0, part, other)
+    high = jnp.where(chip == 0, other, part)
+    part = jnp.concatenate([low, high], axis=0)
+    other = swap(part, "narrow", 1)
+    low = jnp.where(core == 0, part, other)
+    high = jnp.where(core == 0, other, part)
+    w_grad = jnp.concatenate([low, high], axis=0)[:inputs].T
+    return (new_table[None], new_accum, w_grad)
+
+
 def solution(mesh):
     placed = (
         P(("wide", "narrow"), None),

time: 195 us -> 61.6 us (0.32)
  waiting for transfers between devices: 112 us -> 18.5 us
  other arithmetic: 49.8 us -> 2.19 us
  starting transfers between devices: 7.4 us -> 23.4 us
  Pallas kernels: 0 us -> 14.1 us
  between operations: 14 us -> 0.85 us
  matrix products: 4.61 us -> 0 us
  local copies, waits for them, and re-layouts: 6.38 us -> 2.21 us
    reduce_scatter x1 -> x0, waiting for transfers between devices: 57.3 us -> none  [body(): lax.psum_scatter(jnp.dot(part.T, z_in, preferred_element_type=jnp.float32...]
    scatter-add x2 -> x0, other arithmetic: 46.1 us -> none  [row_sums(): jax.ops.segment_sum(grads, local[:, slot], num_segments=count + 1)[:count]]
    psum x1 -> x0, waiting for transfers between devices: 31.3 us -> none  [body(): w_grad = lax.psum(wide_part, 'narrow') / math.sqrt(total)]
    all_gather x1 -> x0, waiting for transfers between devices: 23.9 us -> none  [body(): every = lax.all_gather(owned, 'narrow', axis=0, tiled=True)]
    ppermute x0 -> x14, starting transfers between devices: none -> 18.4 us  [swap(): return lax.ppermute(array, axis, [(i, i ^ bit) for i in range(n)])]
    pallas_call x0 -> x2, Pallas kernels: none -> 14.1 us  [the longest x1 8.34 us: update_part(): pl.pallas_call(update_kernel, out_shape=(jax.ShapeDtypeStruct((rows, widt...]
    ppermute x0 -> x14, waiting for transfers between devices: none -> 14 us  [swap(): return lax.ppermute(array, axis, [(i, i ^ bit) for i in range(n)])]
    dot_general x5 -> x0, matrix products: 4.61 us -> none  [the longest x1 2.03 us: body(): jnp.einsum('bfd,bgd->bfg', feats, feats, preferred_element_type=jnp.float32)]
  transfers between devices with their start and end apart: 4 -> 15, of which waited for: 3 -> 5; matrix products, arithmetic and copies ran while one was open for 3% -> 1% of each run, Pallas kernels for 0% -> 14%
where the time goes in v1:
time: 61.6 us; the launch traced here: 61.3 us
  starting transfers between devices  23.4 us (38%)
  waiting for transfers between devices  18.5 us (30%)
  Pallas kernels  14.1 us (23%)
  local copies, waits for them, and re-layouts  2.21 us (4%)
  other arithmetic  2.19 us (4%)
  between operations  0.85 us (1%)
    ppermute x14, starting transfers between devices, swap(): return lax.ppermute(array, axis, [(i, i ^ bit) for i in range(n)])  18.4 us
    ppermute x14, waiting for transfers between devices, swap(): return lax.ppermute(array, axis, [(i, i ^ bit) for i in range(n)])  14 us
    pallas_call x1, Pallas kernels, update_part(): pl.pallas_call(update_kernel, out_shape=(jax.ShapeDtypeStruct((rows, widt...  8.34 us
    pallas_call x1, Pallas kernels, local_part(): pl.pallas_call(local_kernel, out_shape=(jax.ShapeDtypeStruct((tables, sam...  5.75 us
    all_to_all x1, starting transfers between devices, body(): got = lax.all_to_all(blocks, 'wide', 0, 0, tiled=True)  4.99 us
    all_to_all x1, waiting for transfers between devices, body(): got = lax.all_to_all(blocks, 'wide', 0, 0, tiled=True)  4.51 us
  transfers between devices with their start and end apart: 15, of which 5 were waited for; matrix products, arithmetic and copies ran while one was open for 1% of the time, Pallas kernels for 14%

profile of v1, /device:TPU:0, one launch (start us, length us, event | category | flops | bytes accessed | tf_op | source)
XLA Modules:
  0.0 61.3 jit_solution(7351406510508526027)
XLA Ops:
  0.6 0.7 %pad_add_fusion.place = s32[3]{0:T(128)} fusion(s32[1]{0:T(128)} %bitcast.2, s32[1]{0:T(128)} %bitcast.1, s32[1]{0:T(128)} %bitcast), kind=kLoop, calls=%fused_computation.28 | loop fusion | flops 6 | bytes 24 | tf_op jit(solution)/shard_map/stack | solution.py:276
  1.3 5.7 %shard_map.103 = (bf16[8,128,256]{2,1,0:T(8,128)(2,1)}, f32[160,1024]{1,0:T(8,128)}, f32[160,1024]{1,0:T(8,128)}) custom-call(s32[3]{0:T(128)} %pad_add_fusion.place, bf16[128,256]{1,0:T(8,128)(2,1)} %dense_in.1, bf16[1024,256]{1,0:T(8,128)(2,1)} %bitcast.50, bf16[292,1024]{1,0:T(8,128)(2,1)} %bitcast.49, f32[1,1024]{1,0:T(1,128)} %bitcast.52, ...), custom_call_target="tpu_custom_call" | custom-call | tf_op jit(solution)/shard_map/pallas_call | solution.py:120
  7.1 1.2 %slice_bitcast_fusion = (bf16[128,256]{1,0:T(8,128)(2,1)S(1)}, bf16[128,256]{1,0:T(8,128)(2,1)S(1)}, bf16[128,256]{1,0:T(8,128)(2,1)S(1)}, bf16[128,256]{1,0:T(8...) fusion(bf16[8,128,256]{2,1,0:T(8,128)(2,1)} %get-tuple-element.8), kind=kLoop, calls=%fused_computation.15 | loop fusion | bytes 1048576 | tf_op jit(solution)/shard_map/squeeze | solution.py:283
  8.2 0.0 copy-start.1
  8.3 3.0 %collective-permute-start = (bf16[128,256]{1,0:T(8,128)(2,1)S(1)}, bf16[128,256]{1,0:T(8,128)(2,1)S(1)}, u32[]{:S(2)}, u32[]{:S(2)}) collective-permute-start(bf16[128,256]{1,0:T(8,128)(2,1)S(1)} %get-tuple-element.19), channel_id=1, source_target_pairs={{0,4},{4,0},{8,12},{12,8},{16,20},{20,16},{24,28},{28,24},{1,5},{5... | collective-permute-start | bytes 196616 | tf_op jit(solution)/shard_map/ppermute | solution.py:280
  11.3 0.0 collective-permute-start.10
  11.3 1.6 %collective-permute-start.1 = (bf16[128,256]{1,0:T(8,128)(2,1)S(1)}, bf16[128,256]{1,0:T(8,128)(2,1)S(1)}, u32[]{:S(2)}, u32[]{:S(2)}) collective-permute-start(bf16[128,256]{1,0:T(8,128)(2,1)S(1)} %get-tuple-element.18), channel_id=1, source_target_pairs={{0,8},{4,12},{8,0},{12,4},{16,24},{20,28},{24,16},{28,20},{1,9},{5... | collective-permute-start | bytes 196616 | tf_op jit(solution)/shard_map/ppermute | solution.py:280
  12.9 0.0 collective-permute-start.2
  12.9 2.9 %collective-permute-start.3 = (bf16[128,256]{1,0:T(8,128)(2,1)S(1)}, bf16[128,256]{1,0:T(8,128)(2,1)S(1)}, u32[]{:S(2)}, u32[]{:S(2)}) collective-permute-start(bf16[128,256]{1,0:T(8,128)(2,1)S(1)} %get-tuple-element.16), channel_id=1, source_target_pairs={{0,16},{4,20},{8,24},{12,28},{16,0},{20,4},{24,8},{28,12},{1,17},{... | collective-permute-start | bytes 196616 | tf_op jit(solution)/shard_map/ppermute | solution.py:280
  15.9 0.0 collective-permute-done
  15.9 1.7 %collective-permute-start.4 = (bf16[128,256]{1,0:T(8,128)(2,1)S(1)}, bf16[128,256]{1,0:T(8,128)(2,1)S(1)}, u32[]{:S(2)}, u32[]{:S(2)}) collective-permute-start(bf16[128,256]{1,0:T(8,128)(2,1)S(1)} %get-tuple-element.15), channel_id=1, source_target_pairs={{0,20},{4,16},{8,28},{12,24},{16,4},{20,0},{24,12},{28,8},{1,21},{... | collective-permute-start | bytes 196616 | tf_op jit(solution)/shard_map/ppermute | solution.py:280
  17.6 3.2 %collective-permute-start.5 = (bf16[128,256]{1,0:T(8,128)(2,1)S(1)}, bf16[128,256]{1,0:T(8,128)(2,1)S(1)}, u32[]{:S(2)}, u32[]{:S(2)}) collective-permute-start(bf16[128,256]{1,0:T(8,128)(2,1)S(1)} %get-tuple-element.14), channel_id=1, source_target_pairs={{0,24},{4,28},{8,16},{12,20},{16,8},{20,12},{24,0},{28,4},{1,25},{... | collective-permute-start | bytes 196616 | tf_op jit(solution)/shard_map/ppermute | solution.py:280
  20.8 1.3 %collective-permute-start.6 = (bf16[128,256]{1,0:T(8,128)(2,1)S(1)}, bf16[128,256]{1,0:T(8,128)(2,1)S(1)}, u32[]{:S(2)}, u32[]{:S(2)}) collective-permute-start(bf16[128,256]{1,0:T(8,128)(2,1)S(1)} %get-tuple-element.13), channel_id=1, source_target_pairs={{0,28},{4,24},{8,20},{12,16},{16,12},{20,8},{24,4},{28,0},{1,29},{... | collective-permute-start | bytes 196616 | tf_op jit(solution)/shard_map/ppermute | solution.py:280
  22.1 4.2 %collective-permute-done.4 = bf16[128,256]{1,0:T(8,128)(2,1)S(1)} collective-permute-done((bf16[128,256]{1,0:T(8,128)(2,1)S(1)}, bf16[128,256]{1,0:T(8,128)(2,1)S(1)}, u32[]{:S(2)}, u32[]{:S(2)}) %collective-permute-start.4) | collective-permute-done | bytes 65568 | tf_op jit(solution)/shard_map/ppermute | solution.py:280
  26.4 0.0 collective-permute-done.10
  26.4 0.1 add.18
  26.6 1.6 %collective-permute-start.11 = (bf16[80,1024]{1,0:T(8,128)(2,1)S(1)}, bf16[80,1024]{1,0:T(8,128)(2,1)S(1)}, u32[]{:S(2)}, u32[]{:S(2)}) collective-permute-start(bf16[80,1024]{1,0:T(8,128)(2,1)S(1)} %dynamic-slice_convert_fusion), channel_id=1, source_target_pairs={{0,2},{1,3},{2,0},{3,1},{4,6},{5,7},{6,4},{7,5},{8,10},{9,11},{10,... | collective-permute-start | bytes 491528 | tf_op jit(solution)/shard_map/ppermute | solution.py:280
  28.1 0.0 collective-permute-done.6
  28.1 1.4 %collective-permute-start.8 = (bf16[8,128,256]{2,1,0:T(8,128)(2,1)S(1)}, bf16[8,128,256]{2,1,0:T(8,128)(2,1)S(1)}, u32[]{:S(2)}, u32[]{:S(2)}) collective-permute-start(bf16[8,128,256]{2,1,0:T(8,128)(2,1)S(1)} %bitcast_dynamic-update-slice_fusion.refs_0_), channel_id=1, source_target_pairs={{0,2},{1,3},{2,0},{3,1},{4,6},{5,7},{6,4},{7,5},{8,10},{9,11},{10,... | collective-permute-start | bytes 1572872 | tf_op jit(solution)/shard_map/ppermute | solution.py:280
  29.5 4.2 %collective-permute-done.11 = bf16[80,1024]{1,0:T(8,128)(2,1)S(1)} collective-permute-done((bf16[80,1024]{1,0:T(8,128)(2,1)S(1)}, bf16[80,1024]{1,0:T(8,128)(2,1)S(1)}, u32[]{:S(2)}, u32[]{:S(2)}) %collective-permute-start.11) | collective-permute-done | bytes 163872 | tf_op jit(solution)/shard_map/ppermute | solution.py:280
  33.8 0.7 %bitcast_bitcast_fusion = bf16[8,80,128]{2,1,0:T(8,128)(2,1)} fusion(bf16[80,1024]{1,0:T(8,128)(2,1)S(1)} %collective-permute-done.11, f32[160,1024]{1,0:T(8,128)S(1)} %add.18, s32[]{:T(128)S(6)} %select_n.45), kind=kLoop, calls=%fused_computation.4 | loop fusion | flops 245760 | bytes 655364 | tf_op jit(solution)/shard_map/transpose | solution.py:297
  34.5 5.0 %all-to-all-start = ((bf16[8,80,128]{2,1,0:T(8,128)(2,1)}), bf16[8,80,128]{2,1,0:T(8,128)(2,1)S(1)}, u32[]{:S(2)}, u32[]{:S(2)}) async-start(bf16[8,80,128]{2,1,0:T(8,128)(2,1)} %bitcast_bitcast_fusion), calls=%async_computation | async-start | bytes 327680 | tf_op jit(solution)/shard_map/all_to_all | solution.py:298
  39.4 0.0 collective-permute-start.7
  39.5 3.0 %collective-permute-done.8.refs_2_ = bf16[8,128,256]{2,1,0:T(8,128)(2,1)S(1)} collective-permute-done((bf16[8,128,256]{2,1,0:T(8,128)(2,1)S(1)}, bf16[8,128,256]{2,1,0:T(8,128)(2,1)S(1)}, u32[]{:S(2)}, u32[]{:S(2)}) %collective-permute-start.8) | collective-permute-done | bytes 524320 | tf_op jit(solution)/shard_map/ppermute | solution.py:280
  42.5 4.5 %all-to-all-done = bf16[8,80,128]{2,1,0:T(8,128)(2,1)S(1)} async-done(((bf16[8,80,128]{2,1,0:T(8,128)(2,1)}), bf16[8,80,128]{2,1,0:T(8,128)(2,1)S(1)}, u32[]{:S(2)}, u32[]{:S(2)}) %all-to-all-start) | async-done | bytes 163872 | tf_op jit(solution)/shard_map/all_to_all | solution.py:298
  47.1 1.6 %collective-permute-start.12 = (f32[80,128]{1,0:T(8,128)S(1)}, f32[80,128]{1,0:T(8,128)S(1)}, u32[]{:S(2)}, u32[]{:S(2)}) collective-permute-start(f32[80,128]{1,0:T(8,128)S(1)} %broadcast_multiply_fusion), channel_id=1, source_target_pairs={{0,2},{1,3},{2,0},{3,1},{4,6},{5,7},{6,4},{7,5},{8,10},{9,11},{10,... | collective-permute-start | bytes 122888 | tf_op jit(solution)/shard_map/ppermute | solution.py:280
  48.6 2.5 %collective-permute-done.12 = f32[80,128]{1,0:T(8,128)S(1)} collective-permute-done((f32[80,128]{1,0:T(8,128)S(1)}, f32[80,128]{1,0:T(8,128)S(1)}, u32[]{:S(2)}, u32[]{:S(2)}) %collective-permute-start.12) | collective-permute-done | bytes 40992 | tf_op jit(solution)/shard_map/ppermute | solution.py:280
  51.2 0.1 collective-permute-start.13
  51.3 0.8 %copy-done.3 = bf16[8,128,256]{2,1,0:T(8,128)(2,1)} copy-done((bf16[8,128,256]{2,1,0:T(8,128)(2,1)}, bf16[8,128,256]{2,1,0:T(8,128)(2,1)S(1)}, u32[]{:S(2)}) %copy-start.3) | copy-done | bytes 524312
  52.1 0.2 copy-done.4
  52.3 8.3 %shard_map.104 = (f32[1024,256]{1,0:T(8,128)}, f32[1,1024]{1,0:T(1,128)}) custom-call(s32[3]{0:T(128)} %pad_add_fusion.place, s32[2,4096]{1,0:T(2,128)} %bitcast.51, f32[1024,256]{1,0:T(8,128)} %bitcast.48, f32[1,1024]{1,0:T(1,128)} %accum.1, bf16[8,128,256]{2,1,0:T(8,128)(2,1)} %copy-done, bf16[8,128,256]{2,1,0:T(8,128)(2,1)} %copy-done.3, ...), custom_call_target="tpu_custom_call" | custom-call | tf_op jit(solution)/shard_map/pallas_call | solution.py:197
  60.6 0.7 %fusion.1 = f32[128,292]{0,1:T(8,128)} fusion(f32[160,128]{1,0:T(8,128)S(1)} %get-tuple-element.22, f32[160,128]{1,0:T(8,128)S(1)} %get-tuple-element.21), kind=kLoop, calls=%fused_computation.6 | loop fusion | flops 37376 | bytes 313344 | tf_op jit(solution)/shard_map/transpose | solution.py:307
  (30 shorter events, 0.2 us)
Async XLA Ops:
  7.1 4.2 %copy-start.5 = (f32[160,1024]{1,0:T(8,128)S(1)}, f32[160,1024]{1,0:T(8,128)}, u32[]{:S(2)}) copy-start(f32[160,1024]{1,0:T(8,128)} %get-tuple-element.12) | copy-start | bytes 1966084
  8.2 18.2 %copy-start.1 = (f32[160,1024]{1,0:T(8,128)S(1)}, f32[160,1024]{1,0:T(8,128)}, u32[]{:S(2)}) copy-start(f32[160,1024]{1,0:T(8,128)} %get-tuple-element.11) | copy-start | bytes 1966084
  8.3 7.6 %collective-permute-start = (bf16[128,256]{1,0:T(8,128)(2,1)S(1)}, bf16[128,256]{1,0:T(8,128)(2,1)S(1)}, u32[]{:S(2)}, u32[]{:S(2)}) collective-permute-start(bf16[128,256]{1,0:T(8,128)(2,1)S(1)} %get-tuple-element.19), channel_id=1, source_target_pairs={{0,4},{4,0},{8,12},{12,8},{16,20},{20,16},{24,28},{28,24},{1,5},{5... | collective-permute-start | bytes 196616 | tf_op jit(solution)/shard_map/ppermute | solution.py:280
  11.3 15.1 %collective-permute-start.10 = (f32[160,1024]{1,0:T(8,128)S(1)}, f32[160,1024]{1,0:T(8,128)S(1)}, u32[]{:S(2)}, u32[]{:S(2)}) collective-permute-start(f32[160,1024]{1,0:T(8,128)S(1)} %copy-done.5), channel_id=1, source_target_pairs={{0,1},{1,0},{2,3},{3,2},{4,5},{5,4},{6,7},{7,6},{8,9},{9,8},{10,11... | collective-permute-start | bytes 1966088 | tf_op jit(solution)/shard_map/ppermute | solution.py:280
  11.3 6.3 %collective-permute-start.1 = (bf16[128,256]{1,0:T(8,128)(2,1)S(1)}, bf16[128,256]{1,0:T(8,128)(2,1)S(1)}, u32[]{:S(2)}, u32[]{:S(2)}) collective-permute-start(bf16[128,256]{1,0:T(8,128)(2,1)S(1)} %get-tuple-element.18), channel_id=1, source_target_pairs={{0,8},{4,12},{8,0},{12,4},{16,24},{20,28},{24,16},{28,20},{1,9},{5... | collective-permute-start | bytes 196616 | tf_op jit(solution)/shard_map/ppermute | solution.py:280
  12.9 8.0 %collective-permute-start.2 = (bf16[128,256]{1,0:T(8,128)(2,1)S(1)}, bf16[128,256]{1,0:T(8,128)(2,1)S(1)}, u32[]{:S(2)}, u32[]{:S(2)}) collective-permute-start(bf16[128,256]{1,0:T(8,128)(2,1)S(1)} %get-tuple-element.17), channel_id=1, source_target_pairs={{0,12},{4,8},{8,4},{12,0},{16,28},{20,24},{24,20},{28,16},{1,13},{... | collective-permute-start | bytes 196616 | tf_op jit(solution)/shard_map/ppermute | solution.py:280
  12.9 9.2 %collective-permute-start.3 = (bf16[128,256]{1,0:T(8,128)(2,1)S(1)}, bf16[128,256]{1,0:T(8,128)(2,1)S(1)}, u32[]{:S(2)}, u32[]{:S(2)}) collective-permute-start(bf16[128,256]{1,0:T(8,128)(2,1)S(1)} %get-tuple-element.16), channel_id=1, source_target_pairs={{0,16},{4,20},{8,24},{12,28},{16,0},{20,4},{24,8},{28,12},{1,17},{... | collective-permute-start | bytes 196616 | tf_op jit(solution)/shard_map/ppermute | solution.py:280
  15.9 10.5 %collective-permute-start.4 = (bf16[128,256]{1,0:T(8,128)(2,1)S(1)}, bf16[128,256]{1,0:T(8,128)(2,1)S(1)}, u32[]{:S(2)}, u32[]{:S(2)}) collective-permute-start(bf16[128,256]{1,0:T(8,128)(2,1)S(1)} %get-tuple-element.15), channel_id=1, source_target_pairs={{0,20},{4,16},{8,28},{12,24},{16,4},{20,0},{24,12},{28,8},{1,21},{... | collective-permute-start | bytes 196616 | tf_op jit(solution)/shard_map/ppermute | solution.py:280
  17.6 8.8 %collective-permute-start.5 = (bf16[128,256]{1,0:T(8,128)(2,1)S(1)}, bf16[128,256]{1,0:T(8,128)(2,1)S(1)}, u32[]{:S(2)}, u32[]{:S(2)}) collective-permute-start(bf16[128,256]{1,0:T(8,128)(2,1)S(1)} %get-tuple-element.14), channel_id=1, source_target_pairs={{0,24},{4,28},{8,16},{12,20},{16,8},{20,12},{24,0},{28,4},{1,25},{... | collective-permute-start | bytes 196616 | tf_op jit(solution)/shard_map/ppermute | solution.py:280
  20.8 7.3 %collective-permute-start.6 = (bf16[128,256]{1,0:T(8,128)(2,1)S(1)}, bf16[128,256]{1,0:T(8,128)(2,1)S(1)}, u32[]{:S(2)}, u32[]{:S(2)}) collective-permute-start(bf16[128,256]{1,0:T(8,128)(2,1)S(1)} %get-tuple-element.13), channel_id=1, source_target_pairs={{0,28},{4,24},{8,20},{12,16},{16,12},{20,8},{24,4},{28,0},{1,29},{... | collective-permute-start | bytes 196616 | tf_op jit(solution)/shard_map/ppermute | solution.py:280
  26.6 7.2 %collective-permute-start.11 = (bf16[80,1024]{1,0:T(8,128)(2,1)S(1)}, bf16[80,1024]{1,0:T(8,128)(2,1)S(1)}, u32[]{:S(2)}, u32[]{:S(2)}) collective-permute-start(bf16[80,1024]{1,0:T(8,128)(2,1)S(1)} %dynamic-slice_convert_fusion), channel_id=1, source_target_pairs={{0,2},{1,3},{2,0},{3,1},{4,6},{5,7},{6,4},{7,5},{8,10},{9,11},{10,... | collective-permute-start | bytes 491528 | tf_op jit(solution)/shard_map/ppermute | solution.py:280
  28.1 18.9 %copy-start = (bf16[8,128,256]{2,1,0:T(8,128)(2,1)}, bf16[8,128,256]{2,1,0:T(8,128)(2,1)S(1)}, u32[]{:S(2)}) copy-start(bf16[8,128,256]{2,1,0:T(8,128)(2,1)S(1)} %bitcast_dynamic-update-slice_fusion.refs_0_) | copy-start | bytes 1572868
  28.1 14.4 %collective-permute-start.8 = (bf16[8,128,256]{2,1,0:T(8,128)(2,1)S(1)}, bf16[8,128,256]{2,1,0:T(8,128)(2,1)S(1)}, u32[]{:S(2)}, u32[]{:S(2)}) collective-permute-start(bf16[8,128,256]{2,1,0:T(8,128)(2,1)S(1)} %bitcast_dynamic-update-slice_fusion.refs_0_), channel_id=1, source_target_pairs={{0,2},{1,3},{2,0},{3,1},{4,6},{5,7},{6,4},{7,5},{8,10},{9,11},{10,... | collective-permute-start | bytes 1572872 | tf_op jit(solution)/shard_map/ppermute | solution.py:280
  34.5 12.6 %all-to-all-start = ((bf16[8,80,128]{2,1,0:T(8,128)(2,1)}), bf16[8,80,128]{2,1,0:T(8,128)(2,1)S(1)}, u32[]{:S(2)}, u32[]{:S(2)}) async-start(bf16[8,80,128]{2,1,0:T(8,128)(2,1)} %bitcast_bitcast_fusion), calls=%async_computation | async-start | bytes 327680 | tf_op jit(solution)/shard_map/all_to_all | solution.py:298
  39.4 11.8 %collective-permute-start.7 = (bf16[8,128,256]{2,1,0:T(8,128)(2,1)S(1)}, bf16[8,128,256]{2,1,0:T(8,128)(2,1)S(1)}, u32[]{:S(2)}, u32[]{:S(2)}) collective-permute-start(bf16[8,128,256]{2,1,0:T(8,128)(2,1)S(1)} %bitcast_dynamic-update-slice_fusion.refs_0_), channel_id=1, source_target_pairs={{0,1},{1,0},{2,3},{3,2},{4,5},{5,4},{6,7},{7,6},{8,9},{9,8},{10,11... | collective-permute-start | bytes 1572872 | tf_op jit(solution)/shard_map/ppermute | solution.py:280
  42.5 8.8 %copy-start.2 = (bf16[8,128,256]{2,1,0:T(8,128)(2,1)}, bf16[8,128,256]{2,1,0:T(8,128)(2,1)S(1)}, u32[]{:S(2)}) copy-start(bf16[8,128,256]{2,1,0:T(8,128)(2,1)S(1)} %collective-permute-done.8.refs_2_) | copy-start | bytes 1572868
  42.5 8.8 %collective-permute-start.9 = (bf16[8,128,256]{2,1,0:T(8,128)(2,1)S(1)}, bf16[8,128,256]{2,1,0:T(8,128)(2,1)S(1)}, u32[]{:S(2)}, u32[]{:S(2)}) collective-permute-start(bf16[8,128,256]{2,1,0:T(8,128)(2,1)S(1)} %collective-permute-done.8.refs_2_), channel_id=1, source_target_pairs={{0,1},{1,0},{2,3},{3,2},{4,5},{5,4},{6,7},{7,6},{8,9},{9,8},{10,11... | collective-permute-start | bytes 1572872 | tf_op jit(solution)/shard_map/ppermute | solution.py:280
  47.1 4.1 %collective-permute-start.12 = (f32[80,128]{1,0:T(8,128)S(1)}, f32[80,128]{1,0:T(8,128)S(1)}, u32[]{:S(2)}, u32[]{:S(2)}) collective-permute-start(f32[80,128]{1,0:T(8,128)S(1)} %broadcast_multiply_fusion), channel_id=1, source_target_pairs={{0,2},{1,3},{2,0},{3,1},{4,6},{5,7},{6,4},{7,5},{8,10},{9,11},{10,... | collective-permute-start | bytes 122888 | tf_op jit(solution)/shard_map/ppermute | solution.py:280
  51.2 9.4 %collective-permute-start.13 = (f32[160,128]{1,0:T(8,128)S(1)}, f32[160,128]{1,0:T(8,128)S(1)}, u32[]{:S(2)}, u32[]{:S(2)}) collective-permute-start(f32[160,128]{1,0:T(8,128)S(1)} %pad_maximum_fusion.1), channel_id=1, source_target_pairs={{0,1},{1,0},{2,3},{3,2},{4,5},{5,4},{6,7},{7,6},{8,9},{9,8},{10,11... | collective-permute-start | bytes 245768 | tf_op jit(solution)/shard_map/ppermute | solution.py:280
  51.3 0.8 %copy-start.3 = (bf16[8,128,256]{2,1,0:T(8,128)(2,1)}, bf16[8,128,256]{2,1,0:T(8,128)(2,1)S(1)}, u32[]{:S(2)}) copy-start(bf16[8,128,256]{2,1,0:T(8,128)(2,1)S(1)} %collective-permute-done.7.refs_1_) | copy-start | bytes 1572868
  51.3 1.0 %copy-start.4 = (bf16[8,128,256]{2,1,0:T(8,128)(2,1)}, bf16[8,128,256]{2,1,0:T(8,128)(2,1)S(1)}, u32[]{:S(2)}) copy-start(bf16[8,128,256]{2,1,0:T(8,128)(2,1)S(1)} %collective-permute-done.9.refs_3_) | copy-start | bytes 1572868

commit v2 on v1

--- a/solution.py
+++ b/solution.py
@@ -18,12 +18,9 @@
     return jnp.where(r == c, 1.0, 0.0).astype(jnp.bfloat16)
 
 
-def local_kernel(
-    place, dense_in, pooled_in, w_in, bias_in, d_hidden_in,
-    out, keep, send,
-    dense, pooled, w_t, bias, d_hidden,
-    pooled32, feat_t, zrows, z_t, dp_t, wg, sems,
-):
+def local_kernel(place, dense_in, pooled_in, w_in, bias_in, d_hidden_in, *refs):
+    dense, pooled, w_t, bias, d_hidden, pooled32, feat_t, zrows, z_t, dp_t, wg, sems = refs[-12:]
+    hold, give, keep, send = refs[:4]
     moves = [
         pltpu.make_async_copy(source, target, sems.at[i])
         for i, (source, target) in enumerate(
@@ -99,33 +96,35 @@
 
     lax.fori_loop(0, width // 16, gradients, 0)
     ident_s = eye(samples)
-    for t in range(tables):
-        got = lax.dot_general(ident_s, dp_t[t].astype(jnp.bfloat16), NT, preferred_element_type=jnp.float32)
-        out[jnp.bitwise_xor(wide, t)] = got.astype(jnp.bfloat16)
-
-    half = wg.shape[1]
+    for i in range(tables // 2):
+        for target, side in ((give, 1 - core), (hold, core)):
+            held = dp_t[jnp.bitwise_xor(wide, 2 * i + side)].astype(jnp.bfloat16)
+            got = lax.dot_general(ident_s, held, NT, preferred_element_type=jnp.float32)
+            target[i] = got.astype(jnp.bfloat16)
+    half, block = keep.shape[1:]
     for h in range(2):
-        wg[h] = jnp.dot(z_t[h * half : (h + 1) * half, :], dpre, preferred_element_type=jnp.float32)
+        part = jnp.dot(z_t[h * half : (h + 1) * half, :], dpre, preferred_element_type=jnp.float32)
+        for b in range(tables):
+            wg[h, jnp.bitwise_xor(wide, b)] = part[:, b * block : (b + 1) * block]
     keep[...] = wg[core]
-    send[...] = wg[1 - core].astype(send.dtype)
-
-
-def local_part(place, dense, pooled, w_t, bias, d_hidden, send_type):
+    send[...] = wg[1 - core]
+
+
+def local_part(place, dense, pooled, w_t, bias, d_hidden):
     samples, width = dense.shape
     tables = pooled.shape[1]
     hidden = w_t.shape[1]
-    padded = -(-w_t.shape[0] // 64) * 64
+    padded = -(-w_t.shape[0] // 32) * 32
     half = padded // 2
-    vmem = pl.BlockSpec(memory_space=pltpu.VMEM)
+    vmem, hbm = pl.BlockSpec(memory_space=pltpu.VMEM), pl.BlockSpec(memory_space=pltpu.HBM)
+    gradients = [(tables // 2, samples, width)] * 2
+    operands = (dense, pooled.reshape(samples * tables, width), w_t, bias.reshape(1, hidden), d_hidden)
     return pl.pallas_call(
         local_kernel,
-        out_shape=(
-            jax.ShapeDtypeStruct((tables, samples, width), jnp.bfloat16),
-            jax.ShapeDtypeStruct((half, hidden), jnp.float32),
-            jax.ShapeDtypeStruct((half, hidden), send_type),
-        ),
-        in_specs=[pl.BlockSpec(memory_space=pltpu.SMEM)] + [pl.BlockSpec(memory_space=pltpu.HBM)] * 5,
-        out_specs=(vmem,) * 3,
+        out_shape=[jax.ShapeDtypeStruct(shape, jnp.bfloat16) for shape in gradients]
+        + [jax.ShapeDtypeStruct((tables, half, hidden // tables), jnp.float32)] * 2,
+        in_specs=[pl.BlockSpec(memory_space=pltpu.SMEM)] + [hbm] * 5,
+        out_specs=[vmem] * (len(gradients) + 2),
         scratch_shapes=[
             pltpu.VMEM((samples, width), dense.dtype),
             pltpu.VMEM((samples * tables, width), pooled.dtype),
@@ -137,74 +136,138 @@
             pltpu.VMEM((128, samples), jnp.float32),
             pltpu.VMEM((padded, samples), jnp.bfloat16),
             pltpu.VMEM((tables, width, samples), jnp.float32),
-            pltpu.VMEM((2, half, hidden), jnp.float32),
+            pltpu.VMEM((2, tables, half, hidden // tables), jnp.float32),
             pltpu.SemaphoreType.DMA((5,)),
         ],
-        compiler_params=pltpu.CompilerParams(vmem_limit_bytes=60 * 2**20),
-    )(place, dense, pooled.reshape(samples * tables, width), w_t, bias.reshape(1, hidden), d_hidden)
-
-
-def update_kernel(place, ids, table, accum, *refs):
-    grads, (new_table, new_accum, ids_a, ids_b) = refs[:4], refs[4:]
-    rows, width = table.shape
-    blocks, samples = grads[0].shape[:2]
-    n_narrow = 4
-    wide, narrow = place[0], place[2]
-    step = 16
+        compiler_params=pltpu.CompilerParams(vmem_limit_bytes=14 * 2**20),
+    )(place, *[pltpu.with_memory_space_constraint(x, pltpu.HBM) for x in operands])
+
+
+def row_kernel(groups, first, last, joined, n_narrow, rows, place, ids, *refs):
+    refs = list(refs)
+    table_in, accum = (refs.pop(0), refs.pop(0)) if last else (None, None)
+    before_in = None if first else refs.pop(0)
+    grads = [refs.pop(0) for _ in groups]
+    out_sems, sems, done = refs.pop(), refs.pop(), refs.pop()
+    loads = []
+
+    def load(source, target):
+        move = pltpu.make_async_copy(source, target, sems.at[len(loads)])
+        move.start()
+        loads.append(move)
+
+    if not first:
+        before = refs.pop()
+        load(before_in, before)
+    if last:
+        spread, table = refs.pop(), refs.pop()
+        load(table_in, table)
+        new_table, new_accum = refs.pop(0), refs.pop(0)
+    else:
+        sums = refs.pop(0)
+        if joined:
+            whole, start = refs.pop(0), 0
+            for i in joined:
+                whole[start : start + grads[i].shape[0]] = grads[i][...]
+                start += grads[i].shape[0]
+    kept = refs
+    wide, core, narrow = place[0], place[1], place[2]
+    samples, width = grads[0].shape[1:]
+    step, tile, lane = 16, min(512, rows), 128
     down = lax.broadcasted_iota(jnp.int32, (step, samples), 0)
-    for j in range(4):
-        for k in range(blocks):
-            at = jnp.bitwise_xor(wide, k) * n_narrow + jnp.bitwise_xor(narrow, j)
+    for pieces, keep in zip(groups, kept):
+        for i, (j, k, flip) in enumerate(pieces):
+            at = jnp.bitwise_xor(wide, 2 * k + jnp.bitwise_xor(core, flip)) * n_narrow + jnp.bitwise_xor(narrow, j)
             local = ids[:, pl.ds(pl.multiple_of(at * samples, samples), samples)] - narrow * rows
-            for s, keep in enumerate((ids_a, ids_b)):
-                keep[j, :, k * samples : (k + 1) * samples] = (
+            for s in range(2):
+                keep[s, :, i * samples : (i + 1) * samples] = (
                     jnp.broadcast_to(local[s : s + 1, :], (step, samples)) - down
                 ).astype(jnp.int16)
-    tile = 128
     one, none = jnp.bfloat16(1), jnp.bfloat16(0)
-    scale_rows = width
-
-    def tile_step(m, carry):
+
+    leave = []
+    for m in range(rows // tile):
         base = m * tile
-        total = jnp.zeros((tile, width), jnp.float32)
-        for j in range(4):
-            a, b = ids_a[j], ids_b[j]
+        at = slice(base, base + tile)
+        total = None
+        for grad, keep in zip(grads, kept):
+            a, b = keep[0], keep[1]
             parts = []
             for i in range(tile // step):
-                want = (base + i * step).astype(jnp.int16)
+                want = jnp.int16(base + i * step)
                 parts.append(jnp.where(a == want, one, none) + jnp.where(b == want, one, none))
             hot = jnp.concatenate(parts, axis=0)
-            total += jnp.dot(hot, grads[j][...].reshape(blocks * samples, width), preferred_element_type=jnp.float32)
-        at = pl.ds(pl.multiple_of(base, tile), tile)
-        mean = jnp.sum(total * total, axis=1, keepdims=True) * (1.0 / width)
-        row = jnp.broadcast_to(mean, (tile, tile)).T[:1, :]
-        fresh = accum[:, at] + row
-        new_accum[:, at] = fresh
-        rate = 0.1 / (jnp.sqrt(fresh) + 1e-8)
-        rate = jnp.broadcast_to(rate, (tile, tile)).T
-        for h in range(width // tile):
-            cols = slice(h * tile, (h + 1) * tile)
-            new_table[at, cols] = table[at, cols] - total[:, cols] * rate
-        return carry
-
-    lax.fori_loop(0, rows // tile, tile_step, 0)
-
-
-def update_part(place, ids, table, accum, grads):
-    rows, width = table.shape
-    blocks, samples = grads[0].shape[:2]
-    vmem = pl.BlockSpec(memory_space=pltpu.VMEM)
+            term = jnp.dot(hot, grad[...].reshape(-1, width), preferred_element_type=jnp.float32)
+            total = term if total is None else total + term
+        if not first:
+            if m == 0:
+                loads[0].wait()
+            total = total + before[at, :]
+        done[at, :] = total
+        if last:
+            mean = jnp.sum(total * total, axis=1, keepdims=True) * (1.0 / width)
+            spread[at, :] = jnp.broadcast_to(mean, (tile, lane))
+        else:
+            out = pltpu.make_async_copy(done.at[at, :], sums.at[at, :], out_sems.at[m])
+            out.start()
+            leave.append(out)
+    if not last:
+        for out in leave:
+            out.wait()
+        return
+    parts = [slice(i * lane, (i + 1) * lane) for i in range(rows // lane)]
+    mean = jnp.concatenate([spread[part, :].T[:1, :] for part in parts], axis=1)
+    fresh = accum[...] + mean
+    new_accum[...] = fresh
+    rate = 0.1 / (jnp.sqrt(fresh) + 1e-8)
+    loads[-1].wait()
+    for i, part in enumerate(parts):
+        by_row = jnp.broadcast_to(rate[:, part], (lane, lane)).T
+        for h in range(width // lane):
+            cols = slice(h * lane, (h + 1) * lane)
+            table[part, cols] = table[part, cols] - done[part, cols] * by_row
+        out = pltpu.make_async_copy(table.at[part, :], new_table.at[part, :], out_sems.at[i])
+        out.start()
+        leave.append(out)
+    for out in leave:
+        out.wait()
+
+
+def row_part(groups, place, ids, grads, rows, n_narrow, before=None, table=None, accum=None, joined=()):
+    samples, width = grads[0].shape[1:]
+    first, last = before is None, table is not None
+    vmem, hbm = pl.BlockSpec(memory_space=pltpu.VMEM), pl.BlockSpec(memory_space=pltpu.HBM)
+    operands = ([table, accum] if last else []) + ([] if first else [before]) + list(grads)
+    sums = jax.ShapeDtypeStruct((rows, width), jnp.float32)
+    if last:
+        out_shape = (sums, jax.ShapeDtypeStruct((1, rows), jnp.float32))
+    elif joined:
+        out_shape = (sums, jax.ShapeDtypeStruct((sum(len(groups[i]) for i in joined), samples, width), grads[0].dtype))
+    else:
+        out_shape = (sums,)
+    scratch = [pltpu.VMEM((2, 16, len(pieces) * samples), jnp.int16) for pieces in groups]
+    whole = pltpu.VMEM((rows, width), jnp.float32)
+    if last:
+        scratch += [whole, pltpu.VMEM((rows, 128), jnp.float32)]
+    if not first:
+        scratch += [whole]
+    scratch += [whole, pltpu.SemaphoreType.DMA((2,)), pltpu.SemaphoreType.DMA((rows // 128,))]
     return pl.pallas_call(
-        update_kernel,
-        out_shape=(
-            jax.ShapeDtypeStruct((rows, width), jnp.float32),
-            jax.ShapeDtypeStruct((1, rows), jnp.float32),
+        functools.partial(row_kernel, groups, first, last, joined, n_narrow, rows),
+        out_shape=out_shape,
+        in_specs=[pl.BlockSpec(memory_space=pltpu.SMEM), vmem]
+        + ([hbm, vmem] if last else [])
+        + ([] if first else [hbm])
+        + [vmem] * len(grads),
+        out_specs=(hbm, vmem)[: len(out_shape)],
+        scratch_shapes=scratch,
+        compiler_params=pltpu.CompilerParams(vmem_limit_bytes=14 * 2**20),
+        cost_estimate=pl.CostEstimate(
+            flops=2 * rows * samples * width * sum(len(pieces) for pieces in groups),
+            bytes_accessed=8 * rows * width,
+            transcendentals=0,
         ),
-        in_specs=[pl.BlockSpec(memory_space=pltpu.SMEM)] + [vmem] * 7,
-        out_specs=(vmem,) * 2,
-        scratch_shapes=[pltpu.VMEM((4, 16, blocks * samples), jnp.int16)] * 2,
-        compiler_params=pltpu.CompilerParams(vmem_limit_bytes=60 * 2**20),
-    )(place, ids, table, accum, *grads)
+    )(place, ids, *operands)
 
 
 def row_sums(grads, ids, offset, count):
@@ -279,29 +342,50 @@
         n = lax.axis_size(axis)
         return lax.ppermute(array, axis, [(i, i ^ bit) for i in range(n)])
 
-    out, keep, send = local_part(place, dense, pooled, w_top.T, bias, d_hidden, jnp.float32)
-    owned = jnp.stack([out[0]] + [swap(out[k], "wide", k) for k in range(1, n_wide)])
-    beside = swap(owned, "narrow", 1)
-    across = swap(owned, "narrow", 2)
+    out = local_part(place, dense, pooled, w_top.T, bias, d_hidden)
+    hold, give, keep, send = out
+    ids = bag_ids[0].T
+    tie = lambda *values: lax.optimization_barrier(values)
+    taken = swap(give, "narrow", 1)
+    received = swap(send, "narrow", 1)
+
+    def reach(i):
+        lead = jnp.stack([hold[i], taken[i]])
+        pairs = [
+            (w * n_narrow + n, (w ^ (2 * i + n % 2)) * n_narrow + n) for w in range(n_wide) for n in range(n_narrow)
+        ]
+        return lax.ppermute(lead, ("wide", "narrow"), pairs)
+
+    got = {i: reach(i) for i in (1, 0, 2, 3)}
+    got[0], got[1], received = tie(got[0], got[1], received)
+    half = keep + received
+    half_y = swap(half[1::2].astype(jnp.bfloat16), "wide", 1)
+    near = jnp.concatenate([got[0], got[1]])
+    across_near = swap(near, "narrow", 2)
+    half = half[0::2] + half_y.astype(jnp.float32)
+    half_z = swap(half[1::2].astype(jnp.bfloat16), "wide", 2)
+    got[2], got[3], half_z, across_near = tie(got[2], got[3], half_z, across_near)
+    far = jnp.concatenate([got[2], got[3]])
+    across_far = swap(far, "narrow", 2)
+    half = half[0::2] + half_z.astype(jnp.float32)
+    half_zz = swap(half[1::2].astype(jnp.bfloat16), "wide", 4)
+    mine = jnp.concatenate([near, far])
+    beside = swap(mine, "narrow", 1)
+    across_far, half_zz = tie(across_far, half_zz)
+    across = jnp.concatenate([across_near, across_far])
     opposite = swap(across, "narrow", 1)
-    ids = bag_ids[0].T
-    new_table, new_accum = update_part(place, ids, tables[0], accum, [owned, beside, across, opposite])
-
-    half = keep + swap(send, "narrow", 1)
-    quarter = half.shape[0] // 2
-    mine = lax.dynamic_slice_in_dim(half, chip * quarter, quarter, 0)
-    theirs = lax.dynamic_slice_in_dim(half, (1 - chip) * quarter, quarter, 0)
-    mine = mine + swap(theirs.astype(jnp.bfloat16), "narrow", 2).astype(jnp.float32)
-    hidden = mine.shape[1]
-    block = hidden // n_wide
-    blocks = jnp.transpose(mine.astype(jnp.bfloat16).reshape(quarter, n_wide, block), (1, 0, 2))
-    got = lax.all_to_all(blocks, "wide", 0, 0, tiled=True)
-    part = jnp.sum(got.astype(jnp.float32), axis=0) / math.sqrt(total)
-    other = swap(part, "narrow", 2)
-    low = jnp.where(chip == 0, part, other)
-    high = jnp.where(chip == 0, other, part)
-    part = jnp.concatenate([low, high], axis=0)
+    half = half[0::2] + half_zz.astype(jnp.float32)
+    part = half[0] / math.sqrt(total)
+    part_x = swap(part, "narrow", 2)
+    opposite, part_x = tie(opposite, part_x)
+    part = part + part_x
     other = swap(part, "narrow", 1)
+    pieces = lambda j, flip: tuple((j ^ s, i, flip) for i in range(n_wide // 2) for s in range(2))
+    new_table, new_accum = row_part(
+        [pieces(0, 0), pieces(1, 1), pieces(2, 0), pieces(3, 1)],
+        place, ids, [mine, beside, across, opposite], rows, n_narrow, table=tables[0], accum=accum,
+    )
+    other, new_accum = tie(other, new_accum)
     low = jnp.where(core == 0, part, other)
     high = jnp.where(core == 0, other, part)
     w_grad = jnp.concatenate([low, high], axis=0)[:inputs].T

time: 61.6 us -> 46.1 us (0.75)
  Pallas kernels: 14.1 us -> 9.57 us
  waiting for transfers between devices: 18.5 us -> 14.3 us
  starting transfers between devices: 23.4 us -> 19.8 us
  local copies, waits for them, and re-layouts: 2.21 us -> 0.15 us
  other arithmetic: 2.19 us -> 1.06 us
    ppermute x0 -> x4, starting transfers between devices: none -> 6.4 us  [reach(): return lax.ppermute(lead, ('wide', 'narrow'), pairs)]
    all_to_all x1 -> x0, starting transfers between devices: 4.99 us -> none  [body(): got = lax.all_to_all(blocks, 'wide', 0, 0, tiled=True)]
    ppermute x14 -> x11, starting transfers between devices: 18.4 us -> 13.4 us  [swap(): return lax.ppermute(array, axis, [(i, i ^ bit) for i in range(n)])]
    pallas_call x2, Pallas kernels: 14.1 us -> 9.57 us  [the longest x1 4.97 us: row_part(): pl.pallas_call(functools.partial(row_kernel, groups, first, last, joined,...]
    all_to_all x1 -> x0, waiting for transfers between devices: 4.51 us -> none  [body(): got = lax.all_to_all(blocks, 'wide', 0, 0, tiled=True)]
    squeeze x1 -> x0, local copies, waits for them, and re-layouts: 1.16 us -> none  [body(): out[k]]
    unnamed x18 -> x10, local copies, waits for them, and re-layouts: 1.02 us -> 0.06 us
    transpose x1 -> x0, other arithmetic: 0.7 us -> none  [body(): jnp.transpose(mine.astype(jnp.bfloat16).reshape(quarter, n_wide, block),...]
  transfers between devices with their start and end apart: 15 -> 15, of which waited for: 5 -> 7; matrix products, arithmetic and copies ran while one was open for 1% -> 1% of each run, Pallas kernels for 14% -> 11%
where the time goes in v2:
time: 46.1 us; the launch traced here: 45.8 us
  starting transfers between devices  19.8 us (43%)
  waiting for transfers between devices  14.3 us (31%)
  Pallas kernels  9.57 us (21%)
  other arithmetic  1.06 us (2%)
  between operations  0.89 us (2%)
    ppermute x11, waiting for transfers between devices, swap(): return lax.ppermute(array, axis, [(i, i ^ bit) for i in range(n)])  14.1 us
    ppermute x11, starting transfers between devices, swap(): return lax.ppermute(array, axis, [(i, i ^ bit) for i in range(n)])  13.4 us
    ppermute x4, starting transfers between devices, reach(): return lax.ppermute(lead, ('wide', 'narrow'), pairs)  6.4 us
    pallas_call x1, Pallas kernels, row_part(): pl.pallas_call(functools.partial(row_kernel, groups, first, last, joined,...  4.97 us
    pallas_call x1, Pallas kernels, local_part(): pl.pallas_call(local_kernel, out_shape=[jax.ShapeDtypeStruct(shape, jnp.b...  4.61 us
  transfers between devices with their start and end apart: 15, of which 7 were waited for; matrix products, arithmetic and copies ran while one was open for 1% of the time, Pallas kernels for 11%

profile of v2, /device:TPU:0, one launch (start us, length us, event | category | flops | bytes accessed | tf_op | source)
XLA Modules:
  0.0 45.8 jit_solution(18387176225806097876)
XLA Ops:
  0.6 0.1 pad_add_fusion.place
  0.7 4.6 %shard_map.103 = (bf16[4,128,256]{2,1,0:T(8,128)(2,1)S(1)}, bf16[4,128,256]{2,1,0:T(8,128)(2,1)S(1)}, f32[8,160,128]{2,1,0:T(8,128)S(1)}, f32[8,160,128]{2,1,0:T(8,128)S(1)}) custom-call(s32[3]{0:T(128)S(1)} %pad_add_fusion.place, bf16[128,256]{1,0:T(8,128)(2,1)} %dense_in.1, bf16[1024,256]{1,0:T(8,128)(2,1)} %bitcast.18, bf16[292,1024]{1,0:T(8,128)(2,1)} %bitcast.17, ...), custom_call_target="tpu_custom_call" | custom-call | tf_op jit(solution)/shard_map/pallas_call | solution.py:122
  5.3 0.5 %collective-permute-start = (bf16[4,128,256]{2,1,0:T(8,128)(2,1)S(1)}, bf16[4,128,256]{2,1,0:T(8,128)(2,1)S(1)}, u32[]{:S(2)}, u32[]{:S(2)}) collective-permute-start(bf16[4,128,256]{2,1,0:T(8,128)(2,1)S(1)} %get-tuple-element.23), channel_id=1, source_target_pairs={{0,1},{1,0},{2,3},{3,2},{4,5},{5,4},{6,7},{7,6},{8,9},{9,8},{10,11... | collective-permute-start | bytes 786440 | tf_op jit(solution)/shard_map/ppermute | solution.py:343
  5.9 0.1 collective-permute-start.3
  6.0 1.1 %collective-permute-done = bf16[4,128,256]{2,1,0:T(8,128)(2,1)S(1)} collective-permute-done((bf16[4,128,256]{2,1,0:T(8,128)(2,1)S(1)}, bf16[4,128,256]{2,1,0:T(8,128)(2,1)S(1)}, u32[]{:S(2)}, u32[]{:S(2)}) %collective-permute-start) | collective-permute-done | bytes 262176 | tf_op jit(solution)/shard_map/ppermute | solution.py:343
  7.1 0.7 %collective-permute-start.1 = (bf16[2,128,256]{2,1,0:T(8,128)(2,1)S(1)}, bf16[2,128,256]{2,1,0:T(8,128)(2,1)S(1)}, u32[]{:S(2)}, u32[]{:S(2)}) collective-permute-start(bf16[2,128,256]{2,1,0:T(8,128)(2,1)S(1)} %pad_maximum_fusion.3), channel_id=1, source_target_pairs={{0,0},{1,5},{2,2},{3,7},{4,4},{5,1},{6,6},{7,3},{8,8},{9,13},{10,1... | collective-permute-start | bytes 393224 | tf_op jit(solution)/shard_map/ppermute | solution.py:357
  7.8 3.0 %collective-permute-start.2 = (bf16[2,128,256]{2,1,0:T(8,128)(2,1)S(1)}, bf16[2,128,256]{2,1,0:T(8,128)(2,1)S(1)}, u32[]{:S(2)}, u32[]{:S(2)}) collective-permute-start(bf16[2,128,256]{2,1,0:T(8,128)(2,1)S(1)} %pad_maximum_fusion.4), channel_id=1, source_target_pairs={{0,8},{1,13},{2,10},{3,15},{4,12},{5,9},{6,14},{7,11},{8,0},{9,5},... | collective-permute-start | bytes 393224 | tf_op jit(solution)/shard_map/ppermute | solution.py:357
  10.8 2.7 %collective-permute-start.4 = (bf16[2,128,256]{2,1,0:T(8,128)(2,1)S(1)}, bf16[2,128,256]{2,1,0:T(8,128)(2,1)S(1)}, u32[]{:S(2)}, u32[]{:S(2)}) collective-permute-start(bf16[2,128,256]{2,1,0:T(8,128)(2,1)S(1)} %pad_maximum_fusion.5), channel_id=1, source_target_pairs={{0,16},{1,21},{2,18},{3,23},{4,20},{5,17},{6,22},{7,19},{8,24},{9,... | collective-permute-start | bytes 393224 | tf_op jit(solution)/shard_map/ppermute | solution.py:357
  13.5 0.1 collective-permute-start.5
  13.5 0.0 collective-permute-done.1
  13.5 0.2 collective-permute-done.2
  13.7 0.1 fusion.4
  13.8 2.0 %collective-permute-start.6 = (bf16[4,160,128]{2,1,0:T(8,128)(2,1)S(1)}, bf16[4,160,128]{2,1,0:T(8,128)(2,1)S(1)}, u32[]{:S(2)}, u32[]{:S(2)}) collective-permute-start(bf16[4,160,128]{2,1,0:T(8,128)(2,1)S(1)} %slice.59), channel_id=1, source_target_pairs={{0,4},{4,0},{8,12},{12,8},{16,20},{20,16},{24,28},{28,24},{1,5},{5... | collective-permute-start | bytes 491528 | tf_op jit(solution)/shard_map/ppermute | solution.py:343
  15.9 1.6 %collective-permute-start.8 = (bf16[4,128,256]{2,1,0:T(8,128)(2,1)S(1)}, bf16[4,128,256]{2,1,0:T(8,128)(2,1)S(1)}, u32[]{:S(2)}, u32[]{:S(2)}) collective-permute-start(bf16[4,128,256]{2,1,0:T(8,128)(2,1)S(1)} %pad_maximum_fusion), channel_id=1, source_target_pairs={{0,2},{1,3},{2,0},{3,1},{4,6},{5,7},{6,4},{7,5},{8,10},{9,11},{10,... | collective-permute-start | bytes 786440 | tf_op jit(solution)/shard_map/ppermute | solution.py:343
  17.5 2.6 %collective-permute-done.6 = bf16[4,160,128]{2,1,0:T(8,128)(2,1)S(1)} collective-permute-done((bf16[4,160,128]{2,1,0:T(8,128)(2,1)S(1)}, bf16[4,160,128]{2,1,0:T(8,128)(2,1)S(1)}, u32[]{:S(2)}, u32[]{:S(2)}) %collective-permute-start.6) | collective-permute-done | bytes 163872 | tf_op jit(solution)/shard_map/ppermute | solution.py:343
  20.1 0.1 fusion.3
  20.1 2.9 %collective-permute-start.7 = (bf16[2,160,128]{2,1,0:T(8,128)(2,1)S(1)}, bf16[2,160,128]{2,1,0:T(8,128)(2,1)S(1)}, u32[]{:S(2)}, u32[]{:S(2)}) collective-permute-start(bf16[2,160,128]{2,1,0:T(8,128)(2,1)S(1)} %slice.60), channel_id=1, source_target_pairs={{0,8},{4,12},{8,0},{12,4},{16,24},{20,28},{24,16},{28,20},{1,9},{5... | collective-permute-start | bytes 245768 | tf_op jit(solution)/shard_map/ppermute | solution.py:343
  23.0 0.0 collective-permute-done.4
  23.0 3.0 %collective-permute-done.7 = bf16[2,160,128]{2,1,0:T(8,128)(2,1)S(1)} collective-permute-done((bf16[2,160,128]{2,1,0:T(8,128)(2,1)S(1)}, bf16[2,160,128]{2,1,0:T(8,128)(2,1)S(1)}, u32[]{:S(2)}, u32[]{:S(2)}) %collective-permute-start.7) | collective-permute-done | bytes 81952 | tf_op jit(solution)/shard_map/ppermute | solution.py:343
  26.0 0.0 collective-permute-done.8
  26.1 1.6 %collective-permute-start.10 = (bf16[4,128,256]{2,1,0:T(8,128)(2,1)S(1)}, bf16[4,128,256]{2,1,0:T(8,128)(2,1)S(1)}, u32[]{:S(2)}, u32[]{:S(2)}) collective-permute-start(bf16[4,128,256]{2,1,0:T(8,128)(2,1)S(1)} %pad_maximum_fusion.1), channel_id=1, source_target_pairs={{0,2},{1,3},{2,0},{3,1},{4,6},{5,7},{6,4},{7,5},{8,10},{9,11},{10,... | collective-permute-start | bytes 786440 | tf_op jit(solution)/shard_map/ppermute | solution.py:343
  27.7 0.0 copy-start
  27.7 2.6 %collective-permute-start.11 = (bf16[1,160,128]{2,1,0:T(8,128)(2,1)S(1)}, bf16[1,160,128]{2,1,0:T(8,128)(2,1)S(1)}, u32[]{:S(2)}, u32[]{:S(2)}) collective-permute-start(bf16[1,160,128]{2,1,0:T(8,128)(2,1)S(1)} %slice.79), channel_id=1, source_target_pairs={{0,16},{4,20},{8,24},{12,28},{16,0},{20,4},{24,8},{28,12},{1,17},{... | collective-permute-start | bytes 122888 | tf_op jit(solution)/shard_map/ppermute | solution.py:343
  30.3 2.4 %collective-permute-done.11 = bf16[1,160,128]{2,1,0:T(8,128)(2,1)S(1)} collective-permute-done((bf16[1,160,128]{2,1,0:T(8,128)(2,1)S(1)}, bf16[1,160,128]{2,1,0:T(8,128)(2,1)S(1)}, u32[]{:S(2)}, u32[]{:S(2)}) %collective-permute-start.11) | collective-permute-done | bytes 40992 | tf_op jit(solution)/shard_map/ppermute | solution.py:343
  32.6 2.1 %collective-permute-done.10 = bf16[4,128,256]{2,1,0:T(8,128)(2,1)S(1)} collective-permute-done((bf16[4,128,256]{2,1,0:T(8,128)(2,1)S(1)}, bf16[4,128,256]{2,1,0:T(8,128)(2,1)S(1)}, u32[]{:S(2)}, u32[]{:S(2)}) %collective-permute-start.10) | collective-permute-done | bytes 262176 | tf_op jit(solution)/shard_map/ppermute | solution.py:343
  34.8 0.1 collective-permute-start.12
  34.9 0.6 %collective-permute-start.9 = (bf16[8,128,256]{2,1,0:T(8,128)(2,1)S(1)}, bf16[8,128,256]{2,1,0:T(8,128)(2,1)S(1)}, u32[]{:S(2)}, u32[]{:S(2)}) collective-permute-start(bf16[8,128,256]{2,1,0:T(8,128)(2,1)S(1)} %constant_dynamic-update-slice_fusion.refs_2_), channel_id=1, source_target_pairs={{0,1},{1,0},{2,3},{3,2},{4,5},{5,4},{6,7},{7,6},{8,9},{9,8},{10,11... | collective-permute-start | bytes 1572872 | tf_op jit(solution)/shard_map/ppermute | solution.py:343
  35.5 1.6 %collective-permute-start.13 = (f32[160,128]{1,0:T(8,128)S(1)}, f32[160,128]{1,0:T(8,128)S(1)}, u32[]{:S(2)}, u32[]{:S(2)}) collective-permute-start(f32[160,128]{1,0:T(8,128)S(1)} %fusion.2), channel_id=1, source_target_pairs={{0,2},{1,3},{2,0},{3,1},{4,6},{5,7},{6,4},{7,5},{8,10},{9,11},{10,... | collective-permute-start | bytes 245768 | tf_op jit(solution)/shard_map/ppermute | solution.py:343
  37.1 2.9 %collective-permute-done.13 = f32[160,128]{1,0:T(8,128)S(1)} collective-permute-done((f32[160,128]{1,0:T(8,128)S(1)}, f32[160,128]{1,0:T(8,128)S(1)}, u32[]{:S(2)}, u32[]{:S(2)}) %collective-permute-start.13) | collective-permute-done | bytes 81952 | tf_op jit(solution)/shard_map/ppermute | solution.py:343
  40.0 0.1 collective-permute-start.14
  40.1 5.0 %shard_map.104 = (f32[1024,256]{1,0:T(8,128)}, f32[1,1024]{1,0:T(1,128)}) custom-call(s32[3]{0:T(128)S(1)} %pad_add_fusion.place, s32[2,4096]{1,0:T(2,128)S(1)} %bitcast.16, f32[1024,256]{1,0:T(8,128)S(1)} %bitcast.15, f32[1,1024]{1,0:T(1,128)S(1)} %copy-done.2, bf16[8,128,256]{2,1,0:T(8,128)(2,1)S(1)} %constant_dynamic-update-slice_fusion.refs_2_, ...), custom_call_target="tpu_custom_call" | custom-call | flops 2147483648 | bytes 2097152 | tf_op jit(solution)/shard_map/pallas_call | solution.py:255
  45.1 0.7 %fusion = f32[128,292]{0,1:T(8,128)} fusion(f32[160,128]{1,0:T(8,128)S(1)} %get-tuple-element.54, f32[160,128]{1,0:T(8,128)S(1)} %get-tuple-element.53), kind=kLoop, calls=%fused_computation.5 | loop fusion | flops 37376 | bytes 313344 | tf_op jit(solution)/shard_map/transpose | solution.py:391
  (31 shorter events, 0.3 us)
Async XLA Ops:
  5.3 1.7 %collective-permute-start = (bf16[4,128,256]{2,1,0:T(8,128)(2,1)S(1)}, bf16[4,128,256]{2,1,0:T(8,128)(2,1)S(1)}, u32[]{:S(2)}, u32[]{:S(2)}) collective-permute-start(bf16[4,128,256]{2,1,0:T(8,128)(2,1)S(1)} %get-tuple-element.23), channel_id=1, source_target_pairs={{0,1},{1,0},{2,3},{3,2},{4,5},{5,4},{6,7},{7,6},{8,9},{9,8},{10,11... | collective-permute-start | bytes 786440 | tf_op jit(solution)/shard_map/ppermute | solution.py:343
  5.9 7.9 %collective-permute-start.3 = (f32[8,160,128]{2,1,0:T(8,128)S(1)}, f32[8,160,128]{2,1,0:T(8,128)S(1)}, u32[]{:S(2)}, u32[]{:S(2)}) collective-permute-start(f32[8,160,128]{2,1,0:T(8,128)S(1)} %get-tuple-element.24), channel_id=1, source_target_pairs={{0,1},{1,0},{2,3},{3,2},{4,5},{5,4},{6,7},{7,6},{8,9},{9,8},{10,11... | collective-permute-start | bytes 1966088 | tf_op jit(solution)/shard_map/ppermute | solution.py:343
  7.1 6.5 %collective-permute-start.1 = (bf16[2,128,256]{2,1,0:T(8,128)(2,1)S(1)}, bf16[2,128,256]{2,1,0:T(8,128)(2,1)S(1)}, u32[]{:S(2)}, u32[]{:S(2)}) collective-permute-start(bf16[2,128,256]{2,1,0:T(8,128)(2,1)S(1)} %pad_maximum_fusion.3), channel_id=1, source_target_pairs={{0,0},{1,5},{2,2},{3,7},{4,4},{5,1},{6,6},{7,3},{8,8},{9,13},{10,1... | collective-permute-start | bytes 393224 | tf_op jit(solution)/shard_map/ppermute | solution.py:357
  7.8 6.0 %collective-permute-start.2 = (bf16[2,128,256]{2,1,0:T(8,128)(2,1)S(1)}, bf16[2,128,256]{2,1,0:T(8,128)(2,1)S(1)}, u32[]{:S(2)}, u32[]{:S(2)}) collective-permute-start(bf16[2,128,256]{2,1,0:T(8,128)(2,1)S(1)} %pad_maximum_fusion.4), channel_id=1, source_target_pairs={{0,8},{1,13},{2,10},{3,15},{4,12},{5,9},{6,14},{7,11},{8,0},{9,5},... | collective-permute-start | bytes 393224 | tf_op jit(solution)/shard_map/ppermute | solution.py:357
  10.8 12.2 %collective-permute-start.4 = (bf16[2,128,256]{2,1,0:T(8,128)(2,1)S(1)}, bf16[2,128,256]{2,1,0:T(8,128)(2,1)S(1)}, u32[]{:S(2)}, u32[]{:S(2)}) collective-permute-start(bf16[2,128,256]{2,1,0:T(8,128)(2,1)S(1)} %pad_maximum_fusion.5), channel_id=1, source_target_pairs={{0,16},{1,21},{2,18},{3,23},{4,20},{5,17},{6,22},{7,19},{8,24},{9,... | collective-permute-start | bytes 393224 | tf_op jit(solution)/shard_map/ppermute | solution.py:357
  13.5 9.6 %collective-permute-start.5 = (bf16[2,128,256]{2,1,0:T(8,128)(2,1)S(1)}, bf16[2,128,256]{2,1,0:T(8,128)(2,1)S(1)}, u32[]{:S(2)}, u32[]{:S(2)}) collective-permute-start(bf16[2,128,256]{2,1,0:T(8,128)(2,1)S(1)} %pad_maximum_fusion.6), channel_id=1, source_target_pairs={{0,24},{1,29},{2,26},{3,31},{4,28},{5,25},{6,30},{7,27},{8,16},{9,... | collective-permute-start | bytes 393224 | tf_op jit(solution)/shard_map/ppermute | solution.py:357
  13.8 6.2 %collective-permute-start.6 = (bf16[4,160,128]{2,1,0:T(8,128)(2,1)S(1)}, bf16[4,160,128]{2,1,0:T(8,128)(2,1)S(1)}, u32[]{:S(2)}, u32[]{:S(2)}) collective-permute-start(bf16[4,160,128]{2,1,0:T(8,128)(2,1)S(1)} %slice.59), channel_id=1, source_target_pairs={{0,4},{4,0},{8,12},{12,8},{16,20},{20,16},{24,28},{28,24},{1,5},{5... | collective-permute-start | bytes 491528 | tf_op jit(solution)/shard_map/ppermute | solution.py:343
  15.9 10.1 %collective-permute-start.8 = (bf16[4,128,256]{2,1,0:T(8,128)(2,1)S(1)}, bf16[4,128,256]{2,1,0:T(8,128)(2,1)S(1)}, u32[]{:S(2)}, u32[]{:S(2)}) collective-permute-start(bf16[4,128,256]{2,1,0:T(8,128)(2,1)S(1)} %pad_maximum_fusion), channel_id=1, source_target_pairs={{0,2},{1,3},{2,0},{3,1},{4,6},{5,7},{6,4},{7,5},{8,10},{9,11},{10,... | collective-permute-start | bytes 786440 | tf_op jit(solution)/shard_map/ppermute | solution.py:343
  20.1 5.9 %collective-permute-start.7 = (bf16[2,160,128]{2,1,0:T(8,128)(2,1)S(1)}, bf16[2,160,128]{2,1,0:T(8,128)(2,1)S(1)}, u32[]{:S(2)}, u32[]{:S(2)}) collective-permute-start(bf16[2,160,128]{2,1,0:T(8,128)(2,1)S(1)} %slice.60), channel_id=1, source_target_pairs={{0,8},{4,12},{8,0},{12,4},{16,24},{20,28},{24,16},{28,20},{1,9},{5... | collective-permute-start | bytes 245768 | tf_op jit(solution)/shard_map/ppermute | solution.py:343
  26.1 8.7 %collective-permute-start.10 = (bf16[4,128,256]{2,1,0:T(8,128)(2,1)S(1)}, bf16[4,128,256]{2,1,0:T(8,128)(2,1)S(1)}, u32[]{:S(2)}, u32[]{:S(2)}) collective-permute-start(bf16[4,128,256]{2,1,0:T(8,128)(2,1)S(1)} %pad_maximum_fusion.1), channel_id=1, source_target_pairs={{0,2},{1,3},{2,0},{3,1},{4,6},{5,7},{6,4},{7,5},{8,10},{9,11},{10,... | collective-permute-start | bytes 786440 | tf_op jit(solution)/shard_map/ppermute | solution.py:343
  27.7 12.4 %copy-start = (f32[1,1024,256]{2,1,0:T(8,128)S(1)}, f32[1,1024,256]{2,1,0:T(8,128)}, u32[]{:S(2)}) copy-start(f32[1,1024,256]{2,1,0:T(8,128)} %param.14) | copy-start | bytes 3145732
  27.7 5.0 %collective-permute-start.11 = (bf16[1,160,128]{2,1,0:T(8,128)(2,1)S(1)}, bf16[1,160,128]{2,1,0:T(8,128)(2,1)S(1)}, u32[]{:S(2)}, u32[]{:S(2)}) collective-permute-start(bf16[1,160,128]{2,1,0:T(8,128)(2,1)S(1)} %slice.79), channel_id=1, source_target_pairs={{0,16},{4,20},{8,24},{12,28},{16,0},{20,4},{24,8},{28,12},{1,17},{... | collective-permute-start | bytes 122888 | tf_op jit(solution)/shard_map/ppermute | solution.py:343
  34.8 5.2 %collective-permute-start.12 = (bf16[8,128,256]{2,1,0:T(8,128)(2,1)S(1)}, bf16[8,128,256]{2,1,0:T(8,128)(2,1)S(1)}, u32[]{:S(2)}, u32[]{:S(2)}) collective-permute-start(bf16[8,128,256]{2,1,0:T(8,128)(2,1)S(1)} %constant_dynamic-update-slice_fusion.4.refs_4_), channel_id=1, source_target_pairs={{0,1},{1,0},{2,3},{3,2},{4,5},{5,4},{6,7},{7,6},{8,9},{9,8},{10,11... | collective-permute-start | bytes 1572872 | tf_op jit(solution)/shard_map/ppermute | solution.py:343
  34.9 5.2 %collective-permute-start.9 = (bf16[8,128,256]{2,1,0:T(8,128)(2,1)S(1)}, bf16[8,128,256]{2,1,0:T(8,128)(2,1)S(1)}, u32[]{:S(2)}, u32[]{:S(2)}) collective-permute-start(bf16[8,128,256]{2,1,0:T(8,128)(2,1)S(1)} %constant_dynamic-update-slice_fusion.refs_2_), channel_id=1, source_target_pairs={{0,1},{1,0},{2,3},{3,2},{4,5},{5,4},{6,7},{7,6},{8,9},{9,8},{10,11... | collective-permute-start | bytes 1572872 | tf_op jit(solution)/shard_map/ppermute | solution.py:343
  35.5 4.5 %collective-permute-start.13 = (f32[160,128]{1,0:T(8,128)S(1)}, f32[160,128]{1,0:T(8,128)S(1)}, u32[]{:S(2)}, u32[]{:S(2)}) collective-permute-start(f32[160,128]{1,0:T(8,128)S(1)} %fusion.2), channel_id=1, source_target_pairs={{0,2},{1,3},{2,0},{3,1},{4,6},{5,7},{6,4},{7,5},{8,10},{9,11},{10,... | collective-permute-start | bytes 245768 | tf_op jit(solution)/shard_map/ppermute | solution.py:343
  37.0 3.1 %copy-start.1 = (s32[1,4096,2]{1,2,0:T(2,128)S(1)}, s32[1,4096,2]{1,2,0:T(2,128)}, u32[]{:S(2)}) copy-start(s32[1,4096,2]{1,2,0:T(2,128)} %param.13) | copy-start | bytes 98308
  37.1 3.1 %copy-start.2 = (f32[1,1024]{1,0:T(1,128)S(1)}, f32[1,1024]{1,0:T(1,128)}, u32[]{:S(2)}) copy-start(f32[1,1024]{1,0:T(1,128)} %refs_1_.1) | copy-start | bytes 12292
  40.0 5.1 %collective-permute-start.14 = (f32[160,128]{1,0:T(8,128)S(1)}, f32[160,128]{1,0:T(8,128)S(1)}, u32[]{:S(2)}, u32[]{:S(2)}) collective-permute-start(f32[160,128]{1,0:T(8,128)S(1)} %add.24), channel_id=1, source_target_pairs={{0,1},{1,0},{2,3},{3,2},{4,5},{5,4},{6,7},{7,6},{8,9},{9,8},{10,11... | collective-permute-start | bytes 245768 | tf_op jit(solution)/shard_map/ppermute | solution.py:343

commit v3 on v2

--- a/solution.py
+++ b/solution.py
@@ -19,7 +19,7 @@
 
 
 def local_kernel(place, dense_in, pooled_in, w_in, bias_in, d_hidden_in, *refs):
-    dense, pooled, w_t, bias, d_hidden, pooled32, feat_t, zrows, z_t, dp_t, wg, sems = refs[-12:]
+    dense, pooled, w_t, bias, d_hidden, pooled32, feat_t, zrows, z_t, dp_t, sems = refs[-11:]
     hold, give, keep, send = refs[:4]
     moves = [
         pltpu.make_async_copy(source, target, sems.at[i])
@@ -94,7 +94,7 @@
                 dp_t[t, at, :] = total
         return carry
 
-    lax.fori_loop(0, width // 16, gradients, 0)
+    lax.fori_loop(0, width // 16, gradients, 0, unroll=2)
     ident_s = eye(samples)
     for i in range(tables // 2):
         for target, side in ((give, 1 - core), (hold, core)):
@@ -102,12 +102,11 @@
             got = lax.dot_general(ident_s, held, NT, preferred_element_type=jnp.float32)
             target[i] = got.astype(jnp.bfloat16)
     half, block = keep.shape[1:]
-    for h in range(2):
-        part = jnp.dot(z_t[h * half : (h + 1) * half, :], dpre, preferred_element_type=jnp.float32)
+    for target, side in ((send, 1 - core), (keep, core)):
+        mine = z_t[pl.ds(pl.multiple_of(side * half, 16), half), :]
+        part = jnp.dot(mine, dpre, preferred_element_type=jnp.float32)
         for b in range(tables):
-            wg[h, jnp.bitwise_xor(wide, b)] = part[:, b * block : (b + 1) * block]
-    keep[...] = wg[core]
-    send[...] = wg[1 - core]
+            target[jnp.bitwise_xor(wide, b)] = part[:, b * block : (b + 1) * block]
 
 
 def local_part(place, dense, pooled, w_t, bias, d_hidden):
@@ -136,44 +135,22 @@
             pltpu.VMEM((128, samples), jnp.float32),
             pltpu.VMEM((padded, samples), jnp.bfloat16),
             pltpu.VMEM((tables, width, samples), jnp.float32),
-            pltpu.VMEM((2, tables, half, hidden // tables), jnp.float32),
             pltpu.SemaphoreType.DMA((5,)),
         ],
         compiler_params=pltpu.CompilerParams(vmem_limit_bytes=14 * 2**20),
     )(place, *[pltpu.with_memory_space_constraint(x, pltpu.HBM) for x in operands])
 
 
-def row_kernel(groups, first, last, joined, n_narrow, rows, place, ids, *refs):
-    refs = list(refs)
-    table_in, accum = (refs.pop(0), refs.pop(0)) if last else (None, None)
-    before_in = None if first else refs.pop(0)
-    grads = [refs.pop(0) for _ in groups]
-    out_sems, sems, done = refs.pop(), refs.pop(), refs.pop()
-    loads = []
-
-    def load(source, target):
-        move = pltpu.make_async_copy(source, target, sems.at[len(loads)])
-        move.start()
-        loads.append(move)
-
-    if not first:
-        before = refs.pop()
-        load(before_in, before)
-    if last:
-        spread, table = refs.pop(), refs.pop()
-        load(table_in, table)
-        new_table, new_accum = refs.pop(0), refs.pop(0)
-    else:
-        sums = refs.pop(0)
-        if joined:
-            whole, start = refs.pop(0), 0
-            for i in joined:
-                whole[start : start + grads[i].shape[0]] = grads[i][...]
-                start += grads[i].shape[0]
-    kept = refs
+def row_kernel(groups, n_narrow, place, ids, table_in, accum, *refs):
+    count = len(groups)
+    grads, (new_table, new_accum), kept = refs[:count], refs[count : count + 2], refs[count + 2 : 2 * count + 2]
+    table, fresh_out, done, spread, sems = refs[2 * count + 2 :]
+    arrive = pltpu.make_async_copy(table_in, table, sems.at[0])
+    arrive.start()
     wide, core, narrow = place[0], place[1], place[2]
     samples, width = grads[0].shape[1:]
-    step, tile, lane = 16, min(512, rows), 128
+    rows = table.shape[0]
+    step, tile, lane = 16, min(256, rows), 128
     down = lax.broadcasted_iota(jnp.int32, (step, samples), 0)
     for pieces, keep in zip(groups, kept):
         for i, (j, k, flip) in enumerate(pieces):
@@ -184,11 +161,8 @@
                     jnp.broadcast_to(local[s : s + 1, :], (step, samples)) - down
                 ).astype(jnp.int16)
     one, none = jnp.bfloat16(1), jnp.bfloat16(0)
-
     leave = []
-    for m in range(rows // tile):
-        base = m * tile
-        at = slice(base, base + tile)
+    for base in range(0, rows, tile):
         total = None
         for grad, keep in zip(grads, kept):
             a, b = keep[0], keep[1]
@@ -199,75 +173,58 @@
             hot = jnp.concatenate(parts, axis=0)
             term = jnp.dot(hot, grad[...].reshape(-1, width), preferred_element_type=jnp.float32)
             total = term if total is None else total + term
-        if not first:
-            if m == 0:
-                loads[0].wait()
-            total = total + before[at, :]
+        at = slice(base, base + tile)
         done[at, :] = total
-        if last:
-            mean = jnp.sum(total * total, axis=1, keepdims=True) * (1.0 / width)
-            spread[at, :] = jnp.broadcast_to(mean, (tile, lane))
-        else:
-            out = pltpu.make_async_copy(done.at[at, :], sums.at[at, :], out_sems.at[m])
-            out.start()
-            leave.append(out)
-    if not last:
-        for out in leave:
-            out.wait()
-        return
-    parts = [slice(i * lane, (i + 1) * lane) for i in range(rows // lane)]
-    mean = jnp.concatenate([spread[part, :].T[:1, :] for part in parts], axis=1)
-    fresh = accum[...] + mean
-    new_accum[...] = fresh
-    rate = 0.1 / (jnp.sqrt(fresh) + 1e-8)
-    loads[-1].wait()
-    for i, part in enumerate(parts):
-        by_row = jnp.broadcast_to(rate[:, part], (lane, lane)).T
+        mean = jnp.sum(total * total, axis=1, keepdims=True) * (1.0 / width)
+        spread[at, :] = jnp.broadcast_to(mean, (tile, lane))
+    cuts = [slice(start, start + lane) for start in range(0, rows, lane)]
+    fresh_out[...] = accum[...] + jnp.concatenate([spread[cut, :].T[:1, :] for cut in cuts], axis=1)
+
+    def depart(source, target):
+        move = pltpu.make_async_copy(source, target, sems.at[1 + len(leave)])
+        move.start()
+        leave.append(move)
+
+    depart(fresh_out, new_accum)
+    rate = 0.1 / (jnp.sqrt(fresh_out[...]) + 1e-8)
+    arrive.wait()
+    for cut in cuts:
+        by_row = jnp.broadcast_to(rate[:, cut], (lane, lane)).T
         for h in range(width // lane):
             cols = slice(h * lane, (h + 1) * lane)
-            table[part, cols] = table[part, cols] - done[part, cols] * by_row
-        out = pltpu.make_async_copy(table.at[part, :], new_table.at[part, :], out_sems.at[i])
-        out.start()
-        leave.append(out)
-    for out in leave:
-        out.wait()
-
-
-def row_part(groups, place, ids, grads, rows, n_narrow, before=None, table=None, accum=None, joined=()):
-    samples, width = grads[0].shape[1:]
-    first, last = before is None, table is not None
+            table[cut, cols] = table[cut, cols] - done[cut, cols] * by_row
+        depart(table.at[cut, :], new_table.at[cut, :])
+    for move in leave:
+        move.wait()
+
+
+def row_part(groups, place, ids, grads, n_narrow, table, accum):
+    rows, width = table.shape
+    samples = grads[0].shape[1]
     vmem, hbm = pl.BlockSpec(memory_space=pltpu.VMEM), pl.BlockSpec(memory_space=pltpu.HBM)
-    operands = ([table, accum] if last else []) + ([] if first else [before]) + list(grads)
-    sums = jax.ShapeDtypeStruct((rows, width), jnp.float32)
-    if last:
-        out_shape = (sums, jax.ShapeDtypeStruct((1, rows), jnp.float32))
-    elif joined:
-        out_shape = (sums, jax.ShapeDtypeStruct((sum(len(groups[i]) for i in joined), samples, width), grads[0].dtype))
-    else:
-        out_shape = (sums,)
-    scratch = [pltpu.VMEM((2, 16, len(pieces) * samples), jnp.int16) for pieces in groups]
-    whole = pltpu.VMEM((rows, width), jnp.float32)
-    if last:
-        scratch += [whole, pltpu.VMEM((rows, 128), jnp.float32)]
-    if not first:
-        scratch += [whole]
-    scratch += [whole, pltpu.SemaphoreType.DMA((2,)), pltpu.SemaphoreType.DMA((rows // 128,))]
     return pl.pallas_call(
-        functools.partial(row_kernel, groups, first, last, joined, n_narrow, rows),
-        out_shape=out_shape,
-        in_specs=[pl.BlockSpec(memory_space=pltpu.SMEM), vmem]
-        + ([hbm, vmem] if last else [])
-        + ([] if first else [hbm])
-        + [vmem] * len(grads),
-        out_specs=(hbm, vmem)[: len(out_shape)],
-        scratch_shapes=scratch,
+        functools.partial(row_kernel, groups, n_narrow),
+        out_shape=(
+            jax.ShapeDtypeStruct((rows, width), jnp.float32),
+            jax.ShapeDtypeStruct((1, rows), jnp.float32),
+        ),
+        in_specs=[pl.BlockSpec(memory_space=pltpu.SMEM), vmem, hbm, vmem] + [vmem] * len(grads),
+        out_specs=(hbm, hbm),
+        scratch_shapes=[pltpu.VMEM((2, 16, len(pieces) * samples), jnp.int16) for pieces in groups]
+        + [
+            pltpu.VMEM((rows, width), jnp.float32),
+            pltpu.VMEM((1, rows), jnp.float32),
+            pltpu.VMEM((rows, width), jnp.float32),
+            pltpu.VMEM((rows, 128), jnp.float32),
+            pltpu.SemaphoreType.DMA((2 + rows // 128,)),
+        ],
         compiler_params=pltpu.CompilerParams(vmem_limit_bytes=14 * 2**20),
         cost_estimate=pl.CostEstimate(
             flops=2 * rows * samples * width * sum(len(pieces) for pieces in groups),
             bytes_accessed=8 * rows * width,
             transcendentals=0,
         ),
-    )(place, ids, *operands)
+    )(place, ids, table, accum, *grads)
 
 
 def row_sums(grads, ids, offset, count):
@@ -362,30 +319,25 @@
     half_y = swap(half[1::2].astype(jnp.bfloat16), "wide", 1)
     near = jnp.concatenate([got[0], got[1]])
     across_near = swap(near, "narrow", 2)
-    half = half[0::2] + half_y.astype(jnp.float32)
-    half_z = swap(half[1::2].astype(jnp.bfloat16), "wide", 2)
-    got[2], got[3], half_z, across_near = tie(got[2], got[3], half_z, across_near)
+    got[2], got[3], across_near = tie(got[2], got[3], across_near)
     far = jnp.concatenate([got[2], got[3]])
     across_far = swap(far, "narrow", 2)
-    half = half[0::2] + half_z.astype(jnp.float32)
-    half_zz = swap(half[1::2].astype(jnp.bfloat16), "wide", 4)
+    half = half[0::2] + half_y.astype(jnp.float32)
+    columns = [swap(half[i].astype(jnp.bfloat16), "wide", 2 * i) for i in range(1, n_wide // 2)]
     mine = jnp.concatenate([near, far])
     beside = swap(mine, "narrow", 1)
-    across_far, half_zz = tie(across_far, half_zz)
+    across_far, *columns = tie(across_far, *columns)
     across = jnp.concatenate([across_near, across_far])
     opposite = swap(across, "narrow", 1)
-    half = half[0::2] + half_zz.astype(jnp.float32)
-    part = half[0] / math.sqrt(total)
-    part_x = swap(part, "narrow", 2)
-    opposite, part_x = tie(opposite, part_x)
-    part = part + part_x
-    other = swap(part, "narrow", 1)
+    part = sum([column.astype(jnp.float32) for column in columns], half[0]) / math.sqrt(total)
+    others = [swap(part, "narrow", bit) for bit in (1, 2, 3)]
     pieces = lambda j, flip: tuple((j ^ s, i, flip) for i in range(n_wide // 2) for s in range(2))
     new_table, new_accum = row_part(
         [pieces(0, 0), pieces(1, 1), pieces(2, 0), pieces(3, 1)],
-        place, ids, [mine, beside, across, opposite], rows, n_narrow, table=tables[0], accum=accum,
-    )
-    other, new_accum = tie(other, new_accum)
+        place, ids, [mine, beside, across, opposite], n_narrow, tables[0], accum,
+    )
+    others[0], others[1], others[2], new_accum = tie(*others, new_accum)
+    part, other = part + others[1], others[0] + others[2]
     low = jnp.where(core == 0, part, other)
     high = jnp.where(core == 0, other, part)
     w_grad = jnp.concatenate([low, high], axis=0)[:inputs].T

time: 46.1 us -> 42.6 us (0.924)
  waiting for transfers between devices: 14.3 us -> 4.83 us
  starting transfers between devices: 19.8 us -> 25.9 us
  Pallas kernels: 9.57 us -> 8.7 us
  other arithmetic: 1.06 us -> 1.85 us
    ppermute x11 -> x13, waiting for transfers between devices: 14.1 us -> 4.65 us  [swap(): return lax.ppermute(array, axis, [(i, i ^ bit) for i in range(n)])]
    ppermute x11 -> x13, starting transfers between devices: 13.4 us -> 19.5 us  [swap(): return lax.ppermute(array, axis, [(i, i ^ bit) for i in range(n)])]
    div x1, other arithmetic: 0.01 us -> 0.83 us  [body(): sum([column.astype(jnp.float32) for column in columns], half[0])]
    pallas_call x1, Pallas kernels: 4.97 us -> 4.29 us  [row_part(): pl.pallas_call(functools.partial(row_kernel, groups, n_narrow), out_shape...]
  transfers between devices with their start and end apart: 15 -> 17, of which waited for: 7 -> 5; matrix products, arithmetic and copies ran while one was open for 1% -> 3% of each run, Pallas kernels for 11% -> 10%
where the time goes in v3:
time: 42.6 us; the launch traced here: 42.3 us
  starting transfers between devices  25.9 us (61%)
  Pallas kernels  8.7 us (20%)
  waiting for transfers between devices  4.83 us (11%)
  other arithmetic  1.85 us (4%)
  between operations  0.87 us (2%)
    ppermute x13, starting transfers between devices, swap(): return lax.ppermute(array, axis, [(i, i ^ bit) for i in range(n)])  19.5 us
    ppermute x4, starting transfers between devices, reach(): return lax.ppermute(lead, ('wide', 'narrow'), pairs)  6.4 us
    ppermute x13, waiting for transfers between devices, swap(): return lax.ppermute(array, axis, [(i, i ^ bit) for i in range(n)])  4.65 us
    pallas_call x1, Pallas kernels, local_part(): pl.pallas_call(local_kernel, out_shape=[jax.ShapeDtypeStruct(shape, jnp.b...  4.41 us
    pallas_call x1, Pallas kernels, row_part(): pl.pallas_call(functools.partial(row_kernel, groups, n_narrow), out_shape...  4.29 us
  transfers between devices with their start and end apart: 17, of which 5 were waited for; matrix products, arithmetic and copies ran while one was open for 3% of the time, Pallas kernels for 10%

profile of v3, /device:TPU:0, one launch (start us, length us, event | category | flops | bytes accessed | tf_op | source)
XLA Modules:
  0.0 42.3 jit_solution(8395817425478445953)
XLA Ops:
  0.6 0.1 pad_add_fusion.place
  0.7 4.4 %shard_map.103 = (bf16[4,128,256]{2,1,0:T(8,128)(2,1)S(1)}, bf16[4,128,256]{2,1,0:T(8,128)(2,1)S(1)}, f32[8,160,128]{2,1,0:T(8,128)S(1)}, f32[8,160,128]{2,1,0:T(8,128)S(1)}) custom-call(s32[3]{0:T(128)S(1)} %pad_add_fusion.place, bf16[128,256]{1,0:T(8,128)(2,1)} %dense_in.1, bf16[1024,256]{1,0:T(8,128)(2,1)} %bitcast.32, bf16[292,1024]{1,0:T(8,128)(2,1)} %bitcast.31, ...), custom_call_target="tpu_custom_call" | custom-call | tf_op jit(solution)/shard_map/pallas_call | solution.py:121
  5.1 0.5 %collective-permute-start = (bf16[4,128,256]{2,1,0:T(8,128)(2,1)S(1)}, bf16[4,128,256]{2,1,0:T(8,128)(2,1)S(1)}, u32[]{:S(2)}, u32[]{:S(2)}) collective-permute-start(bf16[4,128,256]{2,1,0:T(8,128)(2,1)S(1)} %get-tuple-element.24), channel_id=1, source_target_pairs={{0,1},{1,0},{2,3},{3,2},{4,5},{5,4},{6,7},{7,6},{8,9},{9,8},{10,11... | collective-permute-start | bytes 786440 | tf_op jit(solution)/shard_map/ppermute | solution.py:300
  5.7 0.1 collective-permute-start.3
  5.8 1.1 %collective-permute-done = bf16[4,128,256]{2,1,0:T(8,128)(2,1)S(1)} collective-permute-done((bf16[4,128,256]{2,1,0:T(8,128)(2,1)S(1)}, bf16[4,128,256]{2,1,0:T(8,128)(2,1)S(1)}, u32[]{:S(2)}, u32[]{:S(2)}) %collective-permute-start) | collective-permute-done | bytes 262176 | tf_op jit(solution)/shard_map/ppermute | solution.py:300
  6.9 0.7 %collective-permute-start.1 = (bf16[2,128,256]{2,1,0:T(8,128)(2,1)S(1)}, bf16[2,128,256]{2,1,0:T(8,128)(2,1)S(1)}, u32[]{:S(2)}, u32[]{:S(2)}) collective-permute-start(bf16[2,128,256]{2,1,0:T(8,128)(2,1)S(1)} %pad_maximum_fusion.3), channel_id=1, source_target_pairs={{0,0},{1,5},{2,2},{3,7},{4,4},{5,1},{6,6},{7,3},{8,8},{9,13},{10,1... | collective-permute-start | bytes 393224 | tf_op jit(solution)/shard_map/ppermute | solution.py:314
  7.6 3.0 %collective-permute-start.2 = (bf16[2,128,256]{2,1,0:T(8,128)(2,1)S(1)}, bf16[2,128,256]{2,1,0:T(8,128)(2,1)S(1)}, u32[]{:S(2)}, u32[]{:S(2)}) collective-permute-start(bf16[2,128,256]{2,1,0:T(8,128)(2,1)S(1)} %pad_maximum_fusion.4), channel_id=1, source_target_pairs={{0,8},{1,13},{2,10},{3,15},{4,12},{5,9},{6,14},{7,11},{8,0},{9,5},... | collective-permute-start | bytes 393224 | tf_op jit(solution)/shard_map/ppermute | solution.py:314
  10.6 2.7 %collective-permute-start.4 = (bf16[2,128,256]{2,1,0:T(8,128)(2,1)S(1)}, bf16[2,128,256]{2,1,0:T(8,128)(2,1)S(1)}, u32[]{:S(2)}, u32[]{:S(2)}) collective-permute-start(bf16[2,128,256]{2,1,0:T(8,128)(2,1)S(1)} %pad_maximum_fusion.5), channel_id=1, source_target_pairs={{0,16},{1,21},{2,18},{3,23},{4,20},{5,17},{6,22},{7,19},{8,24},{9,... | collective-permute-start | bytes 393224 | tf_op jit(solution)/shard_map/ppermute | solution.py:314
  13.3 0.1 collective-permute-start.5
  13.4 0.2 collective-permute-done.2
  13.5 0.1 fusion.6
  13.7 2.0 %collective-permute-start.9 = (bf16[4,160,128]{2,1,0:T(8,128)(2,1)S(1)}, bf16[4,160,128]{2,1,0:T(8,128)(2,1)S(1)}, u32[]{:S(2)}, u32[]{:S(2)}) collective-permute-start(bf16[4,160,128]{2,1,0:T(8,128)(2,1)S(1)} %slice.58), channel_id=1, source_target_pairs={{0,4},{4,0},{8,12},{12,8},{16,20},{20,16},{24,28},{28,24},{1,5},{5... | collective-permute-start | bytes 491528 | tf_op jit(solution)/shard_map/ppermute | solution.py:300
  15.7 1.6 %collective-permute-start.6 = (bf16[4,128,256]{2,1,0:T(8,128)(2,1)S(1)}, bf16[4,128,256]{2,1,0:T(8,128)(2,1)S(1)}, u32[]{:S(2)}, u32[]{:S(2)}) collective-permute-start(bf16[4,128,256]{2,1,0:T(8,128)(2,1)S(1)} %pad_maximum_fusion), channel_id=1, source_target_pairs={{0,2},{1,3},{2,0},{3,1},{4,6},{5,7},{6,4},{7,5},{8,10},{9,11},{10,... | collective-permute-start | bytes 786440 | tf_op jit(solution)/shard_map/ppermute | solution.py:300
  17.3 2.6 %collective-permute-done.9 = bf16[4,160,128]{2,1,0:T(8,128)(2,1)S(1)} collective-permute-done((bf16[4,160,128]{2,1,0:T(8,128)(2,1)S(1)}, bf16[4,160,128]{2,1,0:T(8,128)(2,1)S(1)}, u32[]{:S(2)}, u32[]{:S(2)}) %collective-permute-start.9) | collective-permute-done | bytes 163872 | tf_op jit(solution)/shard_map/ppermute | solution.py:300
  19.9 3.3 %collective-permute-start.12 = (bf16[160,128]{1,0:T(8,128)(2,1)S(1)}, bf16[160,128]{1,0:T(8,128)(2,1)S(1)}, u32[]{:S(2)}, u32[]{:S(2)}) collective-permute-start(bf16[160,128]{1,0:T(8,128)(2,1)S(1)} %get-tuple-element.57), channel_id=1, source_target_pairs={{0,24},{4,28},{8,16},{12,20},{16,8},{20,12},{24,0},{28,4},{1,25},{... | collective-permute-start | bytes 122888 | tf_op jit(solution)/shard_map/ppermute | solution.py:300
  23.3 1.0 %collective-permute-start.11 = (bf16[160,128]{1,0:T(8,128)(2,1)S(1)}, bf16[160,128]{1,0:T(8,128)(2,1)S(1)}, u32[]{:S(2)}, u32[]{:S(2)}) collective-permute-start(bf16[160,128]{1,0:T(8,128)(2,1)S(1)} %get-tuple-element.58), channel_id=1, source_target_pairs={{0,16},{4,20},{8,24},{12,28},{16,0},{20,4},{24,8},{28,12},{1,17},{... | collective-permute-start | bytes 122888 | tf_op jit(solution)/shard_map/ppermute | solution.py:300
  24.3 0.2 collective-permute-start.10
  24.5 0.0 collective-permute-done.6
  24.5 0.0 copy-start
  24.5 1.7 %collective-permute-start.8 = (bf16[4,128,256]{2,1,0:T(8,128)(2,1)S(1)}, bf16[4,128,256]{2,1,0:T(8,128)(2,1)S(1)}, u32[]{:S(2)}, u32[]{:S(2)}) collective-permute-start(bf16[4,128,256]{2,1,0:T(8,128)(2,1)S(1)} %pad_maximum_fusion.1), channel_id=1, source_target_pairs={{0,2},{1,3},{2,0},{3,1},{4,6},{5,7},{6,4},{7,5},{8,10},{9,11},{10,... | collective-permute-start | bytes 786440 | tf_op jit(solution)/shard_map/ppermute | solution.py:300
  26.2 4.0 %collective-permute-start.7 = (bf16[8,128,256]{2,1,0:T(8,128)(2,1)S(1)}, bf16[8,128,256]{2,1,0:T(8,128)(2,1)S(1)}, u32[]{:S(2)}, u32[]{:S(2)}) collective-permute-start(bf16[8,128,256]{2,1,0:T(8,128)(2,1)S(1)} %constant_dynamic-update-slice_fusion.refs_0_), channel_id=1, source_target_pairs={{0,1},{1,0},{2,3},{3,2},{4,5},{5,4},{6,7},{7,6},{8,9},{9,8},{10,11... | collective-permute-start | bytes 1572872 | tf_op jit(solution)/shard_map/ppermute | solution.py:300
  30.2 0.0 collective-permute-done.12
  30.3 0.0 copy-start.4
  30.3 0.7 %collective-permute-done.8 = bf16[4,128,256]{2,1,0:T(8,128)(2,1)S(1)} collective-permute-done((bf16[4,128,256]{2,1,0:T(8,128)(2,1)S(1)}, bf16[4,128,256]{2,1,0:T(8,128)(2,1)S(1)}, u32[]{:S(2)}, u32[]{:S(2)}) %collective-permute-start.8) | collective-permute-done | bytes 262176 | tf_op jit(solution)/shard_map/ppermute | solution.py:300
  31.0 3.2 %collective-permute-start.13 = (bf16[8,128,256]{2,1,0:T(8,128)(2,1)S(1)}, bf16[8,128,256]{2,1,0:T(8,128)(2,1)S(1)}, u32[]{:S(2)}, u32[]{:S(2)}) collective-permute-start(bf16[8,128,256]{2,1,0:T(8,128)(2,1)S(1)} %constant_dynamic-update-slice_fusion.4.refs_2_), channel_id=1, source_target_pairs={{0,1},{1,0},{2,3},{3,2},{4,5},{5,4},{6,7},{7,6},{8,9},{9,8},{10,11... | collective-permute-start | bytes 1572872 | tf_op jit(solution)/shard_map/ppermute | solution.py:300
  34.2 0.8 %fusion.4 = f32[160,128]{1,0:T(8,128)S(1)} fusion(f32[4,160,128]{2,1,0:T(8,128)S(1)} %get-tuple-element.44, bf16[160,128]{1,0:T(8,128)(2,1)S(1)} %collective-permute-done.12, bf16[160,128]{1,0:T(8,128)(2,1)} %copy-done.3, bf16[160,128]{1,0:T(8,128)(2,1)} %copy-done.4), kind=kLoop, calls=%fused_computation.13 | loop fusion | flops 143360 | bytes 286720 | tf_op jit(solution)/shard_map/div | solution.py:332
  35.1 1.2 %collective-permute-start.16 = (f32[160,128]{1,0:T(8,128)S(1)}, f32[160,128]{1,0:T(8,128)S(1)}, u32[]{:S(2)}, u32[]{:S(2)}) collective-permute-start(f32[160,128]{1,0:T(8,128)S(1)} %fusion.4), channel_id=1, source_target_pairs={{0,3},{1,2},{2,1},{3,0},{4,7},{5,6},{6,5},{7,4},{8,11},{9,10},{10,... | collective-permute-start | bytes 245768 | tf_op jit(solution)/shard_map/ppermute | solution.py:300
  36.3 0.5 %collective-permute-start.15 = (f32[160,128]{1,0:T(8,128)S(1)}, f32[160,128]{1,0:T(8,128)S(1)}, u32[]{:S(2)}, u32[]{:S(2)}) collective-permute-start(f32[160,128]{1,0:T(8,128)S(1)} %fusion.4), channel_id=1, source_target_pairs={{0,2},{1,3},{2,0},{3,1},{4,6},{5,7},{6,4},{7,5},{8,10},{9,11},{10,... | collective-permute-start | bytes 245768 | tf_op jit(solution)/shard_map/ppermute | solution.py:300
  36.8 0.2 collective-permute-start.14
  37.0 4.3 %shard_map.104 = (f32[1024,256]{1,0:T(8,128)}, f32[1,1024]{1,0:T(1,128)}) custom-call(s32[3]{0:T(128)S(1)} %pad_add_fusion.place, s32[2,4096]{1,0:T(2,128)S(1)} %bitcast.30, f32[1024,256]{1,0:T(8,128)S(1)} %bitcast.29, f32[1,1024]{1,0:T(1,128)S(1)} %copy-done.2, bf16[8,128,256]{2,1,0:T(8,128)(2,1)S(1)} %constant_dynamic-update-slice_fusion.refs_0_, ...), custom_call_target="tpu_custom_call" | custom-call | flops 2147483648 | bytes 2097152 | tf_op jit(solution)/shard_map/pallas_call | solution.py:205
  41.3 0.3 collective-permute-done.15
  41.7 0.7 %fusion = f32[128,292]{0,1:T(8,128)} fusion(f32[160,128]{1,0:T(8,128)S(1)} %get-tuple-element.48, f32[160,128]{1,0:T(8,128)S(1)} %get-tuple-element.47), kind=kLoop, calls=%fused_computation.4 | loop fusion | flops 37376 | bytes 313344 | tf_op jit(solution)/shard_map/transpose | solution.py:343
  (36 shorter events, 0.4 us)
Async XLA Ops:
  5.1 1.7 %collective-permute-start = (bf16[4,128,256]{2,1,0:T(8,128)(2,1)S(1)}, bf16[4,128,256]{2,1,0:T(8,128)(2,1)S(1)}, u32[]{:S(2)}, u32[]{:S(2)}) collective-permute-start(bf16[4,128,256]{2,1,0:T(8,128)(2,1)S(1)} %get-tuple-element.24), channel_id=1, source_target_pairs={{0,1},{1,0},{2,3},{3,2},{4,5},{5,4},{6,7},{7,6},{8,9},{9,8},{10,11... | collective-permute-start | bytes 786440 | tf_op jit(solution)/shard_map/ppermute | solution.py:300
  5.7 7.9 %collective-permute-start.3 = (f32[8,160,128]{2,1,0:T(8,128)S(1)}, f32[8,160,128]{2,1,0:T(8,128)S(1)}, u32[]{:S(2)}, u32[]{:S(2)}) collective-permute-start(f32[8,160,128]{2,1,0:T(8,128)S(1)} %get-tuple-element.25), channel_id=1, source_target_pairs={{0,1},{1,0},{2,3},{3,2},{4,5},{5,4},{6,7},{7,6},{8,9},{9,8},{10,11... | collective-permute-start | bytes 1966088 | tf_op jit(solution)/shard_map/ppermute | solution.py:300
  6.9 6.5 %collective-permute-start.1 = (bf16[2,128,256]{2,1,0:T(8,128)(2,1)S(1)}, bf16[2,128,256]{2,1,0:T(8,128)(2,1)S(1)}, u32[]{:S(2)}, u32[]{:S(2)}) collective-permute-start(bf16[2,128,256]{2,1,0:T(8,128)(2,1)S(1)} %pad_maximum_fusion.3), channel_id=1, source_target_pairs={{0,0},{1,5},{2,2},{3,7},{4,4},{5,1},{6,6},{7,3},{8,8},{9,13},{10,1... | collective-permute-start | bytes 393224 | tf_op jit(solution)/shard_map/ppermute | solution.py:314
  7.6 6.0 %collective-permute-start.2 = (bf16[2,128,256]{2,1,0:T(8,128)(2,1)S(1)}, bf16[2,128,256]{2,1,0:T(8,128)(2,1)S(1)}, u32[]{:S(2)}, u32[]{:S(2)}) collective-permute-start(bf16[2,128,256]{2,1,0:T(8,128)(2,1)S(1)} %pad_maximum_fusion.4), channel_id=1, source_target_pairs={{0,8},{1,13},{2,10},{3,15},{4,12},{5,9},{6,14},{7,11},{8,0},{9,5},... | collective-permute-start | bytes 393224 | tf_op jit(solution)/shard_map/ppermute | solution.py:314
  10.6 13.7 %collective-permute-start.4 = (bf16[2,128,256]{2,1,0:T(8,128)(2,1)S(1)}, bf16[2,128,256]{2,1,0:T(8,128)(2,1)S(1)}, u32[]{:S(2)}, u32[]{:S(2)}) collective-permute-start(bf16[2,128,256]{2,1,0:T(8,128)(2,1)S(1)} %pad_maximum_fusion.5), channel_id=1, source_target_pairs={{0,16},{1,21},{2,18},{3,23},{4,20},{5,17},{6,22},{7,19},{8,24},{9,... | collective-permute-start | bytes 393224 | tf_op jit(solution)/shard_map/ppermute | solution.py:314
  13.3 11.2 %collective-permute-start.5 = (bf16[2,128,256]{2,1,0:T(8,128)(2,1)S(1)}, bf16[2,128,256]{2,1,0:T(8,128)(2,1)S(1)}, u32[]{:S(2)}, u32[]{:S(2)}) collective-permute-start(bf16[2,128,256]{2,1,0:T(8,128)(2,1)S(1)} %pad_maximum_fusion.6), channel_id=1, source_target_pairs={{0,24},{1,29},{2,26},{3,31},{4,28},{5,25},{6,30},{7,27},{8,16},{9,... | collective-permute-start | bytes 393224 | tf_op jit(solution)/shard_map/ppermute | solution.py:314
  13.7 6.2 %collective-permute-start.9 = (bf16[4,160,128]{2,1,0:T(8,128)(2,1)S(1)}, bf16[4,160,128]{2,1,0:T(8,128)(2,1)S(1)}, u32[]{:S(2)}, u32[]{:S(2)}) collective-permute-start(bf16[4,160,128]{2,1,0:T(8,128)(2,1)S(1)} %slice.58), channel_id=1, source_target_pairs={{0,4},{4,0},{8,12},{12,8},{16,20},{20,16},{24,28},{28,24},{1,5},{5... | collective-permute-start | bytes 491528 | tf_op jit(solution)/shard_map/ppermute | solution.py:300
  15.7 8.8 %collective-permute-start.6 = (bf16[4,128,256]{2,1,0:T(8,128)(2,1)S(1)}, bf16[4,128,256]{2,1,0:T(8,128)(2,1)S(1)}, u32[]{:S(2)}, u32[]{:S(2)}) collective-permute-start(bf16[4,128,256]{2,1,0:T(8,128)(2,1)S(1)} %pad_maximum_fusion), channel_id=1, source_target_pairs={{0,2},{1,3},{2,0},{3,1},{4,6},{5,7},{6,4},{7,5},{8,10},{9,11},{10,... | collective-permute-start | bytes 786440 | tf_op jit(solution)/shard_map/ppermute | solution.py:300
  19.9 10.3 %collective-permute-start.12 = (bf16[160,128]{1,0:T(8,128)(2,1)S(1)}, bf16[160,128]{1,0:T(8,128)(2,1)S(1)}, u32[]{:S(2)}, u32[]{:S(2)}) collective-permute-start(bf16[160,128]{1,0:T(8,128)(2,1)S(1)} %get-tuple-element.57), channel_id=1, source_target_pairs={{0,24},{4,28},{8,16},{12,20},{16,8},{20,12},{24,0},{28,4},{1,25},{... | collective-permute-start | bytes 122888 | tf_op jit(solution)/shard_map/ppermute | solution.py:300
  23.3 7.0 %collective-permute-start.11 = (bf16[160,128]{1,0:T(8,128)(2,1)S(1)}, bf16[160,128]{1,0:T(8,128)(2,1)S(1)}, u32[]{:S(2)}, u32[]{:S(2)}) collective-permute-start(bf16[160,128]{1,0:T(8,128)(2,1)S(1)} %get-tuple-element.58), channel_id=1, source_target_pairs={{0,16},{4,20},{8,24},{12,28},{16,0},{20,4},{24,8},{28,12},{1,17},{... | collective-permute-start | bytes 122888 | tf_op jit(solution)/shard_map/ppermute | solution.py:300
  24.3 6.0 %collective-permute-start.10 = (bf16[160,128]{1,0:T(8,128)(2,1)S(1)}, bf16[160,128]{1,0:T(8,128)(2,1)S(1)}, u32[]{:S(2)}, u32[]{:S(2)}) collective-permute-start(bf16[160,128]{1,0:T(8,128)(2,1)S(1)} %get-tuple-element.59), channel_id=1, source_target_pairs={{0,8},{4,12},{8,0},{12,4},{16,24},{20,28},{24,16},{28,20},{1,9},{5... | collective-permute-start | bytes 122888 | tf_op jit(solution)/shard_map/ppermute | solution.py:300
  24.5 12.5 %copy-start = (f32[1,1024,256]{2,1,0:T(8,128)S(1)}, f32[1,1024,256]{2,1,0:T(8,128)}, u32[]{:S(2)}) copy-start(f32[1,1024,256]{2,1,0:T(8,128)} %param.14) | copy-start | bytes 3145732
  24.5 6.4 %collective-permute-start.8 = (bf16[4,128,256]{2,1,0:T(8,128)(2,1)S(1)}, bf16[4,128,256]{2,1,0:T(8,128)(2,1)S(1)}, u32[]{:S(2)}, u32[]{:S(2)}) collective-permute-start(bf16[4,128,256]{2,1,0:T(8,128)(2,1)S(1)} %pad_maximum_fusion.1), channel_id=1, source_target_pairs={{0,2},{1,3},{2,0},{3,1},{4,6},{5,7},{6,4},{7,5},{8,10},{9,11},{10,... | collective-permute-start | bytes 786440 | tf_op jit(solution)/shard_map/ppermute | solution.py:300
  26.2 10.8 %collective-permute-start.7 = (bf16[8,128,256]{2,1,0:T(8,128)(2,1)S(1)}, bf16[8,128,256]{2,1,0:T(8,128)(2,1)S(1)}, u32[]{:S(2)}, u32[]{:S(2)}) collective-permute-start(bf16[8,128,256]{2,1,0:T(8,128)(2,1)S(1)} %constant_dynamic-update-slice_fusion.refs_0_), channel_id=1, source_target_pairs={{0,1},{1,0},{2,3},{3,2},{4,5},{5,4},{6,7},{7,6},{8,9},{9,8},{10,11... | collective-permute-start | bytes 1572872 | tf_op jit(solution)/shard_map/ppermute | solution.py:300
  30.2 0.7 %copy-start.3 = (bf16[160,128]{1,0:T(8,128)(2,1)}, bf16[160,128]{1,0:T(8,128)(2,1)S(1)}, u32[]{:S(2)}) copy-start(bf16[160,128]{1,0:T(8,128)(2,1)S(1)} %collective-permute-done.11) | copy-start | bytes 122884
  30.3 0.7 %copy-start.4 = (bf16[160,128]{1,0:T(8,128)(2,1)}, bf16[160,128]{1,0:T(8,128)(2,1)S(1)}, u32[]{:S(2)}) copy-start(bf16[160,128]{1,0:T(8,128)(2,1)S(1)} %collective-permute-done.10) | copy-start | bytes 122884
  31.0 6.0 %collective-permute-start.13 = (bf16[8,128,256]{2,1,0:T(8,128)(2,1)S(1)}, bf16[8,128,256]{2,1,0:T(8,128)(2,1)S(1)}, u32[]{:S(2)}, u32[]{:S(2)}) collective-permute-start(bf16[8,128,256]{2,1,0:T(8,128)(2,1)S(1)} %constant_dynamic-update-slice_fusion.4.refs_2_), channel_id=1, source_target_pairs={{0,1},{1,0},{2,3},{3,2},{4,5},{5,4},{6,7},{7,6},{8,9},{9,8},{10,11... | collective-permute-start | bytes 1572872 | tf_op jit(solution)/shard_map/ppermute | solution.py:300
  34.2 2.8 %copy-start.1 = (s32[1,4096,2]{1,2,0:T(2,128)S(1)}, s32[1,4096,2]{1,2,0:T(2,128)}, u32[]{:S(2)}) copy-start(s32[1,4096,2]{1,2,0:T(2,128)} %param.13) | copy-start | bytes 98308
  34.2 2.8 %copy-start.2 = (f32[1,1024]{1,0:T(1,128)S(1)}, f32[1,1024]{1,0:T(1,128)}, u32[]{:S(2)}) copy-start(f32[1,1024]{1,0:T(1,128)} %accum.1) | copy-start | bytes 12292
  35.1 6.3 %collective-permute-start.16 = (f32[160,128]{1,0:T(8,128)S(1)}, f32[160,128]{1,0:T(8,128)S(1)}, u32[]{:S(2)}, u32[]{:S(2)}) collective-permute-start(f32[160,128]{1,0:T(8,128)S(1)} %fusion.4), channel_id=1, source_target_pairs={{0,3},{1,2},{2,1},{3,0},{4,7},{5,6},{6,5},{7,4},{8,11},{9,10},{10,... | collective-permute-start | bytes 245768 | tf_op jit(solution)/shard_map/ppermute | solution.py:300
  36.3 5.4 %collective-permute-start.15 = (f32[160,128]{1,0:T(8,128)S(1)}, f32[160,128]{1,0:T(8,128)S(1)}, u32[]{:S(2)}, u32[]{:S(2)}) collective-permute-start(f32[160,128]{1,0:T(8,128)S(1)} %fusion.4), channel_id=1, source_target_pairs={{0,2},{1,3},{2,0},{3,1},{4,6},{5,7},{6,4},{7,5},{8,10},{9,11},{10,... | collective-permute-start | bytes 245768 | tf_op jit(solution)/shard_map/ppermute | solution.py:300
  36.8 4.8 %collective-permute-start.14 = (f32[160,128]{1,0:T(8,128)S(1)}, f32[160,128]{1,0:T(8,128)S(1)}, u32[]{:S(2)}, u32[]{:S(2)}) collective-permute-start(f32[160,128]{1,0:T(8,128)S(1)} %fusion.4), channel_id=1, source_target_pairs={{0,1},{1,0},{2,3},{3,2},{4,5},{5,4},{6,7},{7,6},{8,9},{9,8},{10,11... | collective-permute-start | bytes 245768 | tf_op jit(solution)/shard_map/ppermute | solution.py:300

commit v4 on v3

--- a/solution.py
+++ b/solution.py
@@ -19,7 +19,7 @@
 
 
 def local_kernel(place, dense_in, pooled_in, w_in, bias_in, d_hidden_in, *refs):
-    dense, pooled, w_t, bias, d_hidden, pooled32, feat_t, zrows, z_t, dp_t, sems = refs[-11:]
+    dense, pooled, w_t, bias, d_hidden, pooled32, feat_t, zrows, z_t, dp_t, dpre_all, sems = refs[-12:]
     hold, give, keep, send = refs[:4]
     moves = [
         pltpu.make_async_copy(source, target, sems.at[i])
@@ -56,7 +56,7 @@
         return tuple(s + f[i] * f[j] for s, i, j in zip(sums, low_i, low_j))
 
     zero = jnp.zeros((8, samples), jnp.float32)
-    sums = lax.fori_loop(0, width // 8, products, (zero,) * pairs, unroll=4)
+    sums = lax.fori_loop(0, width // 8, products, (zero,) * pairs, unroll=True)
     zrows[...] = jnp.zeros_like(zrows)
     for p in range(pairs):
         zrows[p : p + 1, :] = jnp.sum(sums[p], axis=0, keepdims=True)
@@ -94,34 +94,34 @@
                 dp_t[t, at, :] = total
         return carry
 
-    lax.fori_loop(0, width // 16, gradients, 0, unroll=2)
+    lax.fori_loop(0, width // 16, gradients, 0, unroll=True)
     ident_s = eye(samples)
     for i in range(tables // 2):
         for target, side in ((give, 1 - core), (hold, core)):
-            held = dp_t[jnp.bitwise_xor(wide, 2 * i + side)].astype(jnp.bfloat16)
+            held = dp_t[jnp.bitwise_xor(wide, 2 * i + jnp.bitwise_xor(side, i % 2))].astype(jnp.bfloat16)
             got = lax.dot_general(ident_s, held, NT, preferred_element_type=jnp.float32)
             target[i] = got.astype(jnp.bfloat16)
-    half, block = keep.shape[1:]
-    for target, side in ((send, 1 - core), (keep, core)):
-        mine = z_t[pl.ds(pl.multiple_of(side * half, 16), half), :]
-        part = jnp.dot(mine, dpre, preferred_element_type=jnp.float32)
-        for b in range(tables):
-            target[jnp.bitwise_xor(wide, b)] = part[:, b * block : (b + 1) * block]
+    block = keep.shape[2]
+    dpre_all[...] = dpre
+    for i in range(tables // 2):
+        for target, side in ((send, 1 - core), (keep, core)):
+            column = jnp.bitwise_xor(wide, 2 * i + jnp.bitwise_xor(side, i % 2)) * block
+            mine = dpre_all[:, pl.ds(pl.multiple_of(column, block), block)]
+            target[i] = jnp.dot(z_t[...], mine, preferred_element_type=jnp.float32)
 
 
 def local_part(place, dense, pooled, w_t, bias, d_hidden):
     samples, width = dense.shape
     tables = pooled.shape[1]
     hidden = w_t.shape[1]
-    padded = -(-w_t.shape[0] // 32) * 32
-    half = padded // 2
+    padded = -(-w_t.shape[0] // 16) * 16
     vmem, hbm = pl.BlockSpec(memory_space=pltpu.VMEM), pl.BlockSpec(memory_space=pltpu.HBM)
     gradients = [(tables // 2, samples, width)] * 2
     operands = (dense, pooled.reshape(samples * tables, width), w_t, bias.reshape(1, hidden), d_hidden)
     return pl.pallas_call(
         local_kernel,
         out_shape=[jax.ShapeDtypeStruct(shape, jnp.bfloat16) for shape in gradients]
-        + [jax.ShapeDtypeStruct((tables, half, hidden // tables), jnp.float32)] * 2,
+        + [jax.ShapeDtypeStruct((tables // 2, padded, hidden // tables), jnp.float32)] * 2,
         in_specs=[pl.BlockSpec(memory_space=pltpu.SMEM)] + [hbm] * 5,
         out_specs=[vmem] * (len(gradients) + 2),
         scratch_shapes=[
@@ -135,45 +135,68 @@
             pltpu.VMEM((128, samples), jnp.float32),
             pltpu.VMEM((padded, samples), jnp.bfloat16),
             pltpu.VMEM((tables, width, samples), jnp.float32),
+            pltpu.VMEM((samples, hidden), jnp.bfloat16),
             pltpu.SemaphoreType.DMA((5,)),
         ],
         compiler_params=pltpu.CompilerParams(vmem_limit_bytes=14 * 2**20),
     )(place, *[pltpu.with_memory_space_constraint(x, pltpu.HBM) for x in operands])
 
 
-def row_kernel(groups, n_narrow, place, ids, table_in, accum, *refs):
+def bag_rows(groups, n_narrow, place, ids, kept, rows):
+    wide, core, narrow = place[0], place[1], place[2]
+    step = kept[0].shape[1]
+    samples = kept[0].shape[2] // len(groups[0])
+    down = lax.broadcasted_iota(jnp.int32, (step, samples), 0)
+    for pieces, keep in zip(groups, kept):
+        for i, (j, k, flip) in enumerate(pieces):
+            source = jnp.bitwise_xor(wide, 2 * k + jnp.bitwise_xor(core, (flip + k) % 2))
+            at = source * n_narrow + jnp.bitwise_xor(narrow, j)
+            local = ids[:, pl.ds(pl.multiple_of(at * samples, samples), samples)] - narrow * rows
+            for s in range(2):
+                keep[s, :, i * samples : (i + 1) * samples] = (
+                    jnp.broadcast_to(local[s : s + 1, :], (step, samples)) - down
+                ).astype(jnp.int16)
+
+
+def tile_sums(base, tile, grads, kept, width):
+    one, none = jnp.bfloat16(1), jnp.bfloat16(0)
+    step = kept[0].shape[1]
+    total = None
+    for grad, keep in zip(grads, kept):
+        a, b = keep[0], keep[1]
+        parts = []
+        for i in range(tile // step):
+            want = jnp.int16(base + i * step)
+            parts.append(jnp.where(a == want, one, none) + jnp.where(b == want, one, none))
+        hot = jnp.concatenate(parts, axis=0)
+        term = jnp.dot(hot, grad[...].reshape(-1, width), preferred_element_type=jnp.float32)
+        total = term if total is None else total + term
+    return total
+
+
+def early_kernel(groups, n_narrow, place, ids, *refs):
+    count = len(groups)
+    grads, sums, kept = refs[:count], refs[count], refs[count + 1 :]
+    rows, width = sums.shape
+    bag_rows(groups, n_narrow, place, ids, kept, rows)
+    tile = min(256, rows)
+    for base in range(0, rows, tile):
+        sums[base : base + tile, :] = tile_sums(base, tile, grads, kept, width)
+
+
+def row_kernel(groups, n_narrow, place, ids, table_in, accum, before, *refs):
     count = len(groups)
     grads, (new_table, new_accum), kept = refs[:count], refs[count : count + 2], refs[count + 2 : 2 * count + 2]
     table, fresh_out, done, spread, sems = refs[2 * count + 2 :]
     arrive = pltpu.make_async_copy(table_in, table, sems.at[0])
     arrive.start()
-    wide, core, narrow = place[0], place[1], place[2]
-    samples, width = grads[0].shape[1:]
-    rows = table.shape[0]
-    step, tile, lane = 16, min(256, rows), 128
-    down = lax.broadcasted_iota(jnp.int32, (step, samples), 0)
-    for pieces, keep in zip(groups, kept):
-        for i, (j, k, flip) in enumerate(pieces):
-            at = jnp.bitwise_xor(wide, 2 * k + jnp.bitwise_xor(core, flip)) * n_narrow + jnp.bitwise_xor(narrow, j)
-            local = ids[:, pl.ds(pl.multiple_of(at * samples, samples), samples)] - narrow * rows
-            for s in range(2):
-                keep[s, :, i * samples : (i + 1) * samples] = (
-                    jnp.broadcast_to(local[s : s + 1, :], (step, samples)) - down
-                ).astype(jnp.int16)
-    one, none = jnp.bfloat16(1), jnp.bfloat16(0)
+    rows, width = table.shape
+    tile, lane = min(256, rows), 128
+    bag_rows(groups, n_narrow, place, ids, kept, rows)
     leave = []
     for base in range(0, rows, tile):
-        total = None
-        for grad, keep in zip(grads, kept):
-            a, b = keep[0], keep[1]
-            parts = []
-            for i in range(tile // step):
-                want = jnp.int16(base + i * step)
-                parts.append(jnp.where(a == want, one, none) + jnp.where(b == want, one, none))
-            hot = jnp.concatenate(parts, axis=0)
-            term = jnp.dot(hot, grad[...].reshape(-1, width), preferred_element_type=jnp.float32)
-            total = term if total is None else total + term
         at = slice(base, base + tile)
+        total = before[at, :] + tile_sums(base, tile, grads, kept, width)
         done[at, :] = total
         mean = jnp.sum(total * total, axis=1, keepdims=True) * (1.0 / width)
         spread[at, :] = jnp.broadcast_to(mean, (tile, lane))
@@ -198,7 +221,21 @@
         move.wait()
 
 
-def row_part(groups, place, ids, grads, n_narrow, table, accum):
+def early_part(groups, place, ids, grads, n_narrow, rows):
+    samples, width = grads[0].shape[1:]
+    vmem = pl.BlockSpec(memory_space=pltpu.VMEM)
+    return pl.pallas_call(
+        functools.partial(early_kernel, groups, n_narrow),
+        out_shape=jax.ShapeDtypeStruct((rows, width), jnp.float32),
+        in_specs=[pl.BlockSpec(memory_space=pltpu.SMEM), vmem] + [vmem] * len(grads),
+        out_specs=vmem,
+        scratch_shapes=[pltpu.VMEM((2, 16, len(pieces) * samples), jnp.int16) for pieces in groups],
+        compiler_params=pltpu.CompilerParams(vmem_limit_bytes=14 * 2**20),
+        cost_estimate=pl.CostEstimate(flops=0, bytes_accessed=0, transcendentals=0),
+    )(place, ids, *grads)
+
+
+def row_part(groups, place, ids, grads, n_narrow, table, accum, before):
     rows, width = table.shape
     samples = grads[0].shape[1]
     vmem, hbm = pl.BlockSpec(memory_space=pltpu.VMEM), pl.BlockSpec(memory_space=pltpu.HBM)
@@ -208,7 +245,7 @@
             jax.ShapeDtypeStruct((rows, width), jnp.float32),
             jax.ShapeDtypeStruct((1, rows), jnp.float32),
         ),
-        in_specs=[pl.BlockSpec(memory_space=pltpu.SMEM), vmem, hbm, vmem] + [vmem] * len(grads),
+        in_specs=[pl.BlockSpec(memory_space=pltpu.SMEM), vmem, hbm, vmem, vmem] + [vmem] * len(grads),
         out_specs=(hbm, hbm),
         scratch_shapes=[pltpu.VMEM((2, 16, len(pieces) * samples), jnp.int16) for pieces in groups]
         + [
@@ -224,7 +261,7 @@
             bytes_accessed=8 * rows * width,
             transcendentals=0,
         ),
-    )(place, ids, table, accum, *grads)
+    )(place, ids, table, accum, before, *grads)
 
 
 def row_sums(grads, ids, offset, count):
@@ -306,41 +343,37 @@
     taken = swap(give, "narrow", 1)
     received = swap(send, "narrow", 1)
 
-    def reach(i):
-        lead = jnp.stack([hold[i], taken[i]])
+    def reach(block, i):
         pairs = [
-            (w * n_narrow + n, (w ^ (2 * i + n % 2)) * n_narrow + n) for w in range(n_wide) for n in range(n_narrow)
+            (w * n_narrow + n, (w ^ (2 * i + (n + i) % 2)) * n_narrow + n) for w in range(n_wide) for n in range(n_narrow)
         ]
-        return lax.ppermute(lead, ("wide", "narrow"), pairs)
-
-    got = {i: reach(i) for i in (1, 0, 2, 3)}
+        return lax.ppermute(block, ("wide", "narrow"), pairs)
+
+    got = {i: reach(jnp.stack([hold[i], taken[i]]), i) for i in (1, 0, 2, 3)}
     got[0], got[1], received = tie(got[0], got[1], received)
     half = keep + received
-    half_y = swap(half[1::2].astype(jnp.bfloat16), "wide", 1)
+    columns = [reach(half[i].astype(jnp.bfloat16), i) for i in (0, 1, 2, 3)]
     near = jnp.concatenate([got[0], got[1]])
     across_near = swap(near, "narrow", 2)
     got[2], got[3], across_near = tie(got[2], got[3], across_near)
-    far = jnp.concatenate([got[2], got[3]])
-    across_far = swap(far, "narrow", 2)
-    half = half[0::2] + half_y.astype(jnp.float32)
-    columns = [swap(half[i].astype(jnp.bfloat16), "wide", 2 * i) for i in range(1, n_wide // 2)]
-    mine = jnp.concatenate([near, far])
+    across_far = [swap(got[2], "narrow", 2), swap(got[3], "narrow", 2)]
+    mine = jnp.concatenate([near, got[2], got[3]])
     beside = swap(mine, "narrow", 1)
-    across_far, *columns = tie(across_far, *columns)
-    across = jnp.concatenate([across_near, across_far])
+    pieces = lambda j, flip, those: tuple((j ^ s, i, flip) for i in those for s in range(2))
+    half_way, every = range(n_wide // 4), range(n_wide // 2)
+    sums = early_part([pieces(0, 0, every), pieces(2, 0, half_way)], place, ids, [mine, across_near], n_narrow, rows)
+    *across_far, columns[0], columns[1], columns[2], columns[3], sums = tie(*across_far, *columns, sums)
+    across = jnp.concatenate([across_near, *across_far])
     opposite = swap(across, "narrow", 1)
-    part = sum([column.astype(jnp.float32) for column in columns], half[0]) / math.sqrt(total)
-    others = [swap(part, "narrow", bit) for bit in (1, 2, 3)]
-    pieces = lambda j, flip: tuple((j ^ s, i, flip) for i in range(n_wide // 2) for s in range(2))
+    part = sum(column.astype(jnp.float32) for column in columns) / math.sqrt(total)
+    others = [swap(part.astype(jnp.bfloat16) if bit > 1 else part, "narrow", bit) for bit in (1, 2, 3)]
+    late = jnp.concatenate(across_far)
     new_table, new_accum = row_part(
-        [pieces(0, 0), pieces(1, 1), pieces(2, 0), pieces(3, 1)],
-        place, ids, [mine, beside, across, opposite], n_narrow, tables[0], accum,
+        [pieces(1, 1, every), pieces(2, 0, range(n_wide // 4, n_wide // 2)), pieces(3, 1, every)],
+        place, ids, [beside, late, opposite], n_narrow, tables[0], accum, sums,
     )
     others[0], others[1], others[2], new_accum = tie(*others, new_accum)
-    part, other = part + others[1], others[0] + others[2]
-    low = jnp.where(core == 0, part, other)
-    high = jnp.where(core == 0, other, part)
-    w_grad = jnp.concatenate([low, high], axis=0)[:inputs].T
+    w_grad = sum((other.astype(jnp.float32) for other in others), part)[:inputs].T
     return (new_table[None], new_accum, w_grad)
 
 

time: 42.6 us -> 41.7 us (0.979)
  starting transfers between devices: 25.9 us -> 22.9 us
  waiting for transfers between devices: 4.83 us -> 7.39 us
  other arithmetic: 1.85 us -> 1.07 us
  Pallas kernels: 8.7 us -> 9.17 us
    ppermute x13 -> x10, starting transfers between devices: 19.5 us -> 7.07 us  [swap(): return lax.ppermute(array, axis, [(i, i ^ bit) for i in range(n)])]
    ppermute x4 -> x8, starting transfers between devices: 6.4 us -> 15.8 us  [reach(): return lax.ppermute(block, ('wide', 'narrow'), pairs)]
    ppermute x4 -> x8, waiting for transfers between devices: 0.18 us -> 5.27 us  [reach(): return lax.ppermute(block, ('wide', 'narrow'), pairs)]
    ppermute x13 -> x10, waiting for transfers between devices: 4.65 us -> 2.12 us  [swap(): return lax.ppermute(array, axis, [(i, i ^ bit) for i in range(n)])]
    pallas_call x0 -> x1, Pallas kernels: none -> 1.52 us  [early_part(): pl.pallas_call(functools.partial(early_kernel, groups, n_narrow), out_sha...]
    div x1 -> x0, other arithmetic: 0.83 us -> none  [body(): sum([column.astype(jnp.float32) for column in columns], half[0])]
    pallas_call x1, Pallas kernels: 4.29 us -> 3.49 us  [row_part(): pl.pallas_call(functools.partial(row_kernel, groups, n_narrow), out_shape...]
  transfers between devices with their start and end apart: 17 -> 18, of which waited for: 5 -> 5; matrix products, arithmetic and copies ran while one was open for 3% -> 1% of each run, Pallas kernels for 10% -> 12%
where the time goes in v4:
time: 41.7 us; the launch traced here: 41.5 us
  starting transfers between devices  22.9 us (55%)
  Pallas kernels  9.17 us (22%)
  waiting for transfers between devices  7.39 us (18%)
  other arithmetic  1.07 us (3%)
  between operations  0.88 us (2%)
    ppermute x8, starting transfers between devices, reach(): return lax.ppermute(block, ('wide', 'narrow'), pairs)  15.8 us
    ppermute x10, starting transfers between devices, swap(): return lax.ppermute(array, axis, [(i, i ^ bit) for i in range(n)])  7.07 us
    ppermute x8, waiting for transfers between devices, reach(): return lax.ppermute(block, ('wide', 'narrow'), pairs)  5.27 us
    pallas_call x1, Pallas kernels, local_part(): pl.pallas_call(local_kernel, out_shape=[jax.ShapeDtypeStruct(shape, jnp.b...  4.16 us
    pallas_call x1, Pallas kernels, row_part(): pl.pallas_call(functools.partial(row_kernel, groups, n_narrow), out_shape...  3.49 us
    ppermute x10, waiting for transfers between devices, swap(): return lax.ppermute(array, axis, [(i, i ^ bit) for i in range(n)])  2.12 us
    pallas_call x1, Pallas kernels, early_part(): pl.pallas_call(functools.partial(early_kernel, groups, n_narrow), out_sha...  1.52 us
  transfers between devices with their start and end apart: 18, of which 5 were waited for; matrix products, arithmetic and copies ran while one was open for 1% of the time, Pallas kernels for 12%

profile of v4, /device:TPU:0, one launch (start us, length us, event | category | flops | bytes accessed | tf_op | source)
XLA Modules:
  0.0 41.5 jit_solution(3070670526847627456)
XLA Ops:
  0.6 0.1 pad_add_fusion.place
  0.7 4.2 %shard_map.103 = (bf16[4,128,256]{2,1,0:T(8,128)(2,1)S(1)}, bf16[4,128,256]{2,1,0:T(8,128)(2,1)S(1)}, f32[4,304,128]{2,1,0:T(8,128)S(1)}, f32[4,304,128]{2,1,0:T(8,128)S(1)}) custom-call(s32[3]{0:T(128)S(1)} %pad_add_fusion.place, bf16[128,256]{1,0:T(8,128)(2,1)} %dense_in.1, bf16[1024,256]{1,0:T(8,128)(2,1)} %bitcast.25, bf16[292,1024]{1,0:T(8,128)(2,1)} %bitcast.24, ...), custom_call_target="tpu_custom_call" | custom-call | tf_op jit(solution)/shard_map/pallas_call | solution.py:121
  4.9 0.5 %collective-permute-start = (bf16[4,128,256]{2,1,0:T(8,128)(2,1)S(1)}, bf16[4,128,256]{2,1,0:T(8,128)(2,1)S(1)}, u32[]{:S(2)}, u32[]{:S(2)}) collective-permute-start(bf16[4,128,256]{2,1,0:T(8,128)(2,1)S(1)} %get-tuple-element.27), channel_id=1, source_target_pairs={{0,1},{1,0},{2,3},{3,2},{4,5},{5,4},{6,7},{7,6},{8,9},{9,8},{10,11... | collective-permute-start | bytes 786440 | tf_op jit(solution)/shard_map/ppermute | solution.py:337
  5.4 0.1 collective-permute-start.5
  5.5 1.1 %collective-permute-done = bf16[4,128,256]{2,1,0:T(8,128)(2,1)S(1)} collective-permute-done((bf16[4,128,256]{2,1,0:T(8,128)(2,1)S(1)}, bf16[4,128,256]{2,1,0:T(8,128)(2,1)S(1)}, u32[]{:S(2)}, u32[]{:S(2)}) %collective-permute-start) | collective-permute-done | bytes 262176 | tf_op jit(solution)/shard_map/ppermute | solution.py:337
  6.6 0.7 %collective-permute-start.3 = (bf16[2,128,256]{2,1,0:T(8,128)(2,1)S(1)}, bf16[2,128,256]{2,1,0:T(8,128)(2,1)S(1)}, u32[]{:S(2)}, u32[]{:S(2)}) collective-permute-start(bf16[2,128,256]{2,1,0:T(8,128)(2,1)S(1)} %pad_maximum_fusion.5), channel_id=1, source_target_pairs={{0,0},{1,5},{2,2},{3,7},{4,4},{5,1},{6,6},{7,3},{8,8},{9,13},{10,1... | collective-permute-start | bytes 393224 | tf_op jit(solution)/shard_map/ppermute | solution.py:350
  7.3 4.0 %collective-permute-start.4 = (bf16[2,128,256]{2,1,0:T(8,128)(2,1)S(1)}, bf16[2,128,256]{2,1,0:T(8,128)(2,1)S(1)}, u32[]{:S(2)}, u32[]{:S(2)}) collective-permute-start(bf16[2,128,256]{2,1,0:T(8,128)(2,1)S(1)} %pad_maximum_fusion.6), channel_id=1, source_target_pairs={{0,12},{1,9},{2,14},{3,11},{4,8},{5,13},{6,10},{7,15},{8,4},{9,1},... | collective-permute-start | bytes 393224 | tf_op jit(solution)/shard_map/ppermute | solution.py:350
  11.3 2.7 %collective-permute-start.1 = (bf16[2,128,256]{2,1,0:T(8,128)(2,1)S(1)}, bf16[2,128,256]{2,1,0:T(8,128)(2,1)S(1)}, u32[]{:S(2)}, u32[]{:S(2)}) collective-permute-start(bf16[2,128,256]{2,1,0:T(8,128)(2,1)S(1)} %pad_maximum_fusion.3), channel_id=1, source_target_pairs={{0,16},{1,21},{2,18},{3,23},{4,20},{5,17},{6,22},{7,19},{8,24},{9,... | collective-permute-start | bytes 393224 | tf_op jit(solution)/shard_map/ppermute | solution.py:350
  14.0 0.1 collective-permute-start.2
  14.1 0.7 %collective-permute-done.4 = bf16[2,128,256]{2,1,0:T(8,128)(2,1)S(1)} collective-permute-done((bf16[2,128,256]{2,1,0:T(8,128)(2,1)S(1)}, bf16[2,128,256]{2,1,0:T(8,128)(2,1)S(1)}, u32[]{:S(2)}, u32[]{:S(2)}) %collective-permute-start.4) | collective-permute-done | bytes 131104 | tf_op jit(solution)/shard_map/ppermute | solution.py:350
  14.8 2.2 %collective-permute-start.6 = (bf16[4,128,256]{2,1,0:T(8,128)(2,1)S(1)}, bf16[4,128,256]{2,1,0:T(8,128)(2,1)S(1)}, u32[]{:S(2)}, u32[]{:S(2)}) collective-permute-start(bf16[4,128,256]{2,1,0:T(8,128)(2,1)S(1)} %pad_maximum_fusion.1), channel_id=1, source_target_pairs={{0,2},{1,3},{2,0},{3,1},{4,6},{5,7},{6,4},{7,5},{8,10},{9,11},{10,... | collective-permute-start | bytes 786440 | tf_op jit(solution)/shard_map/ppermute | solution.py:337
  17.0 0.1 add_convert_fusion
  17.1 0.7 %collective-permute-start.9 = (bf16[304,128]{1,0:T(8,128)(2,1)S(1)}, bf16[304,128]{1,0:T(8,128)(2,1)S(1)}, u32[]{:S(2)}, u32[]{:S(2)}) collective-permute-start(bf16[304,128]{1,0:T(8,128)(2,1)S(1)} %get-tuple-element.54), channel_id=1, source_target_pairs={{0,0},{1,5},{2,2},{3,7},{4,4},{5,1},{6,6},{7,3},{8,8},{9,13},{10,1... | collective-permute-start | bytes 233480 | tf_op jit(solution)/shard_map/ppermute | solution.py:350
  17.8 2.6 %collective-permute-start.10 = (bf16[304,128]{1,0:T(8,128)(2,1)S(1)}, bf16[304,128]{1,0:T(8,128)(2,1)S(1)}, u32[]{:S(2)}, u32[]{:S(2)}) collective-permute-start(bf16[304,128]{1,0:T(8,128)(2,1)S(1)} %get-tuple-element.53), channel_id=1, source_target_pairs={{0,12},{1,9},{2,14},{3,11},{4,8},{5,13},{6,10},{7,15},{8,4},{9,1},... | collective-permute-start | bytes 233480 | tf_op jit(solution)/shard_map/ppermute | solution.py:350
  20.4 3.8 %collective-permute-done.1 = bf16[2,128,256]{2,1,0:T(8,128)(2,1)S(1)} collective-permute-done((bf16[2,128,256]{2,1,0:T(8,128)(2,1)S(1)}, bf16[2,128,256]{2,1,0:T(8,128)(2,1)S(1)}, u32[]{:S(2)}, u32[]{:S(2)}) %collective-permute-start.1) | collective-permute-done | bytes 131104 | tf_op jit(solution)/shard_map/ppermute | solution.py:350
  24.1 0.1 collective-permute-start.11
  24.2 1.4 %collective-permute-start.7 = (bf16[2,128,256]{2,1,0:T(8,128)(2,1)S(1)}, bf16[2,128,256]{2,1,0:T(8,128)(2,1)S(1)}, u32[]{:S(2)}, u32[]{:S(2)}) collective-permute-start(bf16[2,128,256]{2,1,0:T(8,128)(2,1)S(1)} %collective-permute-done.1), channel_id=1, source_target_pairs={{0,2},{1,3},{2,0},{3,1},{4,6},{5,7},{6,4},{7,5},{8,10},{9,11},{10,... | collective-permute-start | bytes 393224 | tf_op jit(solution)/shard_map/ppermute | solution.py:337
  25.7 0.6 %collective-permute-start.8 = (bf16[2,128,256]{2,1,0:T(8,128)(2,1)S(1)}, bf16[2,128,256]{2,1,0:T(8,128)(2,1)S(1)}, u32[]{:S(2)}, u32[]{:S(2)}) collective-permute-start(bf16[2,128,256]{2,1,0:T(8,128)(2,1)S(1)} %collective-permute-done.2), channel_id=1, source_target_pairs={{0,2},{1,3},{2,0},{3,1},{4,6},{5,7},{6,4},{7,5},{8,10},{9,11},{10,... | collective-permute-start | bytes 393224 | tf_op jit(solution)/shard_map/ppermute | solution.py:337
  26.3 0.0 copy-start
  26.3 5.1 %collective-permute-start.12 = (bf16[304,128]{1,0:T(8,128)(2,1)S(1)}, bf16[304,128]{1,0:T(8,128)(2,1)S(1)}, u32[]{:S(2)}, u32[]{:S(2)}) collective-permute-start(bf16[304,128]{1,0:T(8,128)(2,1)S(1)} %get-tuple-element.51), channel_id=1, source_target_pairs={{0,28},{1,25},{2,30},{3,27},{4,24},{5,29},{6,26},{7,31},{8,20},{9,... | collective-permute-start | bytes 233480 | tf_op jit(solution)/shard_map/ppermute | solution.py:350
  31.4 1.5 %shard_map.104.before = f32[1024,256]{1,0:T(8,128)S(1)} custom-call(s32[3]{0:T(128)S(1)} %pad_add_fusion.place, s32[2,4096]{1,0:T(2,128)S(1)} %bitcast.21, bf16[8,128,256]{2,1,0:T(8,128)(2,1)S(1)} %constant_dynamic-update-slice_fusion.refs_0_, bf16[4,128,256]{2,1,0:T(8,128)(2,1)S(1)} %collective-permute-done.6.refs_1_), custom_call_target="tpu_custom_call" | custom-call | tf_op jit(solution)/shard_map/pallas_call | solution.py:227
  32.9 0.0 copy-start.1
  32.9 0.1 collective-permute-start.13
  33.0 0.8 %collective-permute-done.12 = bf16[304,128]{1,0:T(8,128)(2,1)S(1)} collective-permute-done((bf16[304,128]{1,0:T(8,128)(2,1)S(1)}, bf16[304,128]{1,0:T(8,128)(2,1)S(1)}, u32[]{:S(2)}, u32[]{:S(2)}) %collective-permute-start.12) | collective-permute-done | bytes 77856 | tf_op jit(solution)/shard_map/ppermute | solution.py:350
  33.9 0.1 pad_maximum_fusion
  33.9 0.1 collective-permute-start.14
  34.0 0.1 fusion.3
  34.1 0.6 %collective-permute-start.15 = (f32[304,128]{1,0:T(8,128)S(1)}, f32[304,128]{1,0:T(8,128)S(1)}, u32[]{:S(2)}, u32[]{:S(2)}) collective-permute-start(f32[304,128]{1,0:T(8,128)S(1)} %get-tuple-element.50), channel_id=1, source_target_pairs={{0,1},{1,0},{2,3},{3,2},{4,5},{5,4},{6,7},{7,6},{8,9},{9,8},{10,11... | collective-permute-start | bytes 466952 | tf_op jit(solution)/shard_map/ppermute | solution.py:337
  34.7 1.6 %collective-permute-start.16 = (bf16[304,128]{1,0:T(8,128)(2,1)S(1)}, bf16[304,128]{1,0:T(8,128)(2,1)S(1)}, u32[]{:S(2)}, u32[]{:S(2)}) collective-permute-start(bf16[304,128]{1,0:T(8,128)(2,1)S(1)} %get-tuple-element.49), channel_id=1, source_target_pairs={{0,2},{1,3},{2,0},{3,1},{4,6},{5,7},{6,4},{7,5},{8,10},{9,11},{10,... | collective-permute-start | bytes 233480 | tf_op jit(solution)/shard_map/ppermute | solution.py:337
  36.3 3.5 %shard_map.105 = (f32[1024,256]{1,0:T(8,128)}, f32[1,1024]{1,0:T(1,128)}) custom-call(s32[3]{0:T(128)S(1)} %pad_add_fusion.place, s32[2,4096]{1,0:T(2,128)S(1)} %bitcast.22, f32[1024,256]{1,0:T(8,128)S(1)} %bitcast.23, f32[1,1024]{1,0:T(1,128)S(1)} %copy-done.2, f32[1024,256]{1,0:T(8,128)S(1)} %shard_map.104.before, ...), custom_call_target="tpu_custom_call" | custom-call | flops 1342177280 | bytes 2097152 | tf_op jit(solution)/shard_map/pallas_call | solution.py:242
  39.8 1.0 %collective-permute-done.17 = bf16[304,128]{1,0:T(8,128)(2,1)S(1)} collective-permute-done((bf16[304,128]{1,0:T(8,128)(2,1)S(1)}, bf16[304,128]{1,0:T(8,128)(2,1)S(1)}, u32[]{:S(2)}, u32[]{:S(2)}) %collective-permute-start.17) | collective-permute-done | bytes 77856 | tf_op jit(solution)/shard_map/ppermute | solution.py:337
  40.8 0.7 %fusion.2 = f32[128,292]{0,1:T(8,128)} fusion(f32[304,128]{1,0:T(8,128)S(1)} %collective-permute-done.15, f32[304,128]{1,0:T(8,128)S(1)} %get-tuple-element.50, bf16[304,128]{1,0:T(8,128)(2,1)S(1)} %collective-permute-done.17, bf16[304,128]{1,0:T(8,128)(2,1)S(1)} %collective-permute-done.16), kind=kLoop, calls=%fused_computation.8 | loop fusion | flops 186880 | bytes 598016 | tf_op jit(solution)/shard_map/transpose | solution.py:376
  (31 shorter events, 0.3 us)
Async XLA Ops:
  4.9 1.7 %collective-permute-start = (bf16[4,128,256]{2,1,0:T(8,128)(2,1)S(1)}, bf16[4,128,256]{2,1,0:T(8,128)(2,1)S(1)}, u32[]{:S(2)}, u32[]{:S(2)}) collective-permute-start(bf16[4,128,256]{2,1,0:T(8,128)(2,1)S(1)} %get-tuple-element.27), channel_id=1, source_target_pairs={{0,1},{1,0},{2,3},{3,2},{4,5},{5,4},{6,7},{7,6},{8,9},{9,8},{10,11... | collective-permute-start | bytes 786440 | tf_op jit(solution)/shard_map/ppermute | solution.py:337
  5.4 9.3 %collective-permute-start.5 = (f32[4,304,128]{2,1,0:T(8,128)S(1)}, f32[4,304,128]{2,1,0:T(8,128)S(1)}, u32[]{:S(2)}, u32[]{:S(2)}) collective-permute-start(f32[4,304,128]{2,1,0:T(8,128)S(1)} %get-tuple-element.28), channel_id=1, source_target_pairs={{0,1},{1,0},{2,3},{3,2},{4,5},{5,4},{6,7},{7,6},{8,9},{9,8},{10,11... | collective-permute-start | bytes 1867784 | tf_op jit(solution)/shard_map/ppermute | solution.py:337
  6.6 7.4 %collective-permute-start.3 = (bf16[2,128,256]{2,1,0:T(8,128)(2,1)S(1)}, bf16[2,128,256]{2,1,0:T(8,128)(2,1)S(1)}, u32[]{:S(2)}, u32[]{:S(2)}) collective-permute-start(bf16[2,128,256]{2,1,0:T(8,128)(2,1)S(1)} %pad_maximum_fusion.5), channel_id=1, source_target_pairs={{0,0},{1,5},{2,2},{3,7},{4,4},{5,1},{6,6},{7,3},{8,8},{9,13},{10,1... | collective-permute-start | bytes 393224 | tf_op jit(solution)/shard_map/ppermute | solution.py:350
  7.3 7.4 %collective-permute-start.4 = (bf16[2,128,256]{2,1,0:T(8,128)(2,1)S(1)}, bf16[2,128,256]{2,1,0:T(8,128)(2,1)S(1)}, u32[]{:S(2)}, u32[]{:S(2)}) collective-permute-start(bf16[2,128,256]{2,1,0:T(8,128)(2,1)S(1)} %pad_maximum_fusion.6), channel_id=1, source_target_pairs={{0,12},{1,9},{2,14},{3,11},{4,8},{5,13},{6,10},{7,15},{8,4},{9,1},... | collective-permute-start | bytes 393224 | tf_op jit(solution)/shard_map/ppermute | solution.py:350
  11.3 12.8 %collective-permute-start.1 = (bf16[2,128,256]{2,1,0:T(8,128)(2,1)S(1)}, bf16[2,128,256]{2,1,0:T(8,128)(2,1)S(1)}, u32[]{:S(2)}, u32[]{:S(2)}) collective-permute-start(bf16[2,128,256]{2,1,0:T(8,128)(2,1)S(1)} %pad_maximum_fusion.3), channel_id=1, source_target_pairs={{0,16},{1,21},{2,18},{3,23},{4,20},{5,17},{6,22},{7,19},{8,24},{9,... | collective-permute-start | bytes 393224 | tf_op jit(solution)/shard_map/ppermute | solution.py:350
  14.0 10.3 %collective-permute-start.2 = (bf16[2,128,256]{2,1,0:T(8,128)(2,1)S(1)}, bf16[2,128,256]{2,1,0:T(8,128)(2,1)S(1)}, u32[]{:S(2)}, u32[]{:S(2)}) collective-permute-start(bf16[2,128,256]{2,1,0:T(8,128)(2,1)S(1)} %pad_maximum_fusion.4), channel_id=1, source_target_pairs={{0,28},{1,25},{2,30},{3,27},{4,24},{5,29},{6,26},{7,31},{8,20},{9,... | collective-permute-start | bytes 393224 | tf_op jit(solution)/shard_map/ppermute | solution.py:350
  14.8 9.5 %collective-permute-start.6 = (bf16[4,128,256]{2,1,0:T(8,128)(2,1)S(1)}, bf16[4,128,256]{2,1,0:T(8,128)(2,1)S(1)}, u32[]{:S(2)}, u32[]{:S(2)}) collective-permute-start(bf16[4,128,256]{2,1,0:T(8,128)(2,1)S(1)} %pad_maximum_fusion.1), channel_id=1, source_target_pairs={{0,2},{1,3},{2,0},{3,1},{4,6},{5,7},{6,4},{7,5},{8,10},{9,11},{10,... | collective-permute-start | bytes 786440 | tf_op jit(solution)/shard_map/ppermute | solution.py:337
  17.1 9.2 %collective-permute-start.9 = (bf16[304,128]{1,0:T(8,128)(2,1)S(1)}, bf16[304,128]{1,0:T(8,128)(2,1)S(1)}, u32[]{:S(2)}, u32[]{:S(2)}) collective-permute-start(bf16[304,128]{1,0:T(8,128)(2,1)S(1)} %get-tuple-element.54), channel_id=1, source_target_pairs={{0,0},{1,5},{2,2},{3,7},{4,4},{5,1},{6,6},{7,3},{8,8},{9,13},{10,1... | collective-permute-start | bytes 233480 | tf_op jit(solution)/shard_map/ppermute | solution.py:350
  17.8 15.2 %collective-permute-start.10 = (bf16[304,128]{1,0:T(8,128)(2,1)S(1)}, bf16[304,128]{1,0:T(8,128)(2,1)S(1)}, u32[]{:S(2)}, u32[]{:S(2)}) collective-permute-start(bf16[304,128]{1,0:T(8,128)(2,1)S(1)} %get-tuple-element.53), channel_id=1, source_target_pairs={{0,12},{1,9},{2,14},{3,11},{4,8},{5,13},{6,10},{7,15},{8,4},{9,1},... | collective-permute-start | bytes 233480 | tf_op jit(solution)/shard_map/ppermute | solution.py:350
  24.1 8.9 %collective-permute-start.11 = (bf16[304,128]{1,0:T(8,128)(2,1)S(1)}, bf16[304,128]{1,0:T(8,128)(2,1)S(1)}, u32[]{:S(2)}, u32[]{:S(2)}) collective-permute-start(bf16[304,128]{1,0:T(8,128)(2,1)S(1)} %get-tuple-element.52), channel_id=1, source_target_pairs={{0,16},{1,21},{2,18},{3,23},{4,20},{5,17},{6,22},{7,19},{8,24},{9,... | collective-permute-start | bytes 233480 | tf_op jit(solution)/shard_map/ppermute | solution.py:350
  24.2 9.6 %collective-permute-start.7 = (bf16[2,128,256]{2,1,0:T(8,128)(2,1)S(1)}, bf16[2,128,256]{2,1,0:T(8,128)(2,1)S(1)}, u32[]{:S(2)}, u32[]{:S(2)}) collective-permute-start(bf16[2,128,256]{2,1,0:T(8,128)(2,1)S(1)} %collective-permute-done.1), channel_id=1, source_target_pairs={{0,2},{1,3},{2,0},{3,1},{4,6},{5,7},{6,4},{7,5},{8,10},{9,11},{10,... | collective-permute-start | bytes 393224 | tf_op jit(solution)/shard_map/ppermute | solution.py:337
  25.7 8.2 %collective-permute-start.8 = (bf16[2,128,256]{2,1,0:T(8,128)(2,1)S(1)}, bf16[2,128,256]{2,1,0:T(8,128)(2,1)S(1)}, u32[]{:S(2)}, u32[]{:S(2)}) collective-permute-start(bf16[2,128,256]{2,1,0:T(8,128)(2,1)S(1)} %collective-permute-done.2), channel_id=1, source_target_pairs={{0,2},{1,3},{2,0},{3,1},{4,6},{5,7},{6,4},{7,5},{8,10},{9,11},{10,... | collective-permute-start | bytes 393224 | tf_op jit(solution)/shard_map/ppermute | solution.py:337
  26.3 5.1 %copy-start = (s32[1,4096,2]{1,2,0:T(2,128)S(1)}, s32[1,4096,2]{1,2,0:T(2,128)}, u32[]{:S(2)}) copy-start(s32[1,4096,2]{1,2,0:T(2,128)} %param.13) | copy-start | bytes 98308
  26.3 7.5 %collective-permute-start.12 = (bf16[304,128]{1,0:T(8,128)(2,1)S(1)}, bf16[304,128]{1,0:T(8,128)(2,1)S(1)}, u32[]{:S(2)}, u32[]{:S(2)}) collective-permute-start(bf16[304,128]{1,0:T(8,128)(2,1)S(1)} %get-tuple-element.51), channel_id=1, source_target_pairs={{0,28},{1,25},{2,30},{3,27},{4,24},{5,29},{6,26},{7,31},{8,20},{9,... | collective-permute-start | bytes 233480 | tf_op jit(solution)/shard_map/ppermute | solution.py:350
  32.9 3.3 %copy-start.1 = (f32[1,1024,256]{2,1,0:T(8,128)S(1)}, f32[1,1024,256]{2,1,0:T(8,128)}, u32[]{:S(2)}) copy-start(f32[1,1024,256]{2,1,0:T(8,128)} %param.14) | copy-start | bytes 3145732
  32.9 3.3 %collective-permute-start.13 = (bf16[8,128,256]{2,1,0:T(8,128)(2,1)S(1)}, bf16[8,128,256]{2,1,0:T(8,128)(2,1)S(1)}, u32[]{:S(2)}, u32[]{:S(2)}) collective-permute-start(bf16[8,128,256]{2,1,0:T(8,128)(2,1)S(1)} %constant_dynamic-update-slice_fusion.refs_0_), channel_id=1, source_target_pairs={{0,1},{1,0},{2,3},{3,2},{4,5},{5,4},{6,7},{7,6},{8,9},{9,8},{10,11... | collective-permute-start | bytes 1572872 | tf_op jit(solution)/shard_map/ppermute | solution.py:337
  33.9 2.3 %collective-permute-start.14 = (bf16[8,128,256]{2,1,0:T(8,128)(2,1)S(1)}, bf16[8,128,256]{2,1,0:T(8,128)(2,1)S(1)}, u32[]{:S(2)}, u32[]{:S(2)}) collective-permute-start(bf16[8,128,256]{2,1,0:T(8,128)(2,1)S(1)} %pad_maximum_fusion), channel_id=1, source_target_pairs={{0,1},{1,0},{2,3},{3,2},{4,5},{5,4},{6,7},{7,6},{8,9},{9,8},{10,11... | collective-permute-start | bytes 1572872 | tf_op jit(solution)/shard_map/ppermute | solution.py:337
  34.1 2.2 %copy-start.2 = (f32[1,1024]{1,0:T(1,128)S(1)}, f32[1,1024]{1,0:T(1,128)}, u32[]{:S(2)}) copy-start(f32[1,1024]{1,0:T(1,128)} %accum.1) | copy-start | bytes 12292
  34.1 6.7 %collective-permute-start.15 = (f32[304,128]{1,0:T(8,128)S(1)}, f32[304,128]{1,0:T(8,128)S(1)}, u32[]{:S(2)}, u32[]{:S(2)}) collective-permute-start(f32[304,128]{1,0:T(8,128)S(1)} %get-tuple-element.50), channel_id=1, source_target_pairs={{0,1},{1,0},{2,3},{3,2},{4,5},{5,4},{6,7},{7,6},{8,9},{9,8},{10,11... | collective-permute-start | bytes 466952 | tf_op jit(solution)/shard_map/ppermute | solution.py:337
  34.7 5.1 %collective-permute-start.16 = (bf16[304,128]{1,0:T(8,128)(2,1)S(1)}, bf16[304,128]{1,0:T(8,128)(2,1)S(1)}, u32[]{:S(2)}, u32[]{:S(2)}) collective-permute-start(bf16[304,128]{1,0:T(8,128)(2,1)S(1)} %get-tuple-element.49), channel_id=1, source_target_pairs={{0,2},{1,3},{2,0},{3,1},{4,6},{5,7},{6,4},{7,5},{8,10},{9,11},{10,... | collective-permute-start | bytes 233480 | tf_op jit(solution)/shard_map/ppermute | solution.py:337
  36.2 4.6 %collective-permute-start.17 = (bf16[304,128]{1,0:T(8,128)(2,1)S(1)}, bf16[304,128]{1,0:T(8,128)(2,1)S(1)}, u32[]{:S(2)}, u32[]{:S(2)}) collective-permute-start(bf16[304,128]{1,0:T(8,128)(2,1)S(1)} %get-tuple-element.49), channel_id=1, source_target_pairs={{0,3},{1,2},{2,1},{3,0},{4,7},{5,6},{6,5},{7,4},{8,11},{9,10},{10,... | collective-permute-start | bytes 233480 | tf_op jit(solution)/shard_map/ppermute | solution.py:337

commit v5 on v4

--- a/solution.py
+++ b/solution.py
@@ -326,7 +326,10 @@
     rows, width = tables.shape[1:]
     inputs = w_top.shape[1]
     total = samples * n_wide * n_narrow
-    if n_narrow != 4 or n_wide & (n_wide - 1) or count != n_wide or total * width > 2**21:
+    fits = (n_wide, n_narrow, count, bag_ids.shape[2], samples) == (8, 4, 8, 2, 128) and inputs - width <= 48
+    fits = fits and width % 128 == 0 and width <= 256 and rows % 256 == 0 and rows * n_narrow < 2**15
+    fits = fits and w_top.shape[0] % (128 * n_wide) == 0 and w_top.shape[0] <= 2048
+    if not fits:
         return plain_body(dense, pooled, w_top, bias, d_hidden, bag_ids, tables, accum)
     wide, narrow = lax.axis_index("wide"), lax.axis_index("narrow")
     core, chip = narrow % 2, narrow // 2
@@ -350,7 +353,7 @@
         return lax.ppermute(block, ("wide", "narrow"), pairs)
 
     got = {i: reach(jnp.stack([hold[i], taken[i]]), i) for i in (1, 0, 2, 3)}
-    got[0], got[1], received = tie(got[0], got[1], received)
+    got[1], got[0], received = tie(got[1], got[0], received)
     half = keep + received
     columns = [reach(half[i].astype(jnp.bfloat16), i) for i in (0, 1, 2, 3)]
     near = jnp.concatenate([got[0], got[1]])
@@ -373,7 +376,8 @@
         place, ids, [beside, late, opposite], n_narrow, tables[0], accum, sums,
     )
     others[0], others[1], others[2], new_accum = tie(*others, new_accum)
-    w_grad = sum((other.astype(jnp.float32) for other in others), part)[:inputs].T
+    parts = [lax.reduce_precision(x, 8, 7) for x in (part, others[0])] + [x.astype(jnp.float32) for x in others[1:]]
+    w_grad = ((parts[0] + parts[1]) + (parts[2] + parts[3]))[:inputs].T
     return (new_table[None], new_accum, w_grad)
 
 

time: 41.7 us -> 41.4 us (level)
  starting transfers between devices: 22.9 us -> 19.8 us
  waiting for transfers between devices: 7.39 us -> 10.1 us
    ppermute x8, waiting for transfers between devices: 5.27 us -> 7.92 us  [reach(): return lax.ppermute(block, ('wide', 'narrow'), pairs)]
    ppermute x8, starting transfers between devices: 15.8 us -> 13.4 us  [reach(): return lax.ppermute(block, ('wide', 'narrow'), pairs)]
    ppermute x10, starting transfers between devices: 7.07 us -> 6.42 us  [swap(): return lax.ppermute(array, axis, [(i, i ^ bit) for i in range(n)])]
  transfers between devices with their start and end apart: 18 -> 18, of which waited for: 5 -> 6; matrix products, arithmetic and copies ran while one was open for 1% -> 1% of each run, Pallas kernels for 12% -> 12%
where the time goes in v5:
time: 41.4 us; the launch traced here: 41.1 us
  starting transfers between devices  19.8 us (48%)
  waiting for transfers between devices  10.1 us (24%)
  Pallas kernels  9.17 us (22%)
  other arithmetic  1.08 us (3%)
  between operations  0.87 us (2%)
    ppermute x8, starting transfers between devices, reach(): return lax.ppermute(block, ('wide', 'narrow'), pairs)  13.4 us
    ppermute x8, waiting for transfers between devices, reach(): return lax.ppermute(block, ('wide', 'narrow'), pairs)  7.92 us
    ppermute x10, starting transfers between devices, swap(): return lax.ppermute(array, axis, [(i, i ^ bit) for i in range(n)])  6.42 us
    pallas_call x1, Pallas kernels, local_part(): pl.pallas_call(local_kernel, out_shape=[jax.ShapeDtypeStruct(shape, jnp.b...  4.16 us
    pallas_call x1, Pallas kernels, row_part(): pl.pallas_call(functools.partial(row_kernel, groups, n_narrow), out_shape...  3.49 us
    ppermute x10, waiting for transfers between devices, swap(): return lax.ppermute(array, axis, [(i, i ^ bit) for i in range(n)])  2.17 us
    pallas_call x1, Pallas kernels, early_part(): pl.pallas_call(functools.partial(early_kernel, groups, n_narrow), out_sha...  1.52 us
  transfers between devices with their start and end apart: 18, of which 6 were waited for; matrix products, arithmetic and copies ran while one was open for 1% of the time, Pallas kernels for 12%

profile of v5, /device:TPU:0, one launch (start us, length us, event | category | flops | bytes accessed | tf_op | source)
XLA Modules:
  0.0 41.1 jit_solution(9104242012663246324)
XLA Ops:
  0.6 0.1 pad_add_fusion.place
  0.7 4.2 %shard_map.103 = (bf16[4,128,256]{2,1,0:T(8,128)(2,1)S(1)}, bf16[4,128,256]{2,1,0:T(8,128)(2,1)S(1)}, f32[4,304,128]{2,1,0:T(8,128)S(1)}, f32[4,304,128]{2,1,0:T(8,128)S(1)}) custom-call(s32[3]{0:T(128)S(1)} %pad_add_fusion.place, bf16[128,256]{1,0:T(8,128)(2,1)} %dense_in.1, bf16[1024,256]{1,0:T(8,128)(2,1)} %bitcast.25, bf16[292,1024]{1,0:T(8,128)(2,1)} %bitcast.24, ...), custom_call_target="tpu_custom_call" | custom-call | tf_op jit(solution)/shard_map/pallas_call | solution.py:121
  4.9 0.5 %collective-permute-start = (bf16[4,128,256]{2,1,0:T(8,128)(2,1)S(1)}, bf16[4,128,256]{2,1,0:T(8,128)(2,1)S(1)}, u32[]{:S(2)}, u32[]{:S(2)}) collective-permute-start(bf16[4,128,256]{2,1,0:T(8,128)(2,1)S(1)} %get-tuple-element.27), channel_id=1, source_target_pairs={{0,1},{1,0},{2,3},{3,2},{4,5},{5,4},{6,7},{7,6},{8,9},{9,8},{10,11... | collective-permute-start | bytes 786440 | tf_op jit(solution)/shard_map/ppermute | solution.py:340
  5.4 0.1 collective-permute-start.5
  5.5 1.1 %collective-permute-done = bf16[4,128,256]{2,1,0:T(8,128)(2,1)S(1)} collective-permute-done((bf16[4,128,256]{2,1,0:T(8,128)(2,1)S(1)}, bf16[4,128,256]{2,1,0:T(8,128)(2,1)S(1)}, u32[]{:S(2)}, u32[]{:S(2)}) %collective-permute-start) | collective-permute-done | bytes 262176 | tf_op jit(solution)/shard_map/ppermute | solution.py:340
  6.6 4.0 %collective-permute-start.3 = (bf16[2,128,256]{2,1,0:T(8,128)(2,1)S(1)}, bf16[2,128,256]{2,1,0:T(8,128)(2,1)S(1)}, u32[]{:S(2)}, u32[]{:S(2)}) collective-permute-start(bf16[2,128,256]{2,1,0:T(8,128)(2,1)S(1)} %pad_maximum_fusion.5), channel_id=1, source_target_pairs={{0,12},{1,9},{2,14},{3,11},{4,8},{5,13},{6,10},{7,15},{8,4},{9,1},... | collective-permute-start | bytes 393224 | tf_op jit(solution)/shard_map/ppermute | solution.py:353
  10.6 0.7 %collective-permute-start.4 = (bf16[2,128,256]{2,1,0:T(8,128)(2,1)S(1)}, bf16[2,128,256]{2,1,0:T(8,128)(2,1)S(1)}, u32[]{:S(2)}, u32[]{:S(2)}) collective-permute-start(bf16[2,128,256]{2,1,0:T(8,128)(2,1)S(1)} %pad_maximum_fusion.6), channel_id=1, source_target_pairs={{0,0},{1,5},{2,2},{3,7},{4,4},{5,1},{6,6},{7,3},{8,8},{9,13},{10,1... | collective-permute-start | bytes 393224 | tf_op jit(solution)/shard_map/ppermute | solution.py:353
  11.3 2.7 %collective-permute-start.1 = (bf16[2,128,256]{2,1,0:T(8,128)(2,1)S(1)}, bf16[2,128,256]{2,1,0:T(8,128)(2,1)S(1)}, u32[]{:S(2)}, u32[]{:S(2)}) collective-permute-start(bf16[2,128,256]{2,1,0:T(8,128)(2,1)S(1)} %pad_maximum_fusion.3), channel_id=1, source_target_pairs={{0,16},{1,21},{2,18},{3,23},{4,20},{5,17},{6,22},{7,19},{8,24},{9,... | collective-permute-start | bytes 393224 | tf_op jit(solution)/shard_map/ppermute | solution.py:353
  14.0 0.1 collective-permute-start.2
  14.0 0.6 %collective-permute-done.3 = bf16[2,128,256]{2,1,0:T(8,128)(2,1)S(1)} collective-permute-done((bf16[2,128,256]{2,1,0:T(8,128)(2,1)S(1)}, bf16[2,128,256]{2,1,0:T(8,128)(2,1)S(1)}, u32[]{:S(2)}, u32[]{:S(2)}) %collective-permute-start.3) | collective-permute-done | bytes 131104 | tf_op jit(solution)/shard_map/ppermute | solution.py:353
  14.7 1.5 %collective-permute-start.6 = (bf16[4,128,256]{2,1,0:T(8,128)(2,1)S(1)}, bf16[4,128,256]{2,1,0:T(8,128)(2,1)S(1)}, u32[]{:S(2)}, u32[]{:S(2)}) collective-permute-start(bf16[4,128,256]{2,1,0:T(8,128)(2,1)S(1)} %pad_maximum_fusion.1), channel_id=1, source_target_pairs={{0,2},{1,3},{2,0},{3,1},{4,6},{5,7},{6,4},{7,5},{8,10},{9,11},{10,... | collective-permute-start | bytes 786440 | tf_op jit(solution)/shard_map/ppermute | solution.py:340
  16.2 0.1 add_convert_fusion
  16.3 0.7 %collective-permute-start.9 = (bf16[304,128]{1,0:T(8,128)(2,1)S(1)}, bf16[304,128]{1,0:T(8,128)(2,1)S(1)}, u32[]{:S(2)}, u32[]{:S(2)}) collective-permute-start(bf16[304,128]{1,0:T(8,128)(2,1)S(1)} %get-tuple-element.54), channel_id=1, source_target_pairs={{0,0},{1,5},{2,2},{3,7},{4,4},{5,1},{6,6},{7,3},{8,8},{9,13},{10,1... | collective-permute-start | bytes 233480 | tf_op jit(solution)/shard_map/ppermute | solution.py:353
  17.0 2.0 %collective-permute-start.10 = (bf16[304,128]{1,0:T(8,128)(2,1)S(1)}, bf16[304,128]{1,0:T(8,128)(2,1)S(1)}, u32[]{:S(2)}, u32[]{:S(2)}) collective-permute-start(bf16[304,128]{1,0:T(8,128)(2,1)S(1)} %get-tuple-element.53), channel_id=1, source_target_pairs={{0,12},{1,9},{2,14},{3,11},{4,8},{5,13},{6,10},{7,15},{8,4},{9,1},... | collective-permute-start | bytes 233480 | tf_op jit(solution)/shard_map/ppermute | solution.py:353
  19.0 5.1 %collective-permute-done.1 = bf16[2,128,256]{2,1,0:T(8,128)(2,1)S(1)} collective-permute-done((bf16[2,128,256]{2,1,0:T(8,128)(2,1)S(1)}, bf16[2,128,256]{2,1,0:T(8,128)(2,1)S(1)}, u32[]{:S(2)}, u32[]{:S(2)}) %collective-permute-start.1) | collective-permute-done | bytes 131104 | tf_op jit(solution)/shard_map/ppermute | solution.py:353
  24.1 1.6 %collective-permute-start.7 = (bf16[2,128,256]{2,1,0:T(8,128)(2,1)S(1)}, bf16[2,128,256]{2,1,0:T(8,128)(2,1)S(1)}, u32[]{:S(2)}, u32[]{:S(2)}) collective-permute-start(bf16[2,128,256]{2,1,0:T(8,128)(2,1)S(1)} %collective-permute-done.1), channel_id=1, source_target_pairs={{0,2},{1,3},{2,0},{3,1},{4,6},{5,7},{6,4},{7,5},{8,10},{9,11},{10,... | collective-permute-start | bytes 393224 | tf_op jit(solution)/shard_map/ppermute | solution.py:340
  25.6 0.6 %collective-permute-start.8 = (bf16[2,128,256]{2,1,0:T(8,128)(2,1)S(1)}, bf16[2,128,256]{2,1,0:T(8,128)(2,1)S(1)}, u32[]{:S(2)}, u32[]{:S(2)}) collective-permute-start(bf16[2,128,256]{2,1,0:T(8,128)(2,1)S(1)} %collective-permute-done.2), channel_id=1, source_target_pairs={{0,2},{1,3},{2,0},{3,1},{4,6},{5,7},{6,4},{7,5},{8,10},{9,11},{10,... | collective-permute-start | bytes 393224 | tf_op jit(solution)/shard_map/ppermute | solution.py:340
  26.2 0.0 copy-start
  26.2 3.3 %collective-permute-start.12 = (bf16[304,128]{1,0:T(8,128)(2,1)S(1)}, bf16[304,128]{1,0:T(8,128)(2,1)S(1)}, u32[]{:S(2)}, u32[]{:S(2)}) collective-permute-start(bf16[304,128]{1,0:T(8,128)(2,1)S(1)} %get-tuple-element.51), channel_id=1, source_target_pairs={{0,28},{1,25},{2,30},{3,27},{4,24},{5,29},{6,26},{7,31},{8,20},{9,... | collective-permute-start | bytes 233480 | tf_op jit(solution)/shard_map/ppermute | solution.py:353
  29.6 1.5 %shard_map.104.before = f32[1024,256]{1,0:T(8,128)S(1)} custom-call(s32[3]{0:T(128)S(1)} %pad_add_fusion.place, s32[2,4096]{1,0:T(2,128)S(1)} %bitcast.21, bf16[8,128,256]{2,1,0:T(8,128)(2,1)S(1)} %constant_dynamic-update-slice_fusion.refs_0_, bf16[4,128,256]{2,1,0:T(8,128)(2,1)S(1)} %collective-permute-done.6.refs_1_), custom_call_target="tpu_custom_call" | custom-call | tf_op jit(solution)/shard_map/pallas_call | solution.py:227
  31.1 0.0 copy-start.1
  31.1 0.1 collective-permute-start.13
  31.2 1.9 %collective-permute-done.11 = bf16[304,128]{1,0:T(8,128)(2,1)S(1)} collective-permute-done((bf16[304,128]{1,0:T(8,128)(2,1)S(1)}, bf16[304,128]{1,0:T(8,128)(2,1)S(1)}, u32[]{:S(2)}, u32[]{:S(2)}) %collective-permute-start.11) | collective-permute-done | bytes 77856 | tf_op jit(solution)/shard_map/ppermute | solution.py:353
  33.1 0.4 collective-permute-done.12
  33.5 0.1 pad_maximum_fusion
  33.5 0.1 collective-permute-start.14
  33.6 0.1 fusion.3
  33.7 0.6 %collective-permute-start.15 = (f32[304,128]{1,0:T(8,128)S(1)}, f32[304,128]{1,0:T(8,128)S(1)}, u32[]{:S(2)}, u32[]{:S(2)}) collective-permute-start(f32[304,128]{1,0:T(8,128)S(1)} %get-tuple-element.50), channel_id=1, source_target_pairs={{0,1},{1,0},{2,3},{3,2},{4,5},{5,4},{6,7},{7,6},{8,9},{9,8},{10,11... | collective-permute-start | bytes 466952 | tf_op jit(solution)/shard_map/ppermute | solution.py:340
  34.3 1.5 %collective-permute-start.16 = (bf16[304,128]{1,0:T(8,128)(2,1)S(1)}, bf16[304,128]{1,0:T(8,128)(2,1)S(1)}, u32[]{:S(2)}, u32[]{:S(2)}) collective-permute-start(bf16[304,128]{1,0:T(8,128)(2,1)S(1)} %get-tuple-element.49), channel_id=1, source_target_pairs={{0,2},{1,3},{2,0},{3,1},{4,6},{5,7},{6,4},{7,5},{8,10},{9,11},{10,... | collective-permute-start | bytes 233480 | tf_op jit(solution)/shard_map/ppermute | solution.py:340
  35.8 3.5 %shard_map.105 = (f32[1024,256]{1,0:T(8,128)}, f32[1,1024]{1,0:T(1,128)}) custom-call(s32[3]{0:T(128)S(1)} %pad_add_fusion.place, s32[2,4096]{1,0:T(2,128)S(1)} %bitcast.22, f32[1024,256]{1,0:T(8,128)S(1)} %bitcast.23, f32[1,1024]{1,0:T(1,128)S(1)} %copy-done.2, f32[1024,256]{1,0:T(8,128)S(1)} %shard_map.104.before, ...), custom_call_target="tpu_custom_call" | custom-call | flops 1342177280 | bytes 2097152 | tf_op jit(solution)/shard_map/pallas_call | solution.py:242
  39.3 1.1 %collective-permute-done.17 = bf16[304,128]{1,0:T(8,128)(2,1)S(1)} collective-permute-done((bf16[304,128]{1,0:T(8,128)(2,1)S(1)}, bf16[304,128]{1,0:T(8,128)(2,1)S(1)}, u32[]{:S(2)}, u32[]{:S(2)}) %collective-permute-start.17) | collective-permute-done | bytes 77856 | tf_op jit(solution)/shard_map/ppermute | solution.py:340
  40.4 0.7 %fusion.2 = f32[128,292]{0,1:T(8,128)} fusion(f32[304,128]{1,0:T(8,128)S(1)} %collective-permute-done.15, f32[304,128]{1,0:T(8,128)S(1)} %get-tuple-element.50, bf16[304,128]{1,0:T(8,128)(2,1)S(1)} %collective-permute-done.17, bf16[304,128]{1,0:T(8,128)(2,1)S(1)} %collective-permute-done.16), kind=kLoop, calls=%fused_computation.8 | loop fusion | flops 261632 | bytes 598016 | tf_op jit(solution)/shard_map/transpose | solution.py:380
  (31 shorter events, 0.3 us)
Async XLA Ops:
  4.9 1.7 %collective-permute-start = (bf16[4,128,256]{2,1,0:T(8,128)(2,1)S(1)}, bf16[4,128,256]{2,1,0:T(8,128)(2,1)S(1)}, u32[]{:S(2)}, u32[]{:S(2)}) collective-permute-start(bf16[4,128,256]{2,1,0:T(8,128)(2,1)S(1)} %get-tuple-element.27), channel_id=1, source_target_pairs={{0,1},{1,0},{2,3},{3,2},{4,5},{5,4},{6,7},{7,6},{8,9},{9,8},{10,11... | collective-permute-start | bytes 786440 | tf_op jit(solution)/shard_map/ppermute | solution.py:340
  5.4 9.2 %collective-permute-start.5 = (f32[4,304,128]{2,1,0:T(8,128)S(1)}, f32[4,304,128]{2,1,0:T(8,128)S(1)}, u32[]{:S(2)}, u32[]{:S(2)}) collective-permute-start(f32[4,304,128]{2,1,0:T(8,128)S(1)} %get-tuple-element.28), channel_id=1, source_target_pairs={{0,1},{1,0},{2,3},{3,2},{4,5},{5,4},{6,7},{7,6},{8,9},{9,8},{10,11... | collective-permute-start | bytes 1867784 | tf_op jit(solution)/shard_map/ppermute | solution.py:340
  6.6 8.0 %collective-permute-start.3 = (bf16[2,128,256]{2,1,0:T(8,128)(2,1)S(1)}, bf16[2,128,256]{2,1,0:T(8,128)(2,1)S(1)}, u32[]{:S(2)}, u32[]{:S(2)}) collective-permute-start(bf16[2,128,256]{2,1,0:T(8,128)(2,1)S(1)} %pad_maximum_fusion.5), channel_id=1, source_target_pairs={{0,12},{1,9},{2,14},{3,11},{4,8},{5,13},{6,10},{7,15},{8,4},{9,1},... | collective-permute-start | bytes 393224 | tf_op jit(solution)/shard_map/ppermute | solution.py:353
  10.6 4.1 %collective-permute-start.4 = (bf16[2,128,256]{2,1,0:T(8,128)(2,1)S(1)}, bf16[2,128,256]{2,1,0:T(8,128)(2,1)S(1)}, u32[]{:S(2)}, u32[]{:S(2)}) collective-permute-start(bf16[2,128,256]{2,1,0:T(8,128)(2,1)S(1)} %pad_maximum_fusion.6), channel_id=1, source_target_pairs={{0,0},{1,5},{2,2},{3,7},{4,4},{5,1},{6,6},{7,3},{8,8},{9,13},{10,1... | collective-permute-start | bytes 393224 | tf_op jit(solution)/shard_map/ppermute | solution.py:353
  11.3 12.8 %collective-permute-start.1 = (bf16[2,128,256]{2,1,0:T(8,128)(2,1)S(1)}, bf16[2,128,256]{2,1,0:T(8,128)(2,1)S(1)}, u32[]{:S(2)}, u32[]{:S(2)}) collective-permute-start(bf16[2,128,256]{2,1,0:T(8,128)(2,1)S(1)} %pad_maximum_fusion.3), channel_id=1, source_target_pairs={{0,16},{1,21},{2,18},{3,23},{4,20},{5,17},{6,22},{7,19},{8,24},{9,... | collective-permute-start | bytes 393224 | tf_op jit(solution)/shard_map/ppermute | solution.py:353
  14.0 10.1 %collective-permute-start.2 = (bf16[2,128,256]{2,1,0:T(8,128)(2,1)S(1)}, bf16[2,128,256]{2,1,0:T(8,128)(2,1)S(1)}, u32[]{:S(2)}, u32[]{:S(2)}) collective-permute-start(bf16[2,128,256]{2,1,0:T(8,128)(2,1)S(1)} %pad_maximum_fusion.4), channel_id=1, source_target_pairs={{0,28},{1,25},{2,30},{3,27},{4,24},{5,29},{6,26},{7,31},{8,20},{9,... | collective-permute-start | bytes 393224 | tf_op jit(solution)/shard_map/ppermute | solution.py:353
  14.7 9.4 %collective-permute-start.6 = (bf16[4,128,256]{2,1,0:T(8,128)(2,1)S(1)}, bf16[4,128,256]{2,1,0:T(8,128)(2,1)S(1)}, u32[]{:S(2)}, u32[]{:S(2)}) collective-permute-start(bf16[4,128,256]{2,1,0:T(8,128)(2,1)S(1)} %pad_maximum_fusion.1), channel_id=1, source_target_pairs={{0,2},{1,3},{2,0},{3,1},{4,6},{5,7},{6,4},{7,5},{8,10},{9,11},{10,... | collective-permute-start | bytes 786440 | tf_op jit(solution)/shard_map/ppermute | solution.py:340
  16.3 9.9 %collective-permute-start.9 = (bf16[304,128]{1,0:T(8,128)(2,1)S(1)}, bf16[304,128]{1,0:T(8,128)(2,1)S(1)}, u32[]{:S(2)}, u32[]{:S(2)}) collective-permute-start(bf16[304,128]{1,0:T(8,128)(2,1)S(1)} %get-tuple-element.54), channel_id=1, source_target_pairs={{0,0},{1,5},{2,2},{3,7},{4,4},{5,1},{6,6},{7,3},{8,8},{9,13},{10,1... | collective-permute-start | bytes 233480 | tf_op jit(solution)/shard_map/ppermute | solution.py:353
  17.0 14.2 %collective-permute-start.10 = (bf16[304,128]{1,0:T(8,128)(2,1)S(1)}, bf16[304,128]{1,0:T(8,128)(2,1)S(1)}, u32[]{:S(2)}, u32[]{:S(2)}) collective-permute-start(bf16[304,128]{1,0:T(8,128)(2,1)S(1)} %get-tuple-element.53), channel_id=1, source_target_pairs={{0,12},{1,9},{2,14},{3,11},{4,8},{5,13},{6,10},{7,15},{8,4},{9,1},... | collective-permute-start | bytes 233480 | tf_op jit(solution)/shard_map/ppermute | solution.py:353
  24.1 9.0 %collective-permute-start.11 = (bf16[304,128]{1,0:T(8,128)(2,1)S(1)}, bf16[304,128]{1,0:T(8,128)(2,1)S(1)}, u32[]{:S(2)}, u32[]{:S(2)}) collective-permute-start(bf16[304,128]{1,0:T(8,128)(2,1)S(1)} %get-tuple-element.52), channel_id=1, source_target_pairs={{0,16},{1,21},{2,18},{3,23},{4,20},{5,17},{6,22},{7,19},{8,24},{9,... | collective-permute-start | bytes 233480 | tf_op jit(solution)/shard_map/ppermute | solution.py:353
  24.1 9.4 %collective-permute-start.7 = (bf16[2,128,256]{2,1,0:T(8,128)(2,1)S(1)}, bf16[2,128,256]{2,1,0:T(8,128)(2,1)S(1)}, u32[]{:S(2)}, u32[]{:S(2)}) collective-permute-start(bf16[2,128,256]{2,1,0:T(8,128)(2,1)S(1)} %collective-permute-done.1), channel_id=1, source_target_pairs={{0,2},{1,3},{2,0},{3,1},{4,6},{5,7},{6,4},{7,5},{8,10},{9,11},{10,... | collective-permute-start | bytes 393224 | tf_op jit(solution)/shard_map/ppermute | solution.py:340
  25.6 7.8 %collective-permute-start.8 = (bf16[2,128,256]{2,1,0:T(8,128)(2,1)S(1)}, bf16[2,128,256]{2,1,0:T(8,128)(2,1)S(1)}, u32[]{:S(2)}, u32[]{:S(2)}) collective-permute-start(bf16[2,128,256]{2,1,0:T(8,128)(2,1)S(1)} %collective-permute-done.2), channel_id=1, source_target_pairs={{0,2},{1,3},{2,0},{3,1},{4,6},{5,7},{6,4},{7,5},{8,10},{9,11},{10,... | collective-permute-start | bytes 393224 | tf_op jit(solution)/shard_map/ppermute | solution.py:340
  26.2 3.4 %copy-start = (s32[1,4096,2]{1,2,0:T(2,128)S(1)}, s32[1,4096,2]{1,2,0:T(2,128)}, u32[]{:S(2)}) copy-start(s32[1,4096,2]{1,2,0:T(2,128)} %param.13) | copy-start | bytes 98308
  26.2 7.2 %collective-permute-start.12 = (bf16[304,128]{1,0:T(8,128)(2,1)S(1)}, bf16[304,128]{1,0:T(8,128)(2,1)S(1)}, u32[]{:S(2)}, u32[]{:S(2)}) collective-permute-start(bf16[304,128]{1,0:T(8,128)(2,1)S(1)} %get-tuple-element.51), channel_id=1, source_target_pairs={{0,28},{1,25},{2,30},{3,27},{4,24},{5,29},{6,26},{7,31},{8,20},{9,... | collective-permute-start | bytes 233480 | tf_op jit(solution)/shard_map/ppermute | solution.py:353
  31.1 4.7 %copy-start.1 = (f32[1,1024,256]{2,1,0:T(8,128)S(1)}, f32[1,1024,256]{2,1,0:T(8,128)}, u32[]{:S(2)}) copy-start(f32[1,1024,256]{2,1,0:T(8,128)} %param.14) | copy-start | bytes 3145732
  31.1 4.6 %collective-permute-start.13 = (bf16[8,128,256]{2,1,0:T(8,128)(2,1)S(1)}, bf16[8,128,256]{2,1,0:T(8,128)(2,1)S(1)}, u32[]{:S(2)}, u32[]{:S(2)}) collective-permute-start(bf16[8,128,256]{2,1,0:T(8,128)(2,1)S(1)} %constant_dynamic-update-slice_fusion.refs_0_), channel_id=1, source_target_pairs={{0,1},{1,0},{2,3},{3,2},{4,5},{5,4},{6,7},{7,6},{8,9},{9,8},{10,11... | collective-permute-start | bytes 1572872 | tf_op jit(solution)/shard_map/ppermute | solution.py:340
  33.5 2.2 %collective-permute-start.14 = (bf16[8,128,256]{2,1,0:T(8,128)(2,1)S(1)}, bf16[8,128,256]{2,1,0:T(8,128)(2,1)S(1)}, u32[]{:S(2)}, u32[]{:S(2)}) collective-permute-start(bf16[8,128,256]{2,1,0:T(8,128)(2,1)S(1)} %pad_maximum_fusion), channel_id=1, source_target_pairs={{0,1},{1,0},{2,3},{3,2},{4,5},{5,4},{6,7},{7,6},{8,9},{9,8},{10,11... | collective-permute-start | bytes 1572872 | tf_op jit(solution)/shard_map/ppermute | solution.py:340
  33.7 2.1 %copy-start.2 = (f32[1,1024]{1,0:T(1,128)S(1)}, f32[1,1024]{1,0:T(1,128)}, u32[]{:S(2)}) copy-start(f32[1,1024]{1,0:T(1,128)} %accum.1) | copy-start | bytes 12292
  33.7 6.7 %collective-permute-start.15 = (f32[304,128]{1,0:T(8,128)S(1)}, f32[304,128]{1,0:T(8,128)S(1)}, u32[]{:S(2)}, u32[]{:S(2)}) collective-permute-start(f32[304,128]{1,0:T(8,128)S(1)} %get-tuple-element.50), channel_id=1, source_target_pairs={{0,1},{1,0},{2,3},{3,2},{4,5},{5,4},{6,7},{7,6},{8,9},{9,8},{10,11... | collective-permute-start | bytes 466952 | tf_op jit(solution)/shard_map/ppermute | solution.py:340
  34.3 5.0 %collective-permute-start.16 = (bf16[304,128]{1,0:T(8,128)(2,1)S(1)}, bf16[304,128]{1,0:T(8,128)(2,1)S(1)}, u32[]{:S(2)}, u32[]{:S(2)}) collective-permute-start(bf16[304,128]{1,0:T(8,128)(2,1)S(1)} %get-tuple-element.49), channel_id=1, source_target_pairs={{0,2},{1,3},{2,0},{3,1},{4,6},{5,7},{6,4},{7,5},{8,10},{9,11},{10,... | collective-permute-start | bytes 233480 | tf_op jit(solution)/shard_map/ppermute | solution.py:340
  35.8 4.6 %collective-permute-start.17 = (bf16[304,128]{1,0:T(8,128)(2,1)S(1)}, bf16[304,128]{1,0:T(8,128)(2,1)S(1)}, u32[]{:S(2)}, u32[]{:S(2)}) collective-permute-start(bf16[304,128]{1,0:T(8,128)(2,1)S(1)} %get-tuple-element.49), channel_id=1, source_target_pairs={{0,3},{1,2},{2,1},{3,0},{4,7},{5,6},{6,5},{7,4},{8,11},{9,10},{10,... | collective-permute-start | bytes 233480 | tf_op jit(solution)/shard_map/ppermute | solution.py:340

commit v6 on v5

--- a/solution.py
+++ b/solution.py
@@ -179,7 +179,7 @@
     grads, sums, kept = refs[:count], refs[count], refs[count + 1 :]
     rows, width = sums.shape
     bag_rows(groups, n_narrow, place, ids, kept, rows)
-    tile = min(256, rows)
+    tile = 512 if rows % 512 == 0 else 256
     for base in range(0, rows, tile):
         sums[base : base + tile, :] = tile_sums(base, tile, grads, kept, width)
 

time: 41.4 us -> 41.4 us (level)
  no operation moved by 1% of the time
where the time goes in v6:
time: 41.4 us; the launch traced here: 41.1 us
  starting transfers between devices  19.8 us (48%)
  waiting for transfers between devices  10.1 us (24%)
  Pallas kernels  9.18 us (22%)
  other arithmetic  1.08 us (3%)
  between operations  0.87 us (2%)
    ppermute x8, starting transfers between devices, reach(): return lax.ppermute(block, ('wide', 'narrow'), pairs)  13.4 us
    ppermute x8, waiting for transfers between devices, reach(): return lax.ppermute(block, ('wide', 'narrow'), pairs)  7.91 us
    ppermute x10, starting transfers between devices, swap(): return lax.ppermute(array, axis, [(i, i ^ bit) for i in range(n)])  6.42 us
    pallas_call x1, Pallas kernels, local_part(): pl.pallas_call(local_kernel, out_shape=[jax.ShapeDtypeStruct(shape, jnp.b...  4.16 us
    pallas_call x1, Pallas kernels, row_part(): pl.pallas_call(functools.partial(row_kernel, groups, n_narrow), out_shape...  3.49 us
    ppermute x10, waiting for transfers between devices, swap(): return lax.ppermute(array, axis, [(i, i ^ bit) for i in range(n)])  2.17 us
    pallas_call x1, Pallas kernels, early_part(): pl.pallas_call(functools.partial(early_kernel, groups, n_narrow), out_sha...  1.53 us
  transfers between devices with their start and end apart: 18, of which 6 were waited for; matrix products, arithmetic and copies ran while one was open for 1% of the time, Pallas kernels for 12%

profile of v6, /device:TPU:0, one launch (start us, length us, event | category | flops | bytes accessed | tf_op | source)
XLA Modules:
  0.0 41.1 jit_solution(10118949339183832676)
XLA Ops:
  0.6 0.1 pad_add_fusion.place
  0.7 4.2 %shard_map.103 = (bf16[4,128,256]{2,1,0:T(8,128)(2,1)S(1)}, bf16[4,128,256]{2,1,0:T(8,128)(2,1)S(1)}, f32[4,304,128]{2,1,0:T(8,128)S(1)}, f32[4,304,128]{2,1,0:T(8,128)S(1)}) custom-call(s32[3]{0:T(128)S(1)} %pad_add_fusion.place, bf16[128,256]{1,0:T(8,128)(2,1)} %dense_in.1, bf16[1024,256]{1,0:T(8,128)(2,1)} %bitcast.25, bf16[292,1024]{1,0:T(8,128)(2,1)} %bitcast.24, ...), custom_call_target="tpu_custom_call" | custom-call | tf_op jit(solution)/shard_map/pallas_call | solution.py:121
  4.9 0.5 %collective-permute-start = (bf16[4,128,256]{2,1,0:T(8,128)(2,1)S(1)}, bf16[4,128,256]{2,1,0:T(8,128)(2,1)S(1)}, u32[]{:S(2)}, u32[]{:S(2)}) collective-permute-start(bf16[4,128,256]{2,1,0:T(8,128)(2,1)S(1)} %get-tuple-element.27), channel_id=1, source_target_pairs={{0,1},{1,0},{2,3},{3,2},{4,5},{5,4},{6,7},{7,6},{8,9},{9,8},{10,11... | collective-permute-start | bytes 786440 | tf_op jit(solution)/shard_map/ppermute | solution.py:340
  5.4 0.1 collective-permute-start.5
  5.5 1.1 %collective-permute-done = bf16[4,128,256]{2,1,0:T(8,128)(2,1)S(1)} collective-permute-done((bf16[4,128,256]{2,1,0:T(8,128)(2,1)S(1)}, bf16[4,128,256]{2,1,0:T(8,128)(2,1)S(1)}, u32[]{:S(2)}, u32[]{:S(2)}) %collective-permute-start) | collective-permute-done | bytes 262176 | tf_op jit(solution)/shard_map/ppermute | solution.py:340
  6.6 4.0 %collective-permute-start.3 = (bf16[2,128,256]{2,1,0:T(8,128)(2,1)S(1)}, bf16[2,128,256]{2,1,0:T(8,128)(2,1)S(1)}, u32[]{:S(2)}, u32[]{:S(2)}) collective-permute-start(bf16[2,128,256]{2,1,0:T(8,128)(2,1)S(1)} %pad_maximum_fusion.5), channel_id=1, source_target_pairs={{0,12},{1,9},{2,14},{3,11},{4,8},{5,13},{6,10},{7,15},{8,4},{9,1},... | collective-permute-start | bytes 393224 | tf_op jit(solution)/shard_map/ppermute | solution.py:353
  10.6 0.7 %collective-permute-start.4 = (bf16[2,128,256]{2,1,0:T(8,128)(2,1)S(1)}, bf16[2,128,256]{2,1,0:T(8,128)(2,1)S(1)}, u32[]{:S(2)}, u32[]{:S(2)}) collective-permute-start(bf16[2,128,256]{2,1,0:T(8,128)(2,1)S(1)} %pad_maximum_fusion.6), channel_id=1, source_target_pairs={{0,0},{1,5},{2,2},{3,7},{4,4},{5,1},{6,6},{7,3},{8,8},{9,13},{10,1... | collective-permute-start | bytes 393224 | tf_op jit(solution)/shard_map/ppermute | solution.py:353
  11.3 2.7 %collective-permute-start.1 = (bf16[2,128,256]{2,1,0:T(8,128)(2,1)S(1)}, bf16[2,128,256]{2,1,0:T(8,128)(2,1)S(1)}, u32[]{:S(2)}, u32[]{:S(2)}) collective-permute-start(bf16[2,128,256]{2,1,0:T(8,128)(2,1)S(1)} %pad_maximum_fusion.3), channel_id=1, source_target_pairs={{0,16},{1,21},{2,18},{3,23},{4,20},{5,17},{6,22},{7,19},{8,24},{9,... | collective-permute-start | bytes 393224 | tf_op jit(solution)/shard_map/ppermute | solution.py:353
  14.0 0.1 collective-permute-start.2
  14.0 0.6 %collective-permute-done.3 = bf16[2,128,256]{2,1,0:T(8,128)(2,1)S(1)} collective-permute-done((bf16[2,128,256]{2,1,0:T(8,128)(2,1)S(1)}, bf16[2,128,256]{2,1,0:T(8,128)(2,1)S(1)}, u32[]{:S(2)}, u32[]{:S(2)}) %collective-permute-start.3) | collective-permute-done | bytes 131104 | tf_op jit(solution)/shard_map/ppermute | solution.py:353
  14.7 1.5 %collective-permute-start.6 = (bf16[4,128,256]{2,1,0:T(8,128)(2,1)S(1)}, bf16[4,128,256]{2,1,0:T(8,128)(2,1)S(1)}, u32[]{:S(2)}, u32[]{:S(2)}) collective-permute-start(bf16[4,128,256]{2,1,0:T(8,128)(2,1)S(1)} %pad_maximum_fusion.1), channel_id=1, source_target_pairs={{0,2},{1,3},{2,0},{3,1},{4,6},{5,7},{6,4},{7,5},{8,10},{9,11},{10,... | collective-permute-start | bytes 786440 | tf_op jit(solution)/shard_map/ppermute | solution.py:340
  16.2 0.1 add_convert_fusion
  16.3 0.7 %collective-permute-start.9 = (bf16[304,128]{1,0:T(8,128)(2,1)S(1)}, bf16[304,128]{1,0:T(8,128)(2,1)S(1)}, u32[]{:S(2)}, u32[]{:S(2)}) collective-permute-start(bf16[304,128]{1,0:T(8,128)(2,1)S(1)} %get-tuple-element.54), channel_id=1, source_target_pairs={{0,0},{1,5},{2,2},{3,7},{4,4},{5,1},{6,6},{7,3},{8,8},{9,13},{10,1... | collective-permute-start | bytes 233480 | tf_op jit(solution)/shard_map/ppermute | solution.py:353
  17.0 2.0 %collective-permute-start.10 = (bf16[304,128]{1,0:T(8,128)(2,1)S(1)}, bf16[304,128]{1,0:T(8,128)(2,1)S(1)}, u32[]{:S(2)}, u32[]{:S(2)}) collective-permute-start(bf16[304,128]{1,0:T(8,128)(2,1)S(1)} %get-tuple-element.53), channel_id=1, source_target_pairs={{0,12},{1,9},{2,14},{3,11},{4,8},{5,13},{6,10},{7,15},{8,4},{9,1},... | collective-permute-start | bytes 233480 | tf_op jit(solution)/shard_map/ppermute | solution.py:353
  19.0 5.1 %collective-permute-done.1 = bf16[2,128,256]{2,1,0:T(8,128)(2,1)S(1)} collective-permute-done((bf16[2,128,256]{2,1,0:T(8,128)(2,1)S(1)}, bf16[2,128,256]{2,1,0:T(8,128)(2,1)S(1)}, u32[]{:S(2)}, u32[]{:S(2)}) %collective-permute-start.1) | collective-permute-done | bytes 131104 | tf_op jit(solution)/shard_map/ppermute | solution.py:353
  24.1 1.6 %collective-permute-start.7 = (bf16[2,128,256]{2,1,0:T(8,128)(2,1)S(1)}, bf16[2,128,256]{2,1,0:T(8,128)(2,1)S(1)}, u32[]{:S(2)}, u32[]{:S(2)}) collective-permute-start(bf16[2,128,256]{2,1,0:T(8,128)(2,1)S(1)} %collective-permute-done.1), channel_id=1, source_target_pairs={{0,2},{1,3},{2,0},{3,1},{4,6},{5,7},{6,4},{7,5},{8,10},{9,11},{10,... | collective-permute-start | bytes 393224 | tf_op jit(solution)/shard_map/ppermute | solution.py:340
  25.6 0.6 %collective-permute-start.8 = (bf16[2,128,256]{2,1,0:T(8,128)(2,1)S(1)}, bf16[2,128,256]{2,1,0:T(8,128)(2,1)S(1)}, u32[]{:S(2)}, u32[]{:S(2)}) collective-permute-start(bf16[2,128,256]{2,1,0:T(8,128)(2,1)S(1)} %collective-permute-done.2), channel_id=1, source_target_pairs={{0,2},{1,3},{2,0},{3,1},{4,6},{5,7},{6,4},{7,5},{8,10},{9,11},{10,... | collective-permute-start | bytes 393224 | tf_op jit(solution)/shard_map/ppermute | solution.py:340
  26.2 0.0 copy-start
  26.2 3.3 %collective-permute-start.12 = (bf16[304,128]{1,0:T(8,128)(2,1)S(1)}, bf16[304,128]{1,0:T(8,128)(2,1)S(1)}, u32[]{:S(2)}, u32[]{:S(2)}) collective-permute-start(bf16[304,128]{1,0:T(8,128)(2,1)S(1)} %get-tuple-element.51), channel_id=1, source_target_pairs={{0,28},{1,25},{2,30},{3,27},{4,24},{5,29},{6,26},{7,31},{8,20},{9,... | collective-permute-start | bytes 233480 | tf_op jit(solution)/shard_map/ppermute | solution.py:353
  29.6 1.5 %shard_map.104.before = f32[1024,256]{1,0:T(8,128)S(1)} custom-call(s32[3]{0:T(128)S(1)} %pad_add_fusion.place, s32[2,4096]{1,0:T(2,128)S(1)} %bitcast.21, bf16[8,128,256]{2,1,0:T(8,128)(2,1)S(1)} %constant_dynamic-update-slice_fusion.refs_0_, bf16[4,128,256]{2,1,0:T(8,128)(2,1)S(1)} %collective-permute-done.6.refs_1_), custom_call_target="tpu_custom_call" | custom-call | tf_op jit(solution)/shard_map/pallas_call | solution.py:227
  31.1 0.0 copy-start.1
  31.2 0.1 collective-permute-start.13
  31.2 1.9 %collective-permute-done.11 = bf16[304,128]{1,0:T(8,128)(2,1)S(1)} collective-permute-done((bf16[304,128]{1,0:T(8,128)(2,1)S(1)}, bf16[304,128]{1,0:T(8,128)(2,1)S(1)}, u32[]{:S(2)}, u32[]{:S(2)}) %collective-permute-start.11) | collective-permute-done | bytes 77856 | tf_op jit(solution)/shard_map/ppermute | solution.py:353
  33.1 0.4 collective-permute-done.12
  33.5 0.1 pad_maximum_fusion
  33.5 0.1 collective-permute-start.14
  33.6 0.1 fusion.3
  33.7 0.6 %collective-permute-start.15 = (f32[304,128]{1,0:T(8,128)S(1)}, f32[304,128]{1,0:T(8,128)S(1)}, u32[]{:S(2)}, u32[]{:S(2)}) collective-permute-start(f32[304,128]{1,0:T(8,128)S(1)} %get-tuple-element.50), channel_id=1, source_target_pairs={{0,1},{1,0},{2,3},{3,2},{4,5},{5,4},{6,7},{7,6},{8,9},{9,8},{10,11... | collective-permute-start | bytes 466952 | tf_op jit(solution)/shard_map/ppermute | solution.py:340
  34.3 1.5 %collective-permute-start.16 = (bf16[304,128]{1,0:T(8,128)(2,1)S(1)}, bf16[304,128]{1,0:T(8,128)(2,1)S(1)}, u32[]{:S(2)}, u32[]{:S(2)}) collective-permute-start(bf16[304,128]{1,0:T(8,128)(2,1)S(1)} %get-tuple-element.49), channel_id=1, source_target_pairs={{0,2},{1,3},{2,0},{3,1},{4,6},{5,7},{6,4},{7,5},{8,10},{9,11},{10,... | collective-permute-start | bytes 233480 | tf_op jit(solution)/shard_map/ppermute | solution.py:340
  35.8 3.5 %shard_map.105 = (f32[1024,256]{1,0:T(8,128)}, f32[1,1024]{1,0:T(1,128)}) custom-call(s32[3]{0:T(128)S(1)} %pad_add_fusion.place, s32[2,4096]{1,0:T(2,128)S(1)} %bitcast.22, f32[1024,256]{1,0:T(8,128)S(1)} %bitcast.23, f32[1,1024]{1,0:T(1,128)S(1)} %copy-done.2, f32[1024,256]{1,0:T(8,128)S(1)} %shard_map.104.before, ...), custom_call_target="tpu_custom_call" | custom-call | flops 1342177280 | bytes 2097152 | tf_op jit(solution)/shard_map/pallas_call | solution.py:242
  39.3 1.1 %collective-permute-done.17 = bf16[304,128]{1,0:T(8,128)(2,1)S(1)} collective-permute-done((bf16[304,128]{1,0:T(8,128)(2,1)S(1)}, bf16[304,128]{1,0:T(8,128)(2,1)S(1)}, u32[]{:S(2)}, u32[]{:S(2)}) %collective-permute-start.17) | collective-permute-done | bytes 77856 | tf_op jit(solution)/shard_map/ppermute | solution.py:340
  40.4 0.7 %fusion.2 = f32[128,292]{0,1:T(8,128)} fusion(f32[304,128]{1,0:T(8,128)S(1)} %collective-permute-done.15, f32[304,128]{1,0:T(8,128)S(1)} %get-tuple-element.50, bf16[304,128]{1,0:T(8,128)(2,1)S(1)} %collective-permute-done.17, bf16[304,128]{1,0:T(8,128)(2,1)S(1)} %collective-permute-done.16), kind=kLoop, calls=%fused_computation.8 | loop fusion | flops 261632 | bytes 598016 | tf_op jit(solution)/shard_map/transpose | solution.py:380
  (31 shorter events, 0.3 us)
Async XLA Ops:
  4.9 1.7 %collective-permute-start = (bf16[4,128,256]{2,1,0:T(8,128)(2,1)S(1)}, bf16[4,128,256]{2,1,0:T(8,128)(2,1)S(1)}, u32[]{:S(2)}, u32[]{:S(2)}) collective-permute-start(bf16[4,128,256]{2,1,0:T(8,128)(2,1)S(1)} %get-tuple-element.27), channel_id=1, source_target_pairs={{0,1},{1,0},{2,3},{3,2},{4,5},{5,4},{6,7},{7,6},{8,9},{9,8},{10,11... | collective-permute-start | bytes 786440 | tf_op jit(solution)/shard_map/ppermute | solution.py:340
  5.4 9.2 %collective-permute-start.5 = (f32[4,304,128]{2,1,0:T(8,128)S(1)}, f32[4,304,128]{2,1,0:T(8,128)S(1)}, u32[]{:S(2)}, u32[]{:S(2)}) collective-permute-start(f32[4,304,128]{2,1,0:T(8,128)S(1)} %get-tuple-element.28), channel_id=1, source_target_pairs={{0,1},{1,0},{2,3},{3,2},{4,5},{5,4},{6,7},{7,6},{8,9},{9,8},{10,11... | collective-permute-start | bytes 1867784 | tf_op jit(solution)/shard_map/ppermute | solution.py:340
  6.6 8.0 %collective-permute-start.3 = (bf16[2,128,256]{2,1,0:T(8,128)(2,1)S(1)}, bf16[2,128,256]{2,1,0:T(8,128)(2,1)S(1)}, u32[]{:S(2)}, u32[]{:S(2)}) collective-permute-start(bf16[2,128,256]{2,1,0:T(8,128)(2,1)S(1)} %pad_maximum_fusion.5), channel_id=1, source_target_pairs={{0,12},{1,9},{2,14},{3,11},{4,8},{5,13},{6,10},{7,15},{8,4},{9,1},... | collective-permute-start | bytes 393224 | tf_op jit(solution)/shard_map/ppermute | solution.py:353
  10.6 4.1 %collective-permute-start.4 = (bf16[2,128,256]{2,1,0:T(8,128)(2,1)S(1)}, bf16[2,128,256]{2,1,0:T(8,128)(2,1)S(1)}, u32[]{:S(2)}, u32[]{:S(2)}) collective-permute-start(bf16[2,128,256]{2,1,0:T(8,128)(2,1)S(1)} %pad_maximum_fusion.6), channel_id=1, source_target_pairs={{0,0},{1,5},{2,2},{3,7},{4,4},{5,1},{6,6},{7,3},{8,8},{9,13},{10,1... | collective-permute-start | bytes 393224 | tf_op jit(solution)/shard_map/ppermute | solution.py:353
  11.3 12.8 %collective-permute-start.1 = (bf16[2,128,256]{2,1,0:T(8,128)(2,1)S(1)}, bf16[2,128,256]{2,1,0:T(8,128)(2,1)S(1)}, u32[]{:S(2)}, u32[]{:S(2)}) collective-permute-start(bf16[2,128,256]{2,1,0:T(8,128)(2,1)S(1)} %pad_maximum_fusion.3), channel_id=1, source_target_pairs={{0,16},{1,21},{2,18},{3,23},{4,20},{5,17},{6,22},{7,19},{8,24},{9,... | collective-permute-start | bytes 393224 | tf_op jit(solution)/shard_map/ppermute | solution.py:353
  14.0 10.1 %collective-permute-start.2 = (bf16[2,128,256]{2,1,0:T(8,128)(2,1)S(1)}, bf16[2,128,256]{2,1,0:T(8,128)(2,1)S(1)}, u32[]{:S(2)}, u32[]{:S(2)}) collective-permute-start(bf16[2,128,256]{2,1,0:T(8,128)(2,1)S(1)} %pad_maximum_fusion.4), channel_id=1, source_target_pairs={{0,28},{1,25},{2,30},{3,27},{4,24},{5,29},{6,26},{7,31},{8,20},{9,... | collective-permute-start | bytes 393224 | tf_op jit(solution)/shard_map/ppermute | solution.py:353
  14.7 9.4 %collective-permute-start.6 = (bf16[4,128,256]{2,1,0:T(8,128)(2,1)S(1)}, bf16[4,128,256]{2,1,0:T(8,128)(2,1)S(1)}, u32[]{:S(2)}, u32[]{:S(2)}) collective-permute-start(bf16[4,128,256]{2,1,0:T(8,128)(2,1)S(1)} %pad_maximum_fusion.1), channel_id=1, source_target_pairs={{0,2},{1,3},{2,0},{3,1},{4,6},{5,7},{6,4},{7,5},{8,10},{9,11},{10,... | collective-permute-start | bytes 786440 | tf_op jit(solution)/shard_map/ppermute | solution.py:340
  16.3 9.9 %collective-permute-start.9 = (bf16[304,128]{1,0:T(8,128)(2,1)S(1)}, bf16[304,128]{1,0:T(8,128)(2,1)S(1)}, u32[]{:S(2)}, u32[]{:S(2)}) collective-permute-start(bf16[304,128]{1,0:T(8,128)(2,1)S(1)} %get-tuple-element.54), channel_id=1, source_target_pairs={{0,0},{1,5},{2,2},{3,7},{4,4},{5,1},{6,6},{7,3},{8,8},{9,13},{10,1... | collective-permute-start | bytes 233480 | tf_op jit(solution)/shard_map/ppermute | solution.py:353
  17.0 14.2 %collective-permute-start.10 = (bf16[304,128]{1,0:T(8,128)(2,1)S(1)}, bf16[304,128]{1,0:T(8,128)(2,1)S(1)}, u32[]{:S(2)}, u32[]{:S(2)}) collective-permute-start(bf16[304,128]{1,0:T(8,128)(2,1)S(1)} %get-tuple-element.53), channel_id=1, source_target_pairs={{0,12},{1,9},{2,14},{3,11},{4,8},{5,13},{6,10},{7,15},{8,4},{9,1},... | collective-permute-start | bytes 233480 | tf_op jit(solution)/shard_map/ppermute | solution.py:353
  24.1 9.0 %collective-permute-start.11 = (bf16[304,128]{1,0:T(8,128)(2,1)S(1)}, bf16[304,128]{1,0:T(8,128)(2,1)S(1)}, u32[]{:S(2)}, u32[]{:S(2)}) collective-permute-start(bf16[304,128]{1,0:T(8,128)(2,1)S(1)} %get-tuple-element.52), channel_id=1, source_target_pairs={{0,16},{1,21},{2,18},{3,23},{4,20},{5,17},{6,22},{7,19},{8,24},{9,... | collective-permute-start | bytes 233480 | tf_op jit(solution)/shard_map/ppermute | solution.py:353
  24.1 9.4 %collective-permute-start.7 = (bf16[2,128,256]{2,1,0:T(8,128)(2,1)S(1)}, bf16[2,128,256]{2,1,0:T(8,128)(2,1)S(1)}, u32[]{:S(2)}, u32[]{:S(2)}) collective-permute-start(bf16[2,128,256]{2,1,0:T(8,128)(2,1)S(1)} %collective-permute-done.1), channel_id=1, source_target_pairs={{0,2},{1,3},{2,0},{3,1},{4,6},{5,7},{6,4},{7,5},{8,10},{9,11},{10,... | collective-permute-start | bytes 393224 | tf_op jit(solution)/shard_map/ppermute | solution.py:340
  25.6 7.8 %collective-permute-start.8 = (bf16[2,128,256]{2,1,0:T(8,128)(2,1)S(1)}, bf16[2,128,256]{2,1,0:T(8,128)(2,1)S(1)}, u32[]{:S(2)}, u32[]{:S(2)}) collective-permute-start(bf16[2,128,256]{2,1,0:T(8,128)(2,1)S(1)} %collective-permute-done.2), channel_id=1, source_target_pairs={{0,2},{1,3},{2,0},{3,1},{4,6},{5,7},{6,4},{7,5},{8,10},{9,11},{10,... | collective-permute-start | bytes 393224 | tf_op jit(solution)/shard_map/ppermute | solution.py:340
  26.2 3.4 %copy-start = (s32[1,4096,2]{1,2,0:T(2,128)S(1)}, s32[1,4096,2]{1,2,0:T(2,128)}, u32[]{:S(2)}) copy-start(s32[1,4096,2]{1,2,0:T(2,128)} %param.13) | copy-start | bytes 98308
  26.2 7.2 %collective-permute-start.12 = (bf16[304,128]{1,0:T(8,128)(2,1)S(1)}, bf16[304,128]{1,0:T(8,128)(2,1)S(1)}, u32[]{:S(2)}, u32[]{:S(2)}) collective-permute-start(bf16[304,128]{1,0:T(8,128)(2,1)S(1)} %get-tuple-element.51), channel_id=1, source_target_pairs={{0,28},{1,25},{2,30},{3,27},{4,24},{5,29},{6,26},{7,31},{8,20},{9,... | collective-permute-start | bytes 233480 | tf_op jit(solution)/shard_map/ppermute | solution.py:353
  31.1 4.7 %copy-start.1 = (f32[1,1024,256]{2,1,0:T(8,128)S(1)}, f32[1,1024,256]{2,1,0:T(8,128)}, u32[]{:S(2)}) copy-start(f32[1,1024,256]{2,1,0:T(8,128)} %param.14) | copy-start | bytes 3145732
  31.2 4.6 %collective-permute-start.13 = (bf16[8,128,256]{2,1,0:T(8,128)(2,1)S(1)}, bf16[8,128,256]{2,1,0:T(8,128)(2,1)S(1)}, u32[]{:S(2)}, u32[]{:S(2)}) collective-permute-start(bf16[8,128,256]{2,1,0:T(8,128)(2,1)S(1)} %constant_dynamic-update-slice_fusion.refs_0_), channel_id=1, source_target_pairs={{0,1},{1,0},{2,3},{3,2},{4,5},{5,4},{6,7},{7,6},{8,9},{9,8},{10,11... | collective-permute-start | bytes 1572872 | tf_op jit(solution)/shard_map/ppermute | solution.py:340
  33.5 2.2 %collective-permute-start.14 = (bf16[8,128,256]{2,1,0:T(8,128)(2,1)S(1)}, bf16[8,128,256]{2,1,0:T(8,128)(2,1)S(1)}, u32[]{:S(2)}, u32[]{:S(2)}) collective-permute-start(bf16[8,128,256]{2,1,0:T(8,128)(2,1)S(1)} %pad_maximum_fusion), channel_id=1, source_target_pairs={{0,1},{1,0},{2,3},{3,2},{4,5},{5,4},{6,7},{7,6},{8,9},{9,8},{10,11... | collective-permute-start | bytes 1572872 | tf_op jit(solution)/shard_map/ppermute | solution.py:340
  33.7 2.1 %copy-start.2 = (f32[1,1024]{1,0:T(1,128)S(1)}, f32[1,1024]{1,0:T(1,128)}, u32[]{:S(2)}) copy-start(f32[1,1024]{1,0:T(1,128)} %accum.1) | copy-start | bytes 12292
  33.7 6.7 %collective-permute-start.15 = (f32[304,128]{1,0:T(8,128)S(1)}, f32[304,128]{1,0:T(8,128)S(1)}, u32[]{:S(2)}, u32[]{:S(2)}) collective-permute-start(f32[304,128]{1,0:T(8,128)S(1)} %get-tuple-element.50), channel_id=1, source_target_pairs={{0,1},{1,0},{2,3},{3,2},{4,5},{5,4},{6,7},{7,6},{8,9},{9,8},{10,11... | collective-permute-start | bytes 466952 | tf_op jit(solution)/shard_map/ppermute | solution.py:340
  34.3 5.0 %collective-permute-start.16 = (bf16[304,128]{1,0:T(8,128)(2,1)S(1)}, bf16[304,128]{1,0:T(8,128)(2,1)S(1)}, u32[]{:S(2)}, u32[]{:S(2)}) collective-permute-start(bf16[304,128]{1,0:T(8,128)(2,1)S(1)} %get-tuple-element.49), channel_id=1, source_target_pairs={{0,2},{1,3},{2,0},{3,1},{4,6},{5,7},{6,4},{7,5},{8,10},{9,11},{10,... | collective-permute-start | bytes 233480 | tf_op jit(solution)/shard_map/ppermute | solution.py:340
  35.8 4.6 %collective-permute-start.17 = (bf16[304,128]{1,0:T(8,128)(2,1)S(1)}, bf16[304,128]{1,0:T(8,128)(2,1)S(1)}, u32[]{:S(2)}, u32[]{:S(2)}) collective-permute-start(bf16[304,128]{1,0:T(8,128)(2,1)S(1)} %get-tuple-element.49), channel_id=1, source_target_pairs={{0,3},{1,2},{2,1},{3,0},{4,7},{5,6},{6,5},{7,4},{8,11},{9,10},{10,... | collective-permute-start | bytes 233480 | tf_op jit(solution)/shard_map/ppermute | solution.py:340
